TPU v7x, 512 devices: a whole 4x8x8 slice. The times are simulated.
512 devices in a mesh: prompt: 32 (over y_hi, x, core), resp: 16 (over y_lo, z).
Axes of the slice: x: 4, y: 8 (y_hi: 4, y_lo: 2; y = y_hi * 2 + y_lo), z: 8, core: 2. Of those that a mesh axis runs over, the one named last changes fastest.
Arguments:
- prefix_keys: bfloat16 [32, 512, 512], P('prompt', 'resp'), may hold values from -6 to 6
- prefix_values: bfloat16 [32, 512, 512], P('prompt', 'resp'), may hold values from -6 to 6
- resp_queries: bfloat16 [32, 16, 128, 2560], P('prompt', 'resp'), may hold values from -6 to 6
- resp_keys: bfloat16 [32, 16, 128, 512], P('prompt', 'resp'), may hold values from -6 to 6
- resp_values: bfloat16 [32, 16, 128, 512], P('prompt', 'resp'), may hold values from -6 to 6
- query_bias: float32 [2560], replicated, may hold values from -3 to 3
- out_grad: bfloat16 [32, 16, 128, 2560], P('prompt', 'resp'), may hold values from -96 to 96
- lengths: int32 [32, 16], P('prompt', 'resp'), may hold values from 16 to 128, as said below
Outputs:
- grad_queries: bfloat16 [32, 16, 128, 2560], P('prompt', 'resp')
- grad_resp_keys: bfloat16 [32, 16, 128, 512], P('prompt', 'resp')
- grad_resp_values: bfloat16 [32, 16, 128, 512], P('prompt', 'resp')
- grad_prefix_keys: bfloat16 [32, 512, 512], P('prompt', 'resp')
- grad_prefix_values: bfloat16 [32, 512, 512], P('prompt', 'resp')
- grad_query_bias: float32 [2560], replicated
Inputs may be any that keep to these rules, and one draw needn't show every extreme that they name: `lengths`: every prompt has one response of exactly 128 live tokens.
All inputs are finite; a program needn't handle non-finite values.
Results may differ from a plain program's by a relative error of at most 0.025.
Values may be sent and summed in bfloat16 or wider, within the bound.
No kernel may reach another device: no remote copies, remote signals or barrier semaphores. Data moves between devices by JAX's collectives and lax.ppermute only.
A program may use at most 64 MiB of HBM per device.

v0:
```python
import math

import jax
import jax.numpy as jnp
from jax import lax
from jax.sharding import PartitionSpec as P

HD = 128
GROUP = 5


def visibility(row_count, prefix_count, length):
    shape = (row_count, prefix_count + row_count)
    rows = lax.broadcasted_iota(jnp.int32, shape, 0)
    cols = lax.broadcasted_iota(jnp.int32, shape, 1)
    later = cols - prefix_count
    return (cols < prefix_count) | (later <= rows) & (later < length)


def head_block(matrix, group, width):
    return matrix[:, group * width : (group + 1) * width]


def attend_groups(queries, keys, values, cotangent, visible):
    scale = 1.0 / math.sqrt(HD)
    kv_heads = keys.shape[1] // HD
    grad_q, grad_k, grad_v, saved = ([], [], [], [])
    for group in range(kv_heads):
        q_group = head_block(queries, group, GROUP * HD).reshape(-1, GROUP, HD)
        do_group = head_block(cotangent, group, GROUP * HD).reshape(-1, GROUP, HD)
        k_group = head_block(keys, group, HD)
        v_group = head_block(values, group, HD)
        scores = (
            jnp.einsum("ich,jh->cij", q_group, k_group, preferred_element_type=jnp.float32) * scale
        )
        scores = jnp.where(visible[None], scores, -jnp.inf)
        top = jnp.max(scores, -1, keepdims=True)
        expd = jnp.exp(scores - top)
        total = jnp.sum(expd, -1, keepdims=True)
        probs = expd / total
        probs_low = probs.astype(jnp.bfloat16)
        dprobs = jnp.einsum("ich,jh->cij", do_group, v_group, preferred_element_type=jnp.float32)
        delta = jnp.sum(probs * dprobs, -1, keepdims=True)
        dscores = (probs * (dprobs - delta) * scale).astype(jnp.bfloat16)
        grad_q.append(
            jnp.einsum("cij,jh->ich", dscores, k_group, preferred_element_type=jnp.float32).reshape(
                -1, GROUP * HD
            )
        )
        grad_k.append(
            jnp.einsum("cij,ich->jh", dscores, q_group, preferred_element_type=jnp.float32)
        )
        grad_v.append(
            jnp.einsum("cij,ich->jh", probs_low, do_group, preferred_element_type=jnp.float32)
        )
        saved.append((top, total, delta))
    return (
        jnp.concatenate(grad_q, 1),
        jnp.concatenate(grad_k, 1),
        jnp.concatenate(grad_v, 1),
        saved,
    )


def body(
    prefix_keys, prefix_values, resp_queries, resp_keys, resp_values, query_bias, out_grad, lengths
):
    length = lengths[0, 0]
    row_count = resp_queries.shape[2]
    queries = (resp_queries[0, 0].astype(jnp.float32) + query_bias[None, :]).astype(jnp.bfloat16)
    live = lax.broadcasted_iota(jnp.int32, (row_count, 1), 0) < length
    cotangent = jnp.where(live, out_grad[0, 0], jnp.zeros((), jnp.bfloat16))
    whole_keys, whole_values = (
        lax.all_gather(prefix_keys[0], "resp", axis=0, tiled=True),
        lax.all_gather(prefix_values[0], "resp", axis=0, tiled=True),
    )
    prefix_count = whole_keys.shape[0]
    keys = jnp.concatenate([whole_keys, resp_keys[0, 0]], 0)
    values = jnp.concatenate([whole_values, resp_values[0, 0]], 0)
    visible = visibility(row_count, prefix_count, length)
    grad_q, grad_k, grad_v, saved = attend_groups(queries, keys, values, cotangent, visible)
    prefix_dk, prefix_dv = (
        lax.psum_scatter(
            grad_k[:prefix_count].astype(jnp.bfloat16), "resp", scatter_dimension=0, tiled=True
        ).astype(jnp.float32),
        lax.psum_scatter(
            grad_v[:prefix_count].astype(jnp.bfloat16), "resp", scatter_dimension=0, tiled=True
        ).astype(jnp.float32),
    )
    resp_dk = grad_k[prefix_count:]
    resp_dv = grad_v[prefix_count:]
    bias_sum = lax.psum(jnp.sum(grad_q, 0), ("prompt", "resp"))
    grad_bias = bias_sum / math.sqrt(lax.axis_size("prompt") * lax.axis_size("resp") * row_count)
    return (
        grad_q.astype(jnp.bfloat16)[None, None],
        resp_dk.astype(jnp.bfloat16)[None, None],
        resp_dv.astype(jnp.bfloat16)[None, None],
        prefix_dk.astype(jnp.bfloat16)[None],
        prefix_dv.astype(jnp.bfloat16)[None],
        grad_bias,
    )


def solution(mesh):
    return jax.shard_map(
        body,
        mesh=mesh,
        in_specs=(
            P("prompt", "resp", None),
            P("prompt", "resp", None),
            P("prompt", "resp", None, None),
            P("prompt", "resp", None, None),
            P("prompt", "resp", None, None),
            P(),
            P("prompt", "resp", None, None),
            P("prompt", "resp"),
        ),
        out_specs=(
            P("prompt", "resp", None, None),
            P("prompt", "resp", None, None),
            P("prompt", "resp", None, None),
            P("prompt", "resp", None),
            P("prompt", "resp", None),
            P(),
        ),
        check_vma=False,
    )
```

profile of v0, /device:TPU:6, one launch (start us, length us, event | category | flops | bytes accessed | tf_op | source)
XLA Modules:
  0.0 274.2 jit_solution(13407780907042568801)
XLA Ops:
  7.9 42.6 %all-gather = bf16[1,512,512]{2,1,0:T(8,128)(2,1)S(1)} all-gather(bf16[1,32,512]{2,1,0:T(8,128)(2,1)} %param.8), channel_id=2, replica_groups=mesh['prompt'=32,'resp'=16] {'resp'}, dimensions={1}, use_global_device_ids=true | all-gather | bytes 557056 | tf_op jit(solution)/shard_map/all_gather | solution.py:74
  50.5 32.6 %all-gather.1 = bf16[1,512,512]{2,1,0:T(8,128)(2,1)S(1)} all-gather(bf16[1,32,512]{2,1,0:T(8,128)(2,1)} %param.9), channel_id=3, replica_groups=mesh['prompt'=32,'resp'=16] {'resp'}, dimensions={1}, use_global_device_ids=true | all-gather | bytes 557056 | tf_op jit(solution)/shard_map/all_gather | solution.py:75
  83.1 1.4 copy.80
  84.6 0.4 fusion.24
  85.0 0.8 fusion.122
  85.8 0.3 copy.82
  86.2 0.8 copy-done
  87.0 1.6 fusion.60
  88.6 1.6 fusion.47
  90.2 1.6 fusion.43
  91.7 0.4 fusion.51
  92.1 0.5 copy-done.19
  92.7 0.3 fusion.40
  93.0 2.8 %exponential_reduce_fusion.3 = (f32[5,128]{1,0:T(8,128)S(1)}, f32[5,128,640]{1,2,0:T(8,128)}) fusion(bf16[128,5,128]{0,2,1:T(8,128)(2,1)} %bitcast.328, pred[128,640]{0,1:T(8,128)(4,1)S(1)} %fusion.40, bf16[512,512]{1,0:T(8,128)(2,1)S(1)} %bitcast.296, bf16[128,512]{1,0:T(8,128)(2,1)} %bitcast.335), kind=kOutput, calls=%fused_computation.43 | convolution fusion | flops 106824320 | bytes 2542080 | tf_op jit(solution)/shard_map/sub | solution.py:38
  95.8 2.8 %exponential_reduce_fusion.1 = (f32[5,128]{1,0:T(8,128)S(1)}, f32[5,128,640]{1,2,0:T(8,128)}) fusion(bf16[128,5,128]{0,2,1:T(8,128)(2,1)S(1)} %bitcast.325, pred[128,640]{0,1:T(8,128)(4,1)} %copy-done.21, bf16[512,512]{1,0:T(8,128)(2,1)S(1)} %bitcast.297, bf16[128,512]{1,0:T(8,128)(2,1)} %bitcast.336), kind=kOutput, calls=%fused_computation.39 | convolution fusion | flops 106824320 | bytes 2542080 | tf_op jit(solution)/shard_map/sub | solution.py:38
  98.6 2.7 exponential_reduce_fusion.2
  101.3 2.7 exponential_reduce_fusion
  104.0 3.9 %convolution_bitcast_fusion.4 = bf16[640,128]{0,1:T(8,128)(2,1)S(1)} fusion(bf16[128,5,128]{0,2,1:T(8,128)(2,1)S(1)} %bitcast.320, f32[640,128,5]{1,0,2:T(8,128)} %fusion.60, f32[5,128,640]{1,2,0:T(8,128)} %get-tuple-element.33, f32[5,128]{1,0:T(8,128)S(1)} %get-tuple-element.32), kind=kOutput, calls=%fused_computation.51 | convolution fusion | flops 107726080 | bytes 3607040 | tf_op jit(solution)/shard_map/cij,ich->jh/dot_general | solution.py:51
  107.9 4.6 %convolution_bitcast_fusion.7 = bf16[640,128]{0,1:T(8,128)(2,1)} fusion(bf16[128,5,128]{0,2,1:T(8,128)(2,1)} %bitcast.329, f32[640,128,5]{1,0,2:T(8,128)} %fusion.47, f32[5,128,640]{1,2,0:T(8,128)} %get-tuple-element.45, f32[5,128]{1,0:T(8,128)S(1)} %get-tuple-element.44), kind=kOutput, calls=%fused_computation.54 | convolution fusion | flops 107726080 | bytes 3607040 | tf_op jit(solution)/shard_map/cij,ich->jh/dot_general | solution.py:51
  112.5 4.5 %convolution_bitcast_fusion.5 = bf16[640,128]{0,1:T(8,128)(2,1)} fusion(bf16[128,5,128]{0,2,1:T(8,128)(2,1)S(1)} %bitcast.326, f32[640,128,5]{1,0,2:T(8,128)} %fusion.43, f32[5,128,640]{1,2,0:T(8,128)} %get-tuple-element.37, f32[5,128]{1,0:T(8,128)S(1)} %get-tuple-element.36), kind=kOutput, calls=%fused_computation.52 | convolution fusion | flops 107726080 | bytes 3607040 | tf_op jit(solution)/shard_map/cij,ich->jh/dot_general | solution.py:51
  117.0 3.4 %convolution_bitcast_fusion.6 = bf16[640,128]{0,1:T(8,128)(2,1)} fusion(bf16[128,5,128]{0,2,1:T(8,128)(2,1)S(1)} %bitcast.323, f32[640,128,5]{1,0,2:T(8,128)S(1)} %fusion.51, f32[5,128,640]{1,2,0:T(8,128)} %get-tuple-element.41, f32[5,128]{1,0:T(8,128)S(1)} %get-tuple-element.40), kind=kOutput, calls=%fused_computation.53 | convolution fusion | flops 107726080 | bytes 3607040 | tf_op jit(solution)/shard_map/cij,ich->jh/dot_general | solution.py:51
  120.4 1.1 fusion.26
  121.5 1.0 copy.142
  122.5 0.2 reduce-scatter.9.cloned.1.call-start
  122.8 1.9 convolution_bitcast_fusion.3
  124.7 1.9 convolution_bitcast_fusion.1
  126.7 1.9 convolution_bitcast_fusion.2
  128.7 2.6 convolution_bitcast_fusion
  131.3 0.9 fusion.25
  132.3 1.0 copy.144
  133.3 4.8 %bitcast_convert_fusion = (bf16[128,5,128]{0,2,1:T(8,128)(2,1)S(1)}, f32[128,5,128]{2,0,1:T(8,128)}) fusion(bf16[640,128,1]{1,0,2:T(8,128)(2,1)} %copy-done.18, f32[640,128,5]{1,0,2:T(8,128)} %fusion.60, f32[5,128]{1,0:T(8,128)S(1)} %get-tuple-element.32, f32[5,128,640]{1,2,0:T(8,128)} %get-tuple-element.33), kind=kOutput, calls=%fused_computation.89 | convolution fusion | flops 107808000 | bytes 3934720 | tf_op jit(solution)/shard_map/cij,jh->ich/dot_general | solution.py:46
  138.1 4.6 %bitcast_convert_fusion.3 = (bf16[128,5,128]{0,2,1:T(8,128)(2,1)S(1)}, f32[128,5,128]{2,0,1:T(8,128)}) fusion(f32[640,128,5]{1,0,2:T(8,128)} %fusion.47, f32[5,128]{1,0:T(8,128)S(1)} %get-tuple-element.44, f32[5,128,640]{1,2,0:T(8,128)} %get-tuple-element.45, bf16[512,512]{1,0:T(8,128)(2,1)S(1)} %bitcast.302, bf16[128,512]{1,0:T(8,128)(2,1)S(1)} %bitcast.343), kind=kOutput, calls=%fused_computation.92 | convolution fusion | flops 108135680 | bytes 7708672 | tf_op jit(solution)/shard_map/cij,jh->ich/dot_general | solution.py:46
  142.7 4.6 %bitcast_convert_fusion.1 = (bf16[128,5,128]{0,2,1:T(8,128)(2,1)S(1)}, f32[128,5,128]{2,0,1:T(8,128)}) fusion(f32[640,128,5]{1,0,2:T(8,128)} %fusion.43, f32[5,128]{1,0:T(8,128)S(1)} %get-tuple-element.36, f32[5,128,640]{1,2,0:T(8,128)} %get-tuple-element.37, bf16[512,512]{1,0:T(8,128)(2,1)S(1)} %bitcast.303, bf16[128,512]{1,0:T(8,128)(2,1)S(1)} %bitcast.344), kind=kOutput, calls=%fused_computation.90 | convolution fusion | flops 108135680 | bytes 7708672 | tf_op jit(solution)/shard_map/cij,jh->ich/dot_general | solution.py:46
  147.5 0.2 copy.98
  147.8 3.7 %bitcast_convert_fusion.2 = (bf16[128,5,128]{0,2,1:T(8,128)(2,1)}, f32[128,5,128]{2,0,1:T(8,128)}) fusion(f32[640,128,5]{1,0,2:T(8,128)S(1)} %fusion.51, f32[5,128]{1,0:T(8,128)S(1)} %get-tuple-element.40, f32[5,128,640]{1,2,0:T(8,128)} %get-tuple-element.41, bf16[512,512]{1,0:T(8,128)(2,1)S(1)} %bitcast.304, bf16[128,512]{1,0:T(8,128)(2,1)} %bitcast.341), kind=kOutput, calls=%fused_computation.91 | convolution fusion | flops 108135680 | bytes 7708672 | tf_op jit(solution)/shard_map/cij,jh->ich/dot_general | solution.py:46
  151.5 1.2 copy.99
  152.7 0.8 copy.110
  153.5 0.8 fusion.65
  154.3 0.8 copy.111
  155.1 0.4 maximum_reduce_fusion
  155.5 97.1 %psum.7 = f32[2560]{0:T(1024)S(1)} all-reduce(f32[2560]{0:T(1024)S(1)} %maximum_reduce_fusion), channel_id=1, replica_groups=mesh['prompt'=32,'resp'=16] {'prompt','resp'}, use_global_device_ids=true, to_apply=%region_15.16 | all-reduce | flops 2560 | bytes 20480 | tf_op jit(solution)/shard_map/psum | solution.py:92
  252.6 0.6 broadcast_multiply_fusion
  253.2 0.9 pad_maximum_fusion.6
  254.1 0.9 copy.143
  255.0 0.7 copy.112
  255.7 10.0 %reduce-scatter.9.cloned.1.call-done = bf16[32,512]{1,0:T(8,128)(2,1)} async-done(((bf16[512,512]{1,0:T(8,128)(2,1)}), bf16[32,512]{1,0:T(8,128)(2,1)}) %reduce-scatter.9.cloned.1.call-update) | async-done | bytes 32784
  265.7 0.9 copy.145
  266.6 0.7 copy.113
  (57 shorter events, 0.6 us)
Async XLA Ops:
  7.2 77.4 %copy-start.22 = (f32[2560]{0:T(1024)S(1)}, f32[2560]{0:T(1024)}, u32[]{:S(2)}) copy-start(f32[2560]{0:T(1024)} %param.13) | copy-start | bytes 30724
  7.2 247.0 %reduce-scatter.7.cloned.1.call-start = ((), (), s32[]{:S(2)}) async-start(), calls=%async_computation.2 | async-start | bytes 557056
  84.5 1.2 copy-start.1
  85.8 18.3 %copy-start.12 = (bf16[128,640]{0,1:T(8,128)(2,1)}, bf16[128,640]{0,1:T(8,128)(2,1)S(1)}, u32[]{:S(2)}) copy-start(bf16[128,640]{0,1:T(8,128)(2,1)S(1)} %get-tuple-element.25) | copy-start | bytes 491524
  86.1 0.9 copy-start
  91.7 0.9 copy-start.19
  92.7 8.7 %copy-start.18 = (bf16[640,128,1]{1,0,2:T(8,128)(2,1)}, bf16[640,128,1]{1,0,2:T(8,128)(2,1)S(1)}, u32[]{:S(2)}) copy-start(bf16[640,128,1]{1,0,2:T(8,128)(2,1)S(1)} %fusion.63) | copy-start | bytes 491524
  93.0 2.8 %copy-start.21 = (pred[128,640]{0,1:T(8,128)(4,1)}, pred[128,640]{0,1:T(8,128)(4,1)S(1)}, u32[]{:S(2)}) copy-start(pred[128,640]{0,1:T(8,128)(4,1)S(1)} %fusion.40) | copy-start | bytes 245764
  93.0 2.8 %copy-start.16 = (bf16[128,640]{0,1:T(8,128)(2,1)S(1)}, bf16[128,640]{0,1:T(8,128)(2,1)}, u32[]{:S(2)}) copy-start(bf16[128,640]{0,1:T(8,128)(2,1)} %get-tuple-element.26) | copy-start | bytes 491524
  95.8 2.8 %copy-start.14 = (bf16[128,640]{0,1:T(8,128)(2,1)S(1)}, bf16[128,640]{0,1:T(8,128)(2,1)}, u32[]{:S(2)}) copy-start(bf16[128,640]{0,1:T(8,128)(2,1)} %get-tuple-element.27) | copy-start | bytes 491524
  122.5 2.2 copy-start.17
  122.5 143.2 %reduce-scatter.9.cloned.1.call-start = ((), (), s32[]{:S(2)}) async-start(), calls=%async_computation.3 | async-start | bytes 557056
  124.7 6.6 %copy-start.5 = (bf16[640,128]{0,1:T(8,128)(2,1)}, bf16[640,128]{0,1:T(8,128)(2,1)S(1)}, u32[]{:S(2)}) copy-start(bf16[640,128]{0,1:T(8,128)(2,1)S(1)} %convolution_bitcast_fusion.3) | copy-start | bytes 491524
  124.7 2.0 copy-start.15
  126.7 4.6 %copy-start.6 = (bf16[640,128]{0,1:T(8,128)(2,1)}, bf16[640,128]{0,1:T(8,128)(2,1)S(1)}, u32[]{:S(2)}) copy-start(bf16[640,128]{0,1:T(8,128)(2,1)S(1)} %convolution_bitcast_fusion.1) | copy-start | bytes 491524
  126.7 2.0 copy-start.13
  128.7 2.7 copy-start.7
  133.3 4.8 %copy-start.20 = (bf16[1,1,128,512]{3,2,1,0:T(8,128)(2,1)S(1)}, bf16[1,1,128,512]{3,2,1,0:T(8,128)(2,1)}, u32[]{:S(2)}) copy-start(bf16[1,1,128,512]{3,2,1,0:T(8,128)(2,1)} %param.11) | copy-start | bytes 393220
  147.8 4.9 %copy-start.2 = (bf16[640,128]{0,1:T(8,128)(2,1)S(1)}, bf16[640,128]{0,1:T(8,128)(2,1)}, u32[]{:S(2)}) copy-start(bf16[640,128]{0,1:T(8,128)(2,1)} %convolution_bitcast_fusion.7) | copy-start | bytes 491524
  147.8 4.9 %copy-start.3 = (bf16[640,128]{0,1:T(8,128)(2,1)S(1)}, bf16[640,128]{0,1:T(8,128)(2,1)}, u32[]{:S(2)}) copy-start(bf16[640,128]{0,1:T(8,128)(2,1)} %convolution_bitcast_fusion.5) | copy-start | bytes 491524
  147.8 4.9 %copy-start.4 = (bf16[640,128]{0,1:T(8,128)(2,1)S(1)}, bf16[640,128]{0,1:T(8,128)(2,1)}, u32[]{:S(2)}) copy-start(bf16[640,128]{0,1:T(8,128)(2,1)} %convolution_bitcast_fusion.6) | copy-start | bytes 491524
  151.5 3.6 %copy-start.8 = (f32[128,5,128]{2,0,1:T(8,128)S(1)}, f32[128,5,128]{2,0,1:T(8,128)}, u32[]{:S(2)}) copy-start(f32[128,5,128]{2,0,1:T(8,128)} %get-tuple-element.35) | copy-start | bytes 983044
  151.5 3.6 %copy-start.9 = (f32[128,5,128]{2,0,1:T(8,128)S(1)}, f32[128,5,128]{2,0,1:T(8,128)}, u32[]{:S(2)}) copy-start(f32[128,5,128]{2,0,1:T(8,128)} %get-tuple-element.47) | copy-start | bytes 983044
  151.5 3.6 %copy-start.10 = (f32[128,5,128]{2,0,1:T(8,128)S(1)}, f32[128,5,128]{2,0,1:T(8,128)}, u32[]{:S(2)}) copy-start(f32[128,5,128]{2,0,1:T(8,128)} %get-tuple-element.39) | copy-start | bytes 983044
  151.5 3.6 %copy-start.11 = (f32[128,5,128]{2,0,1:T(8,128)S(1)}, f32[128,5,128]{2,0,1:T(8,128)}, u32[]{:S(2)}) copy-start(f32[128,5,128]{2,0,1:T(8,128)} %get-tuple-element.43) | copy-start | bytes 983044
Sparse Core Ops, SparseCore 0:
  122.6 70.4 reduce-scatter.6
  196.1 69.5 reduce-scatter.8
where the time goes:
time: 275 us; the launch traced here: 274 us
  blocking collectives  172 us (63%)
  matrix products  58.6 us (21%)
  between operations  15 us (5%)
  local copies, waits for them, and re-layouts  12.4 us (5%)
  waiting for transfers between devices  10 us (4%)
  other arithmetic  5.55 us (2%)
    psum x1, blocking collectives, body(): bias_sum = lax.psum(jnp.sum(grad_q, 0), ('prompt', 'resp'))  97.1 us
    all_gather x1, blocking collectives, body(): lax.all_gather(prefix_keys[0], 'resp', axis=0, tiled=True)  42.6 us
    all_gather x1, blocking collectives, body(): lax.all_gather(prefix_values[0], 'resp', axis=0, tiled=True)  32.6 us
    dot_general x4, matrix products, attend_groups(): jnp.einsum('cij,jh->ich', dscores, k_group, preferred_element_type=jnp.fl...  17.6 us
    dot_general x4, matrix products, attend_groups(): jnp.einsum('cij,ich->jh', dscores, q_group, preferred_element_type=jnp.fl...  16.4 us
    sub x4, matrix products, attend_groups(): expd = jnp.exp(scores - top)  11 us
    unnamed x4, waiting for transfers between devices  10 us
    unnamed x56, local copies, waits for them, and re-layouts  9.88 us
  transfers between devices with their start and end apart: 2, of which 1 were waited for; matrix products, arithmetic and copies ran while one was open for 13% of the time, Pallas kernels for 0%

commit v1 on v0

v1 whole, which is shorter than its diff:
```python
import functools
import math

import jax
import jax.numpy as jnp
from jax import lax
from jax.experimental import pallas as pl
from jax.experimental.pallas import tpu as pltpu
from jax.sharding import PartitionSpec as P

HD = 128
GROUP = 5
KVH = 4
SCALE = 1.0 / math.sqrt(HD)
LOG2E = 1.4426950408889634
F32 = jnp.float32
BF16 = jnp.bfloat16


def dot(a, b, a_dim, b_dim):
    return lax.dot_general(a, b, (((a_dim,), (b_dim,)), ((), ())), preferred_element_type=F32)


def attend_kernel(
    length_ref, q_ref, bias_ref, do_ref, rk_ref, rv_ref, kv_ref,
    dq_ref, drk_ref, drv_ref, pre_ref, bias_sum, probs_s, dscores_s, q_s, do_s,
):
    group = pl.program_id(0)
    length = length_ref[0, 0]
    rows = q_ref.shape[0]
    shards, _, shard_rows, _ = kv_ref.shape
    prefix = shards * shard_rows
    keys = jnp.concatenate([kv_ref[:, 0].reshape(prefix, HD), rk_ref[...]], 0)
    values = jnp.concatenate([kv_ref[:, 1].reshape(prefix, HD), rv_ref[...]], 0)
    live = lax.broadcasted_iota(jnp.int32, (rows, HD), 0) < length
    key_at = lax.broadcasted_iota(jnp.int32, (rows, rows), 0)
    row_at = lax.broadcasted_iota(jnp.int32, (rows, rows), 1)
    visible = (key_at <= row_at) & (key_at < length)
    for head in range(GROUP):
        cols = slice(head * HD, (head + 1) * HD)
        span = slice(head * rows, (head + 1) * rows)
        q = (q_ref[:, cols].astype(F32) + bias_ref[:, cols]).astype(BF16)
        do = jnp.where(live, do_ref[:, cols].astype(F32), 0.0).astype(BF16)
        q_s[span, :] = q
        do_s[span, :] = do
        scores = dot(keys, q, 1, 1) * (SCALE * LOG2E)
        scores = jnp.concatenate(
            [scores[:prefix], jnp.where(visible, scores[prefix:], -jnp.inf)], 0
        )
        expd = jnp.exp2(scores - jnp.max(scores, 0, keepdims=True))
        inverse = 1.0 / jnp.sum(expd, 0, keepdims=True)
        probs = expd * inverse
        dprobs = dot(values, do, 1, 1)
        delta = jnp.sum(probs * dprobs, 0, keepdims=True)
        probs_s[:, span] = probs.astype(BF16)
        dscores_s[:, span] = (probs * (dprobs - delta) * SCALE).astype(BF16)
    dscores = dscores_s[...]
    dk = dot(dscores, q_s[...], 1, 0)
    dv = dot(probs_s[...], do_s[...], 1, 0)
    pre_ref[:, 2 * group] = dk[:prefix].astype(BF16).reshape(shards, shard_rows, HD)
    pre_ref[:, 2 * group + 1] = dv[:prefix].astype(BF16).reshape(shards, shard_rows, HD)
    drk_ref[...] = dk[prefix:].astype(BF16)
    drv_ref[...] = dv[prefix:].astype(BF16)
    dq_t = dot(keys, dscores, 0, 0)
    for head in range(GROUP):
        dq = dq_t[:, head * rows : (head + 1) * rows].T
        dq_ref[:, head * HD : (head + 1) * HD] = dq.astype(BF16)
        bias_sum[pl.ds(group * GROUP + head, 1), :] = jnp.sum(dq, 0, keepdims=True)

    @pl.when(group == pl.num_programs(0) - 1)
    def _():
        per = 2
        heads = KVH * GROUP
        total = bias_sum[...]
        high = total.astype(BF16).astype(F32)
        middle = (total - high).astype(BF16).astype(F32)
        low = total - high - middle
        for shard in range(shards):
            if shard * per < heads:
                at = slice(shard * per, (shard + 1) * per)
                block = jnp.concatenate(
                    [high[at], middle[at], low[at], jnp.zeros((shard_rows - 3 * per, HD), F32)], 0
                )
            else:
                block = jnp.zeros((shard_rows, HD), F32)
            pre_ref[shard, 2 * KVH] = block.astype(BF16)


def attend(length, queries, bias, cotangent, resp_keys, resp_values, gathered):
    rows, width = queries.shape
    shards, _, shard_rows, _ = gathered.shape
    key_count = shards * shard_rows + rows
    wide = GROUP * HD
    heads_out = 2 * KVH + 1
    column = lambda g: (0, g)
    return pl.pallas_call(
        attend_kernel,
        grid=(KVH,),
        out_shape=(
            jax.ShapeDtypeStruct((rows, width), BF16),
            jax.ShapeDtypeStruct((rows, KVH * HD), BF16),
            jax.ShapeDtypeStruct((rows, KVH * HD), BF16),
            jax.ShapeDtypeStruct((shards, heads_out, shard_rows, HD), BF16),
        ),
        in_specs=[
            pl.BlockSpec(memory_space=pltpu.SMEM),
            pl.BlockSpec((rows, wide), column),
            pl.BlockSpec((1, wide), column),
            pl.BlockSpec((rows, wide), column),
            pl.BlockSpec((rows, HD), column),
            pl.BlockSpec((rows, HD), column),
            pl.BlockSpec((shards, 2, shard_rows, HD), lambda g: (0, g, 0, 0)),
        ],
        out_specs=(
            pl.BlockSpec((rows, wide), column),
            pl.BlockSpec((rows, HD), column),
            pl.BlockSpec((rows, HD), column),
            pl.BlockSpec((shards, heads_out, shard_rows, HD), lambda g: (0, 0, 0, 0)),
        ),
        scratch_shapes=[
            pltpu.VMEM((KVH * GROUP, HD), F32),
            pltpu.VMEM((key_count, GROUP * rows), BF16),
            pltpu.VMEM((key_count, GROUP * rows), BF16),
            pltpu.VMEM((GROUP * rows, HD), BF16),
            pltpu.VMEM((GROUP * rows, HD), BF16),
        ],
        compiler_params=pltpu.CompilerParams(
            dimension_semantics=("arbitrary",), vmem_limit_bytes=48 * 1024 * 1024
        ),
        cost_estimate=pl.CostEstimate(
            flops=10 * rows * width * key_count,
            transcendentals=rows * width // HD * key_count,
            bytes_accessed=8 * 1024 * 1024,
        ),
    )(length, queries, bias, cotangent, resp_keys, resp_values, gathered)


def spread(block, axis):
    copies = jnp.broadcast_to(block[None], (lax.axis_size(axis), *block.shape))
    return lax.all_to_all(copies, axis, 0, 0)


def body(
    prefix_keys, prefix_values, resp_queries, resp_keys, resp_values, query_bias, out_grad, lengths
):
    shard_rows = prefix_keys.shape[1]
    rows, width = resp_queries.shape[2:]
    shard = jnp.stack(
        [
            prefix_keys[0].reshape(shard_rows, KVH, HD),
            prefix_values[0].reshape(shard_rows, KVH, HD),
        ],
        2,
    )
    shard = shard.reshape(shard_rows, 2 * KVH, HD).transpose(1, 0, 2)
    gathered = spread(shard, "resp")
    dq, drk, drv, partial = attend(
        lengths, resp_queries[0, 0], query_bias[None, :], out_grad[0, 0],
        resp_keys[0, 0], resp_values[0, 0], gathered,
    )
    summed = jnp.sum(lax.all_to_all(partial, "resp", 0, 0).astype(F32), 0)
    prefix = summed[: 2 * KVH].astype(BF16).reshape(KVH, 2, shard_rows, HD)
    prefix = prefix.transpose(1, 2, 0, 3).reshape(2, shard_rows, KVH * HD)
    bias = summed[2 * KVH, :6].reshape(3, 2, HD).sum(0)
    bias = jnp.sum(spread(bias, "prompt"), 0)
    bias = spread(bias, "resp").reshape(-1)[:width]
    count = lax.axis_size("prompt") * lax.axis_size("resp") * rows
    return (
        dq[None, None],
        drk[None, None],
        drv[None, None],
        prefix[:1],
        prefix[1:],
        bias / math.sqrt(count),
    )


def solution(mesh):
    return jax.shard_map(
        body,
        mesh=mesh,
        in_specs=(
            P("prompt", "resp", None),
            P("prompt", "resp", None),
            P("prompt", "resp", None, None),
            P("prompt", "resp", None, None),
            P("prompt", "resp", None, None),
            P(),
            P("prompt", "resp", None, None),
            P("prompt", "resp"),
        ),
        out_specs=(
            P("prompt", "resp", None, None),
            P("prompt", "resp", None, None),
            P("prompt", "resp", None, None),
            P("prompt", "resp", None),
            P("prompt", "resp", None),
            P(),
        ),
        check_vma=False,
    )
```

time: 275 us -> 122 us (0.44)
  blocking collectives: 172 us -> 37.5 us
  matrix products: 58.6 us -> 0 us
  waiting for transfers between devices: 10 us -> 41.1 us
  starting transfers between devices: 0.26 us -> 24.5 us
  between operations: 15 us -> 1.4 us
  Pallas kernels: 0 us -> 9.72 us
  local copies, waits for them, and re-layouts: 12.4 us -> 5.27 us
  other arithmetic: 5.55 us -> 0.28 us
    psum x1 -> x0, blocking collectives: 97.1 us -> none  [body(): bias_sum = lax.psum(jnp.sum(grad_q, 0), ('prompt', 'resp'))]
    all_gather x2 -> x0, blocking collectives: 75.2 us -> none  [the longest x1 42.6 us: body(): lax.all_gather(prefix_keys[0], 'resp', axis=0, tiled=True)]
    dot_general x16 -> x0, matrix products: 47.6 us -> none  [the longest x4 17.6 us: attend_groups(): jnp.einsum('cij,jh->ich', dscores, k_group, preferred_element_type=jnp.fl...]
    all_to_all x0 -> x3, waiting for transfers between devices: none -> 41.1 us  [spread(): return lax.all_to_all(copies, axis, 0, 0)]
    all_to_all x0 -> x1, blocking collectives: none -> 37.5 us  [body(): summed = jnp.sum(lax.all_to_all(partial, 'resp', 0, 0).astype(F32), 0)]
    all_to_all x0 -> x3, starting transfers between devices: none -> 24.5 us  [spread(): return lax.all_to_all(copies, axis, 0, 0)]
    sub x4 -> x0, matrix products: 11 us -> none  [attend_groups(): expd = jnp.exp(scores - top)]
    unnamed x4 -> x0, waiting for transfers between devices: 10 us -> none
  transfers between devices with their start and end apart: 2 -> 3, of which waited for: 1 -> 3; matrix products, arithmetic and copies ran while one was open for 13% -> 1% of each run, Pallas kernels for 0% -> 0%
where the time goes in v1:
time: 122 us; the launch traced here: 120 us
  waiting for transfers between devices  41.1 us (34%)
  blocking collectives  37.5 us (31%)
  starting transfers between devices  24.5 us (20%)
  Pallas kernels  9.72 us (8%)
  local copies, waits for them, and re-layouts  5.27 us (4%)
  between operations  1.4 us (1%)
    all_to_all x3, waiting for transfers between devices, spread(): return lax.all_to_all(copies, axis, 0, 0)  41.1 us
    all_to_all x1, blocking collectives, body(): summed = jnp.sum(lax.all_to_all(partial, 'resp', 0, 0).astype(F32), 0)  37.5 us
    all_to_all x3, starting transfers between devices, spread(): return lax.all_to_all(copies, axis, 0, 0)  24.5 us
    pallas_call x1, Pallas kernels, attend(): pl.pallas_call(attend_kernel, grid=(KVH,), out_shape=(jax.ShapeDtypeStruc...  9.72 us
  transfers between devices with their start and end apart: 3, of which 3 were waited for; matrix products, arithmetic and copies ran while one was open for 1% of the time, Pallas kernels for 0%

profile of v1, /device:TPU:6, one launch (start us, length us, event | category | flops | bytes accessed | tf_op | source)
XLA Modules:
  0.0 119.8 jit_solution(201073989821668636)
XLA Ops:
  0.6 0.8 stack_reshape_squeeze.6
  1.4 0.8 stack_reshape_squeeze.7
  2.3 1.2 broadcast_in_dim.15
  3.4 0.0 copy-start.4
  3.4 0.0 copy-start
  3.4 0.0 copy-start.1
  3.4 0.0 copy-start.2
  3.4 0.0 copy-start.3
  3.5 11.6 %all-to-all-start = ((bf16[16,8,32,128]{3,2,1,0:T(8,128)(2,1)}), bf16[16,8,32,128]{3,2,1,0:T(8,128)(2,1)S(1)}, u32[]{:S(2)}, u32[]{:S(2)}) async-start(bf16[16,8,32,128]{3,2,1,0:T(8,128)(2,1)} %broadcast_in_dim.15), calls=%async_computation | async-start | bytes 2097152 | tf_op jit(solution)/shard_map/all_to_all | solution.py:140
  15.7 0.0 copy-done.4
  15.7 25.2 %all-to-all-done.kv_ref = bf16[16,8,32,128]{3,2,1,0:T(8,128)(2,1)S(1)} async-done(((bf16[16,8,32,128]{3,2,1,0:T(8,128)(2,1)}), bf16[16,8,32,128]{3,2,1,0:T(8,128)(2,1)S(1)}, u32[]{:S(2)}, u32[]{:S(2)}) %all-to-all-start) | async-done | bytes 1048608 | tf_op jit(solution)/shard_map/all_to_all | solution.py:140
  40.9 0.0 copy-done
  40.9 0.0 copy-done.1
  40.9 0.0 copy-done.2
  40.9 0.0 copy-done.3
  40.9 9.7 %shard_map.127 = (bf16[128,2560]{1,0:T(8,128)(2,1)}, bf16[128,512]{1,0:T(8,128)(2,1)}, bf16[128,512]{1,0:T(8,128)(2,1)}, bf16[16,9,32,128]{3,2,1,0:T(8,128)(2,1)S(1)}) custom-call(s32[1,1]{1,0:T(1,128)S(6)} %copy.33.length_ref, bf16[128,2560]{1,0:T(8,128)(2,1)S(1)} %bitcast.23, f32[1,2560]{1,0:T(1,128)S(1)} %broadcast_in_dim.14.bias_ref, ...), custom_call_target="tpu_custom_call" | custom-call | flops 2097152000 | bytes 8388608 | tf_op jit(solution)/shard_map/pallas_call | solution.py:96
  50.7 37.5 %all_to_all.20 = bf16[16,9,32,128]{3,2,1,0:T(8,128)(2,1)S(1)} all-to-all(bf16[16,9,32,128]{3,2,1,0:T(8,128)(2,1)S(1)} %get-tuple-element.13), channel_id=1, replica_groups=mesh['prompt'=32,'resp'=16] {'resp'}, dimensions={0} | all-to-all | bytes 2359296 | tf_op jit(solution)/shard_map/all_to_all | solution.py:161
  88.2 0.2 convert_reduce_fusion
  88.4 0.6 broadcast_in_dim.35
  89.0 9.3 %all-to-all-start.2 = ((f32[32,2,128]{2,1,0:T(2,128)}), f32[32,2,128]{2,1,0:T(2,128)S(1)}, u32[]{:S(2)}, u32[]{:S(2)}) async-start(f32[32,2,128]{2,1,0:T(2,128)} %broadcast_in_dim.35), calls=%async_computation.2 | async-start | bytes 65536 | tf_op jit(solution)/shard_map/all_to_all | solution.py:140
  98.3 8.0 %all-to-all-done.2 = f32[32,2,128]{2,1,0:T(2,128)S(1)} async-done(((f32[32,2,128]{2,1,0:T(2,128)}), f32[32,2,128]{2,1,0:T(2,128)S(1)}, u32[]{:S(2)}, u32[]{:S(2)}) %all-to-all-start.2) | async-done | bytes 32800 | tf_op jit(solution)/shard_map/all_to_all | solution.py:140
  106.4 0.6 broadcast_in_dim.36
  107.0 3.7 %all-to-all-start.3 = ((f32[16,2,128]{2,1,0:T(2,128)}), f32[16,2,128]{2,1,0:T(2,128)S(1)}, u32[]{:S(2)}, u32[]{:S(2)}) async-start(f32[16,2,128]{2,1,0:T(2,128)} %broadcast_in_dim.36), calls=%async_computation.3 | async-start | bytes 32768 | tf_op jit(solution)/shard_map/all_to_all | solution.py:140
  110.7 0.6 copy_bitcast_fusion
  111.3 7.9 %all-to-all-done.3 = f32[16,2,128]{2,1,0:T(2,128)S(1)} async-done(((f32[16,2,128]{2,1,0:T(2,128)}), f32[16,2,128]{2,1,0:T(2,128)S(1)}, u32[]{:S(2)}, u32[]{:S(2)}) %all-to-all-start.3) | async-done | bytes 16416 | tf_op jit(solution)/shard_map/all_to_all | solution.py:140
  119.2 0.6 div.10
  (10 shorter events, 0.2 us)
Async XLA Ops:
  3.4 12.3 %copy-start.4 = (f32[2560]{0:T(1024)S(1)}, f32[2560]{0:T(1024)}, u32[]{:S(2)}) copy-start(f32[2560]{0:T(1024)} %param.13) | copy-start | bytes 30724
  3.4 37.5 %copy-start = (bf16[1,1,128,2560]{3,2,1,0:T(8,128)(2,1)S(1)}, bf16[1,1,128,2560]{3,2,1,0:T(8,128)(2,1)}, u32[]{:S(2)}) copy-start(bf16[1,1,128,2560]{3,2,1,0:T(8,128)(2,1)} %param.10) | copy-start | bytes 1966084
  3.4 37.5 %copy-start.1 = (bf16[1,1,128,2560]{3,2,1,0:T(8,128)(2,1)S(1)}, bf16[1,1,128,2560]{3,2,1,0:T(8,128)(2,1)}, u32[]{:S(2)}) copy-start(bf16[1,1,128,2560]{3,2,1,0:T(8,128)(2,1)} %param.14) | copy-start | bytes 1966084
  3.4 37.5 %copy-start.2 = (bf16[1,1,128,512]{3,2,1,0:T(8,128)(2,1)S(1)}, bf16[1,1,128,512]{3,2,1,0:T(8,128)(2,1)}, u32[]{:S(2)}) copy-start(bf16[1,1,128,512]{3,2,1,0:T(8,128)(2,1)} %param.11) | copy-start | bytes 393220
  3.4 37.5 %copy-start.3 = (bf16[1,1,128,512]{3,2,1,0:T(8,128)(2,1)S(1)}, bf16[1,1,128,512]{3,2,1,0:T(8,128)(2,1)}, u32[]{:S(2)}) copy-start(bf16[1,1,128,512]{3,2,1,0:T(8,128)(2,1)} %param.12) | copy-start | bytes 393220
  3.5 37.5 %all-to-all-start = ((bf16[16,8,32,128]{3,2,1,0:T(8,128)(2,1)}), bf16[16,8,32,128]{3,2,1,0:T(8,128)(2,1)S(1)}, u32[]{:S(2)}, u32[]{:S(2)}) async-start(bf16[16,8,32,128]{3,2,1,0:T(8,128)(2,1)} %broadcast_in_dim.15), calls=%async_computation | async-start | bytes 2097152 | tf_op jit(solution)/shard_map/all_to_all | solution.py:140
  89.0 17.3 %all-to-all-start.2 = ((f32[32,2,128]{2,1,0:T(2,128)}), f32[32,2,128]{2,1,0:T(2,128)S(1)}, u32[]{:S(2)}, u32[]{:S(2)}) async-start(f32[32,2,128]{2,1,0:T(2,128)} %broadcast_in_dim.35), calls=%async_computation.2 | async-start | bytes 65536 | tf_op jit(solution)/shard_map/all_to_all | solution.py:140
  107.0 12.2 %all-to-all-start.3 = ((f32[16,2,128]{2,1,0:T(2,128)}), f32[16,2,128]{2,1,0:T(2,128)S(1)}, u32[]{:S(2)}, u32[]{:S(2)}) async-start(f32[16,2,128]{2,1,0:T(2,128)} %broadcast_in_dim.36), calls=%async_computation.3 | async-start | bytes 32768 | tf_op jit(solution)/shard_map/all_to_all | solution.py:140

commit v2 on v1

v2 whole, which is shorter than its diff:
```python
import functools
import math

import jax
import jax.numpy as jnp
from jax import lax
from jax.experimental import pallas as pl
from jax.experimental.pallas import tpu as pltpu
from jax.sharding import Mesh, PartitionSpec as P

HD = 128
GROUP = 5
KVH = 4
HALVES = 2
PER = KVH // HALVES
SCALE = 1.0 / math.sqrt(HD)
LOG2E = 1.4426950408889634
F32 = jnp.float32
BF16 = jnp.bfloat16

PROMPT = ("yh", "x1", "x0", "core")
RESP = ("yl", "z2", "z1", "z0")
SIZES = (4, 2, 2, 2, 2, 2, 2, 2)
Z = ("z2", "z1", "z0")


def dot(a, b, a_dim, b_dim):
    return lax.dot_general(a, b, (((a_dim,), (b_dim,)), ((), ())), preferred_element_type=F32)


def two_terms(total):
    high = total.astype(BF16)
    return jnp.concatenate([high, (total - high.astype(F32)).astype(BF16)], 1)


def attend_kernel(
    part, length_ref, q_ref, bias_ref, do_ref, rk_ref, rv_ref, k_near, v_near, k_far, v_far, *refs
):
    (dq_ref, drk_ref, drv_ref, near_ref, far_ref, sums_ref, probs_s, dscores_s, q_s, do_s) = refs[-10:]
    group = pl.program_id(0)

    @pl.when(group == 0)
    def _():
        sums_ref[...] = refs[3][...] if part else jnp.zeros_like(sums_ref)

    length = length_ref[0, 0]
    rows = q_ref.shape[0]
    shards, shard_rows, _ = k_near.shape
    half = shards * shard_rows
    prefix = 2 * half
    keys = jnp.concatenate(
        [k_near[...].reshape(half, HD), k_far[...].reshape(half, HD), rk_ref[...]], 0
    )
    values = jnp.concatenate(
        [v_near[...].reshape(half, HD), v_far[...].reshape(half, HD), rv_ref[...]], 0
    )
    live = lax.broadcasted_iota(jnp.int32, (rows, HD), 0) < length
    key_at = lax.broadcasted_iota(jnp.int32, (rows, rows), 0)
    row_at = lax.broadcasted_iota(jnp.int32, (rows, rows), 1)
    visible = (key_at <= row_at) & (key_at < length)
    for head in range(GROUP):
        cols = slice(head * HD, (head + 1) * HD)
        span = slice(head * rows, (head + 1) * rows)
        q = (q_ref[:, cols].astype(F32) + bias_ref[:, cols]).astype(BF16)
        do = jnp.where(live, do_ref[:, cols].astype(F32), 0.0).astype(BF16)
        q_s[span, :] = q
        do_s[span, :] = do
        scores = dot(keys, q, 1, 1) * (SCALE * LOG2E)
        scores = jnp.concatenate(
            [scores[:prefix], jnp.where(visible, scores[prefix:], -jnp.inf)], 0
        )
        expd = jnp.exp2(scores - jnp.max(scores, 0, keepdims=True))
        inverse = 1.0 / jnp.sum(expd, 0, keepdims=True)
        probs = expd * inverse
        dprobs = dot(values, do, 1, 1)
        delta = jnp.sum(probs * dprobs, 0, keepdims=True)
        probs_s[:, span] = probs.astype(BF16)
        dscores_s[:, span] = (probs * (dprobs - delta) * SCALE).astype(BF16)
    dscores = dscores_s[...]
    dk = dot(dscores, q_s[...], 1, 0)
    dv = dot(probs_s[...], do_s[...], 1, 0)
    for block, at in ((dk, group), (dv, PER + group)):
        lanes = pl.ds(pl.multiple_of(at * HD, HD), HD)
        block = block[:prefix].astype(BF16).reshape(2, shards, shard_rows, HD)
        near_ref[:, :, lanes] = block[0]
        far_ref[:shards, :, lanes] = block[1]
    drk_ref[...] = dk[prefix:].astype(BF16)
    drv_ref[...] = dv[prefix:].astype(BF16)
    dq_t = dot(keys, dscores, 0, 0)
    for head in range(GROUP):
        dq = dq_t[:, head * rows : (head + 1) * rows].T
        dq_ref[:, head * HD : (head + 1) * HD] = dq.astype(BF16)
        row = part * PER * GROUP + group * GROUP + head
        sums_ref[pl.ds(row, 1), :] = jnp.sum(dq, 0, keepdims=True)

    if part == HALVES - 1:

        @pl.when(group == PER - 1)
        def _():
            far_ref[shards, :, : 2 * HD] = two_terms(sums_ref[...])
            far_ref[shards, :, 2 * HD :] = jnp.zeros((shard_rows, (2 * PER - 2) * HD), BF16)


def attend(part, length, queries, bias, cotangent, resp_keys, resp_values, near, far, before):
    rows, width = queries.shape
    shards, shard_rows, _ = near.shape
    key_count = 2 * shards * shard_rows + rows
    slots = shards + (part == HALVES - 1)
    wide = GROUP * HD
    column = lambda g: (0, part * PER + g)
    block = (shards, shard_rows, HD)
    whole = (shards, shard_rows, 2 * PER * HD)
    sums = pl.BlockSpec((shard_rows, HD), lambda g: (0, 0))
    return pl.pallas_call(
        functools.partial(attend_kernel, part),
        grid=(PER,),
        out_shape=(
            jax.ShapeDtypeStruct((rows, width), BF16),
            jax.ShapeDtypeStruct((rows, KVH * HD), BF16),
            jax.ShapeDtypeStruct((rows, KVH * HD), BF16),
            jax.ShapeDtypeStruct(whole, BF16),
            jax.ShapeDtypeStruct((slots, *whole[1:]), BF16),
            jax.ShapeDtypeStruct((shard_rows, HD), F32),
        ),
        in_specs=[
            pl.BlockSpec(memory_space=pltpu.SMEM),
            pl.BlockSpec((rows, wide), column),
            pl.BlockSpec((1, wide), column),
            pl.BlockSpec((rows, wide), column),
            pl.BlockSpec((rows, HD), column),
            pl.BlockSpec((rows, HD), column),
            pl.BlockSpec(block, lambda g: (0, 0, part * 2 * PER + g)),
            pl.BlockSpec(block, lambda g: (0, 0, part * 2 * PER + PER + g)),
            pl.BlockSpec(block, lambda g: (0, 0, g)),
            pl.BlockSpec(block, lambda g: (0, 0, PER + g)),
            *[pl.BlockSpec(memory_space=pl.ANY)] * 3 * part,
            *[sums] * part,
        ],
        out_specs=(
            pl.BlockSpec((rows, wide), column),
            pl.BlockSpec((rows, HD), column),
            pl.BlockSpec((rows, HD), column),
            pl.BlockSpec(whole, lambda g: (0, 0, 0)),
            pl.BlockSpec((slots, *whole[1:]), lambda g: (0, 0, 0)),
            sums,
        ),
        scratch_shapes=[
            pltpu.VMEM((key_count, GROUP * rows), BF16),
            pltpu.VMEM((key_count, GROUP * rows), BF16),
            pltpu.VMEM((GROUP * rows, HD), BF16),
            pltpu.VMEM((GROUP * rows, HD), BF16),
        ],
        input_output_aliases={10 + i: i for i in range(3 * part)},
        compiler_params=pltpu.CompilerParams(
            dimension_semantics=("arbitrary",), vmem_limit_bytes=32 * 1024 * 1024
        ),
        cost_estimate=pl.CostEstimate(
            flops=10 * rows * width * key_count // HALVES,
            transcendentals=rows * width // HD * key_count // HALVES,
            bytes_accessed=4 * 1024 * 1024,
        ),
    )(length, queries, bias, cotangent, resp_keys, resp_values, near, near, far, far, *before)


def pair_kernel(near_a, got_a, near_b, got_b, sums, out):
    wide = near_a.shape[2]
    shards = out.shape[0]
    out[:, :, :wide] = (near_a[...].astype(F32) + got_a[...].astype(F32)).astype(BF16)
    got = got_b[:shards].astype(F32)
    out[:, :, wide : 2 * wide] = (near_b[...].astype(F32) + got).astype(BF16)
    terms = two_terms(sums[...])
    for shard in range(shards):
        out[shard, :, 2 * wide :] = terms


def finish_kernel(got, dk_ref, dv_ref, sums_ref):
    lanes = PER * HD
    total = got[0].astype(F32)
    for shard in range(1, got.shape[0]):
        total = total + got[shard].astype(F32)
    for part in range(HALVES):
        for at, ref in enumerate((dk_ref, dv_ref)):
            start = (2 * part + at) * lanes
            ref[:, part * lanes : (part + 1) * lanes] = total[:, start : start + lanes].astype(BF16)
    sums = total[:, 4 * lanes : 4 * lanes + HD] + total[:, 4 * lanes + HD :]
    for shard in range(sums_ref.shape[0]):
        sums_ref[shard] = sums[: sums_ref.shape[1]]


def spread(block, axis):
    copies = jnp.broadcast_to(block[None], (lax.axis_size(axis), *block.shape))
    return lax.all_to_all(copies, axis, 0, 0)


def swap(block, axis):
    return lax.ppermute(block, axis, [(0, 1), (1, 0)])


def body(
    prefix_keys, prefix_values, resp_queries, resp_keys, resp_values, query_bias, out_grad, lengths
):
    rows, width = resp_queries.shape[2:]
    shard_rows = prefix_keys.shape[1]
    lanes = PER * HD
    shard = jnp.concatenate(
        [
            array[0][:, part * lanes : (part + 1) * lanes]
            for part in range(HALVES)
            for array in (prefix_keys, prefix_values)
        ],
        1,
    )
    near = spread(shard, Z)
    wide = 2 * lanes
    far = [swap(near[:, :, part * wide : (part + 1) * wide], "yl") for part in range(HALVES)]
    operands = (
        lengths, resp_queries[0, 0], query_bias[None, :], out_grad[0, 0],
        resp_keys[0, 0], resp_values[0, 0], near,
    )
    *outs, near_a, far_a, sums = attend(0, *operands, far[0], ())
    got_a = swap(far_a, "yl")
    dq, drk, drv, near_b, far_b, sums = attend(1, *operands, far[1], (*outs, sums))
    far_b, got_a = lax.optimization_barrier((far_b, got_a))
    got_b = swap(far_b, "yl")
    terms = got_b[-1, :, : 2 * HD].astype(F32)
    sums = sums + terms[:, :HD] + terms[:, HD:]
    sums = sums + swap(sums, "core")
    shards = near.shape[0]
    pairs = pl.pallas_call(
        pair_kernel,
        out_shape=jax.ShapeDtypeStruct((shards, shard_rows, 2 * wide + 2 * HD), BF16),
    )(near_a, got_a, near_b, got_b, sums)
    groups = ("yh", "x1", "x0")
    prefix_dk, prefix_dv, sums = pl.pallas_call(
        finish_kernel,
        out_shape=(
            jax.ShapeDtypeStruct((shard_rows, KVH * HD), BF16),
            jax.ShapeDtypeStruct((shard_rows, KVH * HD), BF16),
            jax.ShapeDtypeStruct((lax.axis_size(groups), KVH * GROUP, HD), F32),
        ),
    )(lax.all_to_all(pairs, Z, 0, 0))
    sums = jnp.sum(lax.all_to_all(sums, groups, 0, 0), 0).reshape(width)
    count = math.prod(SIZES) * rows
    return (
        dq[None, None],
        drk[None, None],
        drv[None, None],
        prefix_dk[None],
        prefix_dv[None],
        sums / math.sqrt(count),
    )


def solution(mesh):
    fine = Mesh(mesh.devices.reshape(SIZES), PROMPT + RESP)
    return jax.shard_map(
        body,
        mesh=fine,
        in_specs=(
            P(PROMPT, RESP, None),
            P(PROMPT, RESP, None),
            P(PROMPT, RESP, None, None),
            P(PROMPT, RESP, None, None),
            P(PROMPT, RESP, None, None),
            P(),
            P(PROMPT, RESP, None, None),
            P(PROMPT, RESP),
        ),
        out_specs=(
            P(PROMPT, RESP, None, None),
            P(PROMPT, RESP, None, None),
            P(PROMPT, RESP, None, None),
            P(PROMPT, RESP, None),
            P(PROMPT, RESP, None),
            P(),
        ),
        check_vma=False,
    )
```

time: 122 us -> 118 us (0.967)
  blocking collectives: 37.5 us -> 72.1 us
  waiting for transfers between devices: 41.1 us -> 9.92 us
  starting transfers between devices: 24.5 us -> 15.6 us
  Pallas kernels: 9.72 us -> 14.8 us
  local copies, waits for them, and re-layouts: 5.27 us -> 1.62 us
    all_to_all x3 -> x0, waiting for transfers between devices: 41.1 us -> none  [spread(): return lax.all_to_all(copies, axis, 0, 0)]
    all_to_all x1 -> x3, blocking collectives: 37.5 us -> 72.1 us  [the longest x1 27.7 us: spread(): return lax.all_to_all(copies, axis, 0, 0)]
    all_to_all x3 -> x0, starting transfers between devices: 24.5 us -> none  [spread(): return lax.all_to_all(copies, axis, 0, 0)]
    ppermute x0 -> x5, starting transfers between devices: none -> 15.6 us  [swap(): return lax.ppermute(block, axis, [(0, 1), (1, 0)])]
    ppermute x0 -> x5, waiting for transfers between devices: none -> 9.92 us  [swap(): return lax.ppermute(block, axis, [(0, 1), (1, 0)])]
    pallas_call x1 -> x4, Pallas kernels: 9.72 us -> 14.8 us  [the longest x2 10.7 us: attend(): pl.pallas_call(functools.partial(attend_kernel, part), grid=(PER,), out_s...]
    broadcast_in_dim x3 -> x1, local copies, waits for them, and re-layouts: 2.41 us -> 0.05 us  [spread(): copies = jnp.broadcast_to(block[None], (lax.axis_size(axis), *block.shape))]
    another operation x4 -> x0, local copies, waits for them, and re-layouts: 1.57 us -> none  [the longest x3 1.56 us: body(): jnp.stack([prefix_keys[0].reshape(shard_rows, KVH, HD), prefix_values[0]....]
  transfers between devices with their start and end apart: 3 -> 5, of which waited for: 3 -> 3; matrix products, arithmetic and copies ran while one was open for 1% -> 0% of each run, Pallas kernels for 0% -> 9%
where the time goes in v2:
time: 118 us; the launch traced here: 117 us
  blocking collectives  72.1 us (61%)
  starting transfers between devices  15.6 us (13%)
  Pallas kernels  14.8 us (13%)
  waiting for transfers between devices  9.92 us (8%)
  local copies, waits for them, and re-layouts  1.62 us (1%)
  between operations  1.4 us (1%)
  other arithmetic  1.25 us (1%)
    all_to_all x1, blocking collectives, spread(): return lax.all_to_all(copies, axis, 0, 0)  27.7 us
    all_to_all x1, blocking collectives, body(): lax.all_to_all(pairs, Z, 0, 0)  25.1 us
    all_to_all x1, blocking collectives, body(): sums = jnp.sum(lax.all_to_all(sums, groups, 0, 0), 0).reshape(width)  19.3 us
    ppermute x5, starting transfers between devices, swap(): return lax.ppermute(block, axis, [(0, 1), (1, 0)])  15.6 us
    pallas_call x2, Pallas kernels, attend(): pl.pallas_call(functools.partial(attend_kernel, part), grid=(PER,), out_s...  10.7 us
    ppermute x5, waiting for transfers between devices, swap(): return lax.ppermute(block, axis, [(0, 1), (1, 0)])  9.92 us
  transfers between devices with their start and end apart: 5, of which 3 were waited for; matrix products, arithmetic and copies ran while one was open for 0% of the time, Pallas kernels for 9%

profile of v2, /device:TPU:6, one launch (start us, length us, event | category | flops | bytes accessed | tf_op | source)
XLA Modules:
  0.0 116.7 jit_solution(2090813341702540653)
XLA Ops:
  0.6 0.8 fusion.2
  1.4 0.1 broadcast_in_dim.25
  1.5 0.0 copy-start.1
  1.5 27.7 %all_to_all.15.k_near.v_near = bf16[8,32,1024]{2,1,0:T(8,128)(2,1)S(1)} all-to-all(bf16[8,32,1024]{2,1,0:T(8,128)(2,1)S(1)} %broadcast_in_dim.25), channel_id=1, replica_groups=mesh['yh'=4,'x1'=2,'x0'=2,'core'=2,'yl'=2,'z2'=2,'z1'=2,'z0'=2] {'z2','z..., dimensions={0} | all-to-all | bytes 1048576 | tf_op jit(solution)/shard_map/all_to_all | solution.py:192
  29.2 0.0 copy-start.8
  29.2 0.0 copy-start
  29.2 0.0 copy-start.4
  29.2 0.0 copy-start.5
  29.3 3.6 %collective-permute-start.1 = (bf16[8,32,512]{2,1,0:T(8,128)(2,1)S(1)}, bf16[8,32,512]{2,1,0:T(8,128)(2,1)S(1)}, u32[]{:S(2)}, u32[]{:S(2)}) collective-permute-start(bf16[8,32,512]{2,1,0:T(8,128)(2,1)S(1)} %get-tuple-element.40), channel_id=1, source_target_pairs={{0,8},{8,0},{1,9},{9,1},{2,10},{10,2},{3,11},{11,3},{4,12},{12,4},... | collective-permute-start | bytes 786440 | tf_op jit(solution)/shard_map/ppermute | solution.py:196
  33.6 0.0 copy-done.8
  33.6 2.4 %collective-permute-start = (bf16[8,32,512]{2,1,0:T(8,128)(2,1)S(1)}, bf16[8,32,512]{2,1,0:T(8,128)(2,1)S(1)}, u32[]{:S(2)}, u32[]{:S(2)}) collective-permute-start(bf16[8,32,512]{2,1,0:T(8,128)(2,1)S(1)} %get-tuple-element.41), channel_id=1, source_target_pairs={{0,8},{8,0},{1,9},{9,1},{2,10},{10,2},{3,11},{11,3},{4,12},{12,4},... | collective-permute-start | bytes 786440 | tf_op jit(solution)/shard_map/ppermute | solution.py:196
  36.0 3.6 %collective-permute-done.1.k_far.v_far = bf16[8,32,512]{2,1,0:T(8,128)(2,1)S(1)} collective-permute-done((bf16[8,32,512]{2,1,0:T(8,128)(2,1)S(1)}, bf16[8,32,512]{2,1,0:T(8,128)(2,1)S(1)}, u32[]{:S(2)}, u32[]{:S(2)}) %collective-permute-start.1) | collective-permute-done | bytes 262176 | tf_op jit(solution)/shard_map/ppermute | solution.py:196
  39.5 0.0 copy-done.1
  39.5 0.0 copy-done
  39.5 0.0 copy-done.4
  39.5 0.0 copy-done.5
  39.6 5.3 %shard_map.127 = (bf16[128,2560]{1,0:T(8,128)(2,1)}, bf16[128,512]{1,0:T(8,128)(2,1)}, bf16[128,512]{1,0:T(8,128)(2,1)}, bf16[8,32,512]{2,1,0:T(8,128)(2,1)S(1)}...) custom-call(s32[1,1]{1,0:T(1,128)S(6)} %copy.20.length_ref, bf16[128,2560]{1,0:T(8,128)(2,1)S(1)} %bitcast.18, ...), custom_call_target="tpu_custom_call" | custom-call | flops 1048576000 | bytes 4194304 | tf_op jit(solution)/shard_map/pallas_call | solution.py:114
  44.9 0.0 copy-start.2
  44.9 4.3 %collective-permute-start.2 = (bf16[8,32,512]{2,1,0:T(8,128)(2,1)S(1)}, bf16[8,32,512]{2,1,0:T(8,128)(2,1)S(1)}, u32[]{:S(2)}, u32[]{:S(2)}) collective-permute-start(bf16[8,32,512]{2,1,0:T(8,128)(2,1)S(1)} %get-tuple-element.32), channel_id=1, source_target_pairs={{0,8},{8,0},{1,9},{9,1},{2,10},{10,2},{3,11},{11,3},{4,12},{12,4},... | collective-permute-start | bytes 786440 | tf_op jit(solution)/shard_map/ppermute | solution.py:196
  49.2 0.0 collective-permute-done.k_far.v_far
  49.2 5.4 %shard_map.128 = (bf16[128,2560]{1,0:T(8,128)(2,1)}, bf16[128,512]{1,0:T(8,128)(2,1)}, bf16[128,512]{1,0:T(8,128)(2,1)}, bf16[8,32,512]{2,1,0:T(8,128)(2,1)S(1)}...) custom-call(s32[1,1]{1,0:T(1,128)S(6)} %copy.20.length_ref, ...), custom_call_target="tpu_custom_call", output_to_operand_aliasing={{0}: (10, {}), {1}: (11, {}), {2}: (12, {})} | custom-call | flops 1048576000 | bytes 4194304 | tf_op jit(solution)/shard_map/pallas_call | solution.py:114
  54.6 0.0 copy-done.2
  54.6 0.0 copy-start.3
  54.7 0.7 copy-done.3
  55.4 0.0 collective-permute-done.2.got_a
  55.4 0.0 copy-start.7
  55.4 3.4 %collective-permute-start.3 = (bf16[9,32,512]{2,1,0:T(8,128)(2,1)S(1)}, bf16[9,32,512]{2,1,0:T(8,128)(2,1)S(1)}, u32[]{:S(2)}, u32[]{:S(2)}) collective-permute-start(bf16[9,32,512]{2,1,0:T(8,128)(2,1)S(1)} %get-tuple-element.35), channel_id=1, source_target_pairs={{0,8},{8,0},{1,9},{9,1},{2,10},{10,2},{3,11},{11,3},{4,12},{12,4},... | collective-permute-start | bytes 884744 | tf_op jit(solution)/shard_map/ppermute | solution.py:196
  58.8 5.2 %collective-permute-done.3.got_b = bf16[9,32,512]{2,1,0:T(8,128)(2,1)S(1)} collective-permute-done((bf16[9,32,512]{2,1,0:T(8,128)(2,1)S(1)}, bf16[9,32,512]{2,1,0:T(8,128)(2,1)S(1)}, u32[]{:S(2)}, u32[]{:S(2)}) %collective-permute-start.3) | collective-permute-done | bytes 294944 | tf_op jit(solution)/shard_map/ppermute | solution.py:196
  64.0 0.0 copy-start.6
  64.0 1.9 %collective-permute-start.4 = (f32[32,128]{1,0:T(8,128)S(1)}, f32[32,128]{1,0:T(8,128)S(1)}, u32[]{:S(2)}, u32[]{:S(2)}) collective-permute-start(f32[32,128]{1,0:T(8,128)S(1)} %slice_add_fusion), channel_id=1, source_target_pairs={{0,16},{16,0},{1,17},{17,1},{2,18},{18,2},{3,19},{19,3},{4,20},{20... | collective-permute-start | bytes 49160 | tf_op jit(solution)/shard_map/ppermute | solution.py:196
  65.9 1.1 collective-permute-done.4
  67.1 0.6 add.11.sums
  67.7 0.0 copy-done.7
  67.7 0.0 copy-done.6
  67.7 2.2 %shard_map.129 = bf16[8,32,1280]{2,1,0:T(8,128)(2,1)} custom-call(bf16[8,32,512]{2,1,0:T(8,128)(2,1)} %copy-done.2, bf16[8,32,512]{2,1,0:T(8,128)(2,1)} %copy-done.7, bf16[8,32,512]{2,1,0:T(8,128)(2,1)} %copy-done.3, bf16[9,32,512]{2,1,0:T(8,128)(2,1)} %copy-done.6, f32[32,128]{1,0:T(8,128)} %add.11.sums), custom_call_target="tpu_custom_call" | custom-call | tf_op jit(solution)/shard_map/pallas_call | solution.py:229
  69.9 25.1 %all_to_all.16.got = bf16[8,32,1280]{2,1,0:T(8,128)(2,1)} all-to-all(bf16[8,32,1280]{2,1,0:T(8,128)(2,1)} %shard_map.129), channel_id=1, replica_groups=mesh['yh'=4,'x1'=2,'x0'=2,'core'=2,'yl'=2,'z2'=2,'z1'=2,'z0'=2] {'z2','z..., dimensions={0} | all-to-all | bytes 1310720 | tf_op jit(solution)/shard_map/all_to_all | solution.py:241
  95.0 1.9 %shard_map.130 = (bf16[32,512]{1,0:T(8,128)(2,1)}, bf16[32,512]{1,0:T(8,128)(2,1)}, f32[16,20,128]{2,1,0:T(8,128)}) custom-call(bf16[8,32,1280]{2,1,0:T(8,128)(2,1)} %all_to_all.16.got), custom_call_target="tpu_custom_call" | custom-call | tf_op jit(solution)/shard_map/pallas_call | solution.py:234
  96.8 19.3 %all_to_all.17 = f32[16,20,128]{2,1,0:T(8,128)S(1)} all-to-all(f32[16,20,128]{2,1,0:T(8,128)} %get-tuple-element.39), channel_id=1, replica_groups=mesh['yh'=4,'x1'=2,'x0'=2,'core'=2,'yl'=2,'z2'=2,'z1'=2,'z0'=2] {'yh','x..., dimensions={0} | all-to-all | bytes 327680 | tf_op jit(solution)/shard_map/all_to_all | solution.py:242
  116.1 0.6 multiply_bitcast_fusion
  (6 shorter events, 0.1 us)
Async XLA Ops:
  1.5 38.1 %copy-start.1 = (bf16[1,1,128,2560]{3,2,1,0:T(8,128)(2,1)S(1)}, bf16[1,1,128,2560]{3,2,1,0:T(8,128)(2,1)}, u32[]{:S(2)}) copy-start(bf16[1,1,128,2560]{3,2,1,0:T(8,128)(2,1)} %param.14) | copy-start | bytes 1966084
  29.2 4.3 %copy-start.8 = (f32[2560]{0:T(1024)S(1)}, f32[2560]{0:T(1024)}, u32[]{:S(2)}) copy-start(f32[2560]{0:T(1024)} %param.13) | copy-start | bytes 30724
  29.2 10.3 %copy-start = (bf16[1,1,128,2560]{3,2,1,0:T(8,128)(2,1)S(1)}, bf16[1,1,128,2560]{3,2,1,0:T(8,128)(2,1)}, u32[]{:S(2)}) copy-start(bf16[1,1,128,2560]{3,2,1,0:T(8,128)(2,1)} %param.10) | copy-start | bytes 1966084
  29.2 10.3 %copy-start.4 = (bf16[1,1,128,512]{3,2,1,0:T(8,128)(2,1)S(1)}, bf16[1,1,128,512]{3,2,1,0:T(8,128)(2,1)}, u32[]{:S(2)}) copy-start(bf16[1,1,128,512]{3,2,1,0:T(8,128)(2,1)} %param.11) | copy-start | bytes 393220
  29.2 10.3 %copy-start.5 = (bf16[1,1,128,512]{3,2,1,0:T(8,128)(2,1)S(1)}, bf16[1,1,128,512]{3,2,1,0:T(8,128)(2,1)}, u32[]{:S(2)}) copy-start(bf16[1,1,128,512]{3,2,1,0:T(8,128)(2,1)} %param.12) | copy-start | bytes 393220
  29.3 10.2 %collective-permute-start.1 = (bf16[8,32,512]{2,1,0:T(8,128)(2,1)S(1)}, bf16[8,32,512]{2,1,0:T(8,128)(2,1)S(1)}, u32[]{:S(2)}, u32[]{:S(2)}) collective-permute-start(bf16[8,32,512]{2,1,0:T(8,128)(2,1)S(1)} %get-tuple-element.40), channel_id=1, source_target_pairs={{0,8},{8,0},{1,9},{9,1},{2,10},{10,2},{3,11},{11,3},{4,12},{12,4},... | collective-permute-start | bytes 786440 | tf_op jit(solution)/shard_map/ppermute | solution.py:196
  33.6 15.6 %collective-permute-start = (bf16[8,32,512]{2,1,0:T(8,128)(2,1)S(1)}, bf16[8,32,512]{2,1,0:T(8,128)(2,1)S(1)}, u32[]{:S(2)}, u32[]{:S(2)}) collective-permute-start(bf16[8,32,512]{2,1,0:T(8,128)(2,1)S(1)} %get-tuple-element.41), channel_id=1, source_target_pairs={{0,8},{8,0},{1,9},{9,1},{2,10},{10,2},{3,11},{11,3},{4,12},{12,4},... | collective-permute-start | bytes 786440 | tf_op jit(solution)/shard_map/ppermute | solution.py:196
  44.9 9.8 %copy-start.2 = (bf16[8,32,512]{2,1,0:T(8,128)(2,1)}, bf16[8,32,512]{2,1,0:T(8,128)(2,1)S(1)}, u32[]{:S(2)}) copy-start(bf16[8,32,512]{2,1,0:T(8,128)(2,1)S(1)} %get-tuple-element.30.near_a) | copy-start | bytes 786436
  44.9 10.5 %collective-permute-start.2 = (bf16[8,32,512]{2,1,0:T(8,128)(2,1)S(1)}, bf16[8,32,512]{2,1,0:T(8,128)(2,1)S(1)}, u32[]{:S(2)}, u32[]{:S(2)}) collective-permute-start(bf16[8,32,512]{2,1,0:T(8,128)(2,1)S(1)} %get-tuple-element.32), channel_id=1, source_target_pairs={{0,8},{8,0},{1,9},{9,1},{2,10},{10,2},{3,11},{11,3},{4,12},{12,4},... | collective-permute-start | bytes 786440 | tf_op jit(solution)/shard_map/ppermute | solution.py:196
  54.6 0.7 copy-start.3
  55.4 12.3 %copy-start.7 = (bf16[8,32,512]{2,1,0:T(8,128)(2,1)}, bf16[8,32,512]{2,1,0:T(8,128)(2,1)S(1)}, u32[]{:S(2)}) copy-start(bf16[8,32,512]{2,1,0:T(8,128)(2,1)S(1)} %collective-permute-done.2.got_a) | copy-start | bytes 786436
  55.4 8.6 %collective-permute-start.3 = (bf16[9,32,512]{2,1,0:T(8,128)(2,1)S(1)}, bf16[9,32,512]{2,1,0:T(8,128)(2,1)S(1)}, u32[]{:S(2)}, u32[]{:S(2)}) collective-permute-start(bf16[9,32,512]{2,1,0:T(8,128)(2,1)S(1)} %get-tuple-element.35), channel_id=1, source_target_pairs={{0,8},{8,0},{1,9},{9,1},{2,10},{10,2},{3,11},{11,3},{4,12},{12,4},... | collective-permute-start | bytes 884744 | tf_op jit(solution)/shard_map/ppermute | solution.py:196
  64.0 3.7 %copy-start.6 = (bf16[9,32,512]{2,1,0:T(8,128)(2,1)}, bf16[9,32,512]{2,1,0:T(8,128)(2,1)S(1)}, u32[]{:S(2)}) copy-start(bf16[9,32,512]{2,1,0:T(8,128)(2,1)S(1)} %collective-permute-done.3.got_b) | copy-start | bytes 884740
  64.0 3.1 %collective-permute-start.4 = (f32[32,128]{1,0:T(8,128)S(1)}, f32[32,128]{1,0:T(8,128)S(1)}, u32[]{:S(2)}, u32[]{:S(2)}) collective-permute-start(f32[32,128]{1,0:T(8,128)S(1)} %slice_add_fusion), channel_id=1, source_target_pairs={{0,16},{16,0},{1,17},{17,1},{2,18},{18,2},{3,19},{19,3},{4,20},{20... | collective-permute-start | bytes 49160 | tf_op jit(solution)/shard_map/ppermute | solution.py:196

commit v3 on v2

v3 whole, which is shorter than its diff:
```python
import functools
import math

import jax
import jax.numpy as jnp
from jax import lax
from jax.experimental import pallas as pl
from jax.experimental.pallas import tpu as pltpu
from jax.sharding import Mesh, PartitionSpec as P

HD = 128
GROUP = 5
KVH = 4
PER = KVH // 2
SCALE = 1.0 / math.sqrt(HD)
LOG2E = 1.4426950408889634
F32 = jnp.float32
BF16 = jnp.bfloat16

PROMPT = ("yh", "x1", "x0", "core")
RESP = ("yl", "z2", "z1", "z0")
SIZES = (4, 2, 2, 2, 2, 2, 2, 2)
Z = ("z2", "z1", "z0")


def dot(a, b, a_dim, b_dim):
    return lax.dot_general(a, b, (((a_dim,), (b_dim,)), ((), ())), preferred_element_type=F32)


def prepare_kernel(
    length_ref, q_hbm, bias_ref, do_hbm, rk_hbm, rv_hbm, qs_ref, dos_ref, rk_ref, rv_ref, q_s, do_s, arrived
):
    reads = [
        pltpu.make_async_copy(source, target, arrived.at[i])
        for i, (source, target) in enumerate(
            ((q_hbm, q_s), (do_hbm, do_s), (rk_hbm, rk_ref), (rv_hbm, rv_ref))
        )
    ]
    for read in reads:
        read.start()
    rows = q_s.shape[0]
    live = lax.broadcasted_iota(jnp.int32, (rows, HD), 0) < length_ref[0, 0]
    reads[0].wait()
    for head in range(KVH * GROUP):
        cols = slice(head * HD, (head + 1) * HD)
        span = slice(head % GROUP * rows, (head % GROUP + 1) * rows)
        bias = bias_ref[cols].reshape(1, HD)
        qs_ref[head // GROUP, span, :] = (q_s[:, cols].astype(F32) + bias).astype(BF16)
    reads[1].wait()
    for head in range(KVH * GROUP):
        cols = slice(head * HD, (head + 1) * HD)
        span = slice(head % GROUP * rows, (head % GROUP + 1) * rows)
        dos_ref[head // GROUP, span, :] = jnp.where(live, do_s[:, cols].astype(F32), 0.0).astype(BF16)
    reads[2].wait()
    reads[3].wait()


def prepared(length, queries, bias, cotangent, resp_keys, resp_values):
    rows = queries.shape[0]
    hbm = pl.BlockSpec(memory_space=pltpu.HBM)
    tall = jax.ShapeDtypeStruct((KVH, GROUP * rows, HD), BF16)
    own = jax.ShapeDtypeStruct(resp_keys.shape, BF16)
    return pl.pallas_call(
        prepare_kernel,
        out_shape=(tall, tall, own, own),
        in_specs=[
            pl.BlockSpec(memory_space=pltpu.SMEM),
            hbm,
            pl.BlockSpec(memory_space=pltpu.VMEM),
            hbm,
            hbm,
            hbm,
        ],
        scratch_shapes=[
            pltpu.VMEM(queries.shape, BF16),
            pltpu.VMEM(cotangent.shape, BF16),
            pltpu.SemaphoreType.DMA((4,)),
        ],
        compiler_params=pltpu.CompilerParams(vmem_limit_bytes=16 * 1024 * 1024),
        cost_estimate=pl.CostEstimate(
            flops=queries.size, transcendentals=0, bytes_accessed=4 * 1024 * 1024
        ),
    )(length, queries, bias, cotangent, resp_keys, resp_values)


def attend_kernel(part, length_ref, qs_ref, dos_ref, rk_ref, rv_ref, near_in, far_in, *refs):
    flat_ref, drk_ref, drv_ref, near_ref, far_ref, sums_ref, columns, probs_s, dscores_s = refs[-9:]
    group = pl.program_id(0)
    length = length_ref[0, 0]
    rows = rk_ref.shape[0]
    shards, shard_rows, _ = near_in.shape
    shard_rows //= 2
    half = shards * shard_rows
    prefix = 2 * half
    keys, values = (
        jnp.concatenate(
            [
                near_in[:, at : at + shard_rows, :].reshape(half, HD),
                far_in[:, at : at + shard_rows, :].reshape(half, HD),
                own[...],
            ],
            0,
        )
        for at, own in ((0, rk_ref), (shard_rows, rv_ref))
    )
    key_at = lax.broadcasted_iota(jnp.int32, (rows, rows), 0)
    row_at = lax.broadcasted_iota(jnp.int32, (rows, rows), 1)
    visible = (key_at <= row_at) & (key_at < length)
    for head in range(GROUP):
        span = slice(head * rows, (head + 1) * rows)
        scores = dot(keys, qs_ref[0, span, :], 1, 1) * (SCALE * LOG2E)
        scores = jnp.concatenate(
            [scores[:prefix], jnp.where(visible, scores[prefix:], -jnp.inf)], 0
        )
        expd = jnp.exp2(scores - jnp.max(scores, 0, keepdims=True))
        inverse = 1.0 / jnp.sum(expd, 0, keepdims=True)
        probs = expd * inverse
        dprobs = dot(values, dos_ref[0, span, :], 1, 1)
        delta = jnp.sum(probs * dprobs, 0, keepdims=True)
        probs_s[:, span] = probs.astype(BF16)
        dscores_s[:, span] = (probs * (dprobs - delta) * SCALE).astype(BF16)
    dscores = dscores_s[...]
    for at, left, right, own in (
        (0, dscores, qs_ref, drk_ref),
        (shard_rows, probs_s[...], dos_ref, drv_ref),
    ):
        grad = dot(left, right[0], 1, 0).astype(BF16)
        own[...] = grad[prefix:]
        halves = grad[:prefix].reshape(2, shards, shard_rows, HD)
        near_ref[:, at : at + shard_rows, :] = halves[0]
        far_ref[:, at : at + shard_rows, :] = halves[1]
    dq = dot(keys, dscores, 0, 0)
    flat_ref[0] = dq.astype(BF16)
    for head in range(GROUP):
        columns[group, :, head : head + 1] = jnp.sum(
            dq[:, head * rows : (head + 1) * rows], 1, keepdims=True
        )

    @pl.when(group == PER - 1)
    def _():
        at = part * PER * GROUP
        for step in range(PER):
            sums = columns[step].T[:GROUP]
            for copy in range(sums_ref.shape[0]):
                sums_ref[copy, at + step * GROUP : at + (step + 1) * GROUP, :] = sums
        if part:
            for copy in range(sums_ref.shape[0]):
                sums_ref[copy, :at, :] = refs[5][0, :at, :]


def attend(part, length, qs, dos, resp_keys, resp_values, near, far, before, copies):
    rows = resp_keys.shape[0]
    shards, both_rows, width = near.shape
    key_count = shards * both_rows + rows
    columns = qs.shape[1]
    group_at = lambda g: part * PER + g
    column = lambda g: (0, group_at(g))
    stacked = lambda g: (group_at(g), 0, 0)
    blocked = lambda g: (0, 0, group_at(g))
    block = (shards, both_rows, HD)
    sums = lambda count: pl.BlockSpec((count, KVH * GROUP, HD), lambda g: (0, 0, 0))
    tall = (1, columns, HD)
    flat = (1, HD, columns)
    return pl.pallas_call(
        functools.partial(attend_kernel, part),
        grid=(PER,),
        out_shape=(
            jax.ShapeDtypeStruct((KVH, *flat[1:]), BF16),
            *[jax.ShapeDtypeStruct((rows, width), BF16)] * 2,
            *[jax.ShapeDtypeStruct((shards, both_rows, width), BF16)] * 2,
            jax.ShapeDtypeStruct((copies, KVH * GROUP, HD), F32),
        ),
        in_specs=[
            pl.BlockSpec(memory_space=pltpu.SMEM),
            pl.BlockSpec(tall, stacked),
            pl.BlockSpec(tall, stacked),
            pl.BlockSpec((rows, HD), column),
            pl.BlockSpec((rows, HD), column),
            pl.BlockSpec(block, blocked),
            pl.BlockSpec(block, lambda g: (0, 0, g)),
            *[pl.BlockSpec(memory_space=pl.ANY)] * 5 * part,
            *[sums(1)] * part,
        ],
        out_specs=(
            pl.BlockSpec(flat, stacked),
            *[pl.BlockSpec((rows, HD), column)] * 2,
            *[pl.BlockSpec(block, blocked)] * 2,
            sums(copies),
        ),
        scratch_shapes=[
            pltpu.VMEM((PER, HD, HD), F32),
            pltpu.VMEM((key_count, columns), BF16),
            pltpu.VMEM((key_count, columns), BF16),
        ],
        input_output_aliases={7 + i: i for i in range(5 * part)},
        compiler_params=pltpu.CompilerParams(
            dimension_semantics=("arbitrary",), vmem_limit_bytes=32 * 1024 * 1024
        ),
        cost_estimate=pl.CostEstimate(
            flops=10 * PER * columns * key_count * HD,
            transcendentals=PER * columns * key_count,
            bytes_accessed=4 * 1024 * 1024,
        ),
    )(length, qs, dos, resp_keys, resp_values, near, far, *before)


def turn_kernel(flat_ref, out_ref):
    rows = out_ref.shape[0]
    for group in range(KVH):
        for head in range(GROUP):
            at = (group * GROUP + head) * HD
            out_ref[:, at : at + HD] = flat_ref[group, :, head * rows : (head + 1) * rows].T


def pair_kernel(near, got, sums, out):
    shards, both_rows, width = near.shape
    more = out.shape[1] - both_rows
    out[:, :both_rows, :] = (near[...].astype(F32) + got[...].astype(F32)).astype(BF16)
    total = sums[0]
    for copy in range(1, sums.shape[0]):
        total = total + sums[copy]
    total = jnp.concatenate([total, jnp.zeros((2 * more - total.shape[0], HD), F32)], 0)
    high = total.astype(BF16)
    low = (total - high.astype(F32)).astype(BF16)
    terms = jnp.concatenate([high[:more], high[more:], low[:more], low[more:]], 1)
    for shard in range(shards):
        out[shard, both_rows:, :] = terms


def finish_kernel(got, dk_ref, dv_ref, sums_ref):
    rows = dk_ref.shape[0]
    total = got[0].astype(F32)
    for shard in range(1, got.shape[0]):
        total = total + got[shard].astype(F32)
    dk_ref[...] = total[:rows].astype(BF16)
    dv_ref[...] = total[rows : 2 * rows].astype(BF16)
    terms = total[2 * rows :, : 2 * HD] + total[2 * rows :, 2 * HD :]
    sums = jnp.concatenate([terms[:, :HD], terms[:, HD:]], 0)[: sums_ref.shape[1]]
    for copy in range(sums_ref.shape[0]):
        sums_ref[copy] = sums


def small_call(kernel, out_shape, *operands):
    return pl.pallas_call(
        kernel,
        out_shape=out_shape,
        compiler_params=pltpu.CompilerParams(vmem_limit_bytes=8 * 1024 * 1024),
    )(*operands)


def spread(block, axis):
    copies = jnp.broadcast_to(block[None], (lax.axis_size(axis), *block.shape))
    return lax.all_to_all(copies, axis, 0, 0)


def swap(block, axis):
    return lax.ppermute(block, axis, [(0, 1), (1, 0)])


def body(
    prefix_keys, prefix_values, resp_queries, resp_keys, resp_values, query_bias, out_grad, lengths
):
    rows, width = resp_queries.shape[2:]
    shard_rows, kv_width = prefix_keys.shape[1:]
    near = spread(jnp.concatenate([prefix_keys[0], prefix_values[0]], 0), Z)
    qs, dos, rk, rv = prepared(
        lengths, resp_queries[0, 0], query_bias, out_grad[0, 0], resp_keys[0, 0], resp_values[0, 0]
    )
    near, qs, dos, rk, rv = lax.optimization_barrier((near, qs, dos, rk, rv))
    operands = (lengths, qs, dos, rk, rv, near)
    wide = PER * HD
    far_a = swap(near[:, :, :wide], "yl")
    far_a, near_b = lax.optimization_barrier((far_a, near[:, :, wide:]))
    far_b = swap(near_b, "yl")
    first, last = ("x1", "x0", "core"), ("yh", "yl")
    held = attend(0, *operands, far_a, (), 1)
    flat, drk, drv, mine, others, sums = attend(1, *operands, far_b, held, lax.axis_size(first))
    got = swap(others, "yl")
    sums = lax.all_to_all(sums, first, 0, 0)
    pairs = small_call(
        pair_kernel,
        jax.ShapeDtypeStruct((near.shape[0], 2 * shard_rows + 16, kv_width), BF16),
        mine, got, sums,
    )
    pairs, flat = lax.optimization_barrier((pairs, flat))
    dq = small_call(turn_kernel, jax.ShapeDtypeStruct((rows, width), BF16), flat)
    prefix_dk, prefix_dv, sums = small_call(
        finish_kernel,
        (
            jax.ShapeDtypeStruct((shard_rows, kv_width), BF16),
            jax.ShapeDtypeStruct((shard_rows, kv_width), BF16),
            jax.ShapeDtypeStruct((lax.axis_size(last), KVH * GROUP, HD), F32),
        ),
        lax.all_to_all(pairs, Z, 0, 0),
    )
    sums = jnp.sum(lax.all_to_all(sums, last, 0, 0), 0).reshape(width)
    return (
        dq[None, None],
        drk[None, None],
        drv[None, None],
        prefix_dk[None],
        prefix_dv[None],
        sums / math.sqrt(math.prod(SIZES) * rows),
    )


def solution(mesh):
    fine = Mesh(mesh.devices.reshape(SIZES), PROMPT + RESP)
    return jax.shard_map(
        body,
        mesh=fine,
        in_specs=(
            P(PROMPT, RESP, None),
            P(PROMPT, RESP, None),
            P(PROMPT, RESP, None, None),
            P(PROMPT, RESP, None, None),
            P(PROMPT, RESP, None, None),
            P(),
            P(PROMPT, RESP, None, None),
            P(PROMPT, RESP),
        ),
        out_specs=(
            P(PROMPT, RESP, None, None),
            P(PROMPT, RESP, None, None),
            P(PROMPT, RESP, None, None),
            P(PROMPT, RESP, None),
            P(PROMPT, RESP, None),
            P(),
        ),
        check_vma=False,
    )
```

time: 118 us -> 107 us (0.907)
  blocking collectives: 72.1 us -> 28.9 us
  waiting for transfers between devices: 9.92 us -> 32.2 us
  starting transfers between devices: 15.6 us -> 27.8 us
  Pallas kernels: 14.8 us -> 13.3 us
    all_to_all x2 -> x1, blocking collectives: 47 us -> 8.3 us  [body(): sums = lax.all_to_all(sums, first, 0, 0)]
    all_to_all x0 -> x2, waiting for transfers between devices: none -> 22.8 us  [the longest x1 15.1 us: spread(): return lax.all_to_all(copies, axis, 0, 0)]
    all_to_all x0 -> x2, starting transfers between devices: none -> 17.4 us  [the longest x1 10.5 us: spread(): return lax.all_to_all(copies, axis, 0, 0)]
    ppermute x5 -> x3, starting transfers between devices: 15.6 us -> 10.4 us  [swap(): return lax.ppermute(block, axis, [(0, 1), (1, 0)])]
    all_to_all x1, blocking collectives: 25.1 us -> 20.6 us  [body(): lax.all_to_all(pairs, Z, 0, 0)]
    pallas_call x2 -> x4, Pallas kernels: 4.03 us -> 2.93 us  [the longest x3 1.92 us: small_call(): pl.pallas_call(kernel, out_shape=out_shape, compiler_params=pltpu.Compile...]
    ppermute x5 -> x3, waiting for transfers between devices: 9.92 us -> 9.46 us  [swap(): return lax.ppermute(block, axis, [(0, 1), (1, 0)])]
  transfers between devices with their start and end apart: 5 -> 5, of which waited for: 3 -> 5; matrix products, arithmetic and copies ran while one was open for 0% -> 0% of each run, Pallas kernels for 9% -> 7%
where the time goes in v3:
time: 107 us
  waiting for transfers between devices  32.2 us (30%)
  blocking collectives  28.9 us (27%)
  starting transfers between devices  27.8 us (26%)
  Pallas kernels  13.3 us (12%)
  local copies, waits for them, and re-layouts  1.55 us (1%)
  other arithmetic  1.4 us (1%)
  between operations  1.4 us (1%)
    all_to_all x1, blocking collectives, body(): lax.all_to_all(pairs, Z, 0, 0)  20.6 us
    all_to_all x1, waiting for transfers between devices, spread(): return lax.all_to_all(copies, axis, 0, 0)  15.1 us
    all_to_all x1, starting transfers between devices, spread(): return lax.all_to_all(copies, axis, 0, 0)  10.5 us
    ppermute x3, starting transfers between devices, swap(): return lax.ppermute(block, axis, [(0, 1), (1, 0)])  10.4 us
    pallas_call x2, Pallas kernels, attend(): pl.pallas_call(functools.partial(attend_kernel, part), grid=(PER,), out_s...  10.4 us
    ppermute x3, waiting for transfers between devices, swap(): return lax.ppermute(block, axis, [(0, 1), (1, 0)])  9.46 us
    all_to_all x1, blocking collectives, body(): sums = lax.all_to_all(sums, first, 0, 0)  8.3 us
    all_to_all x1, waiting for transfers between devices, body(): sums = jnp.sum(lax.all_to_all(sums, last, 0, 0), 0).reshape(width)  7.67 us
  transfers between devices with their start and end apart: 5, of which 5 were waited for; matrix products, arithmetic and copies ran while one was open for 0% of the time, Pallas kernels for 7%

profile of v3, /device:TPU:6, one launch (start us, length us, event | category | flops | bytes accessed | tf_op | source)
XLA Modules:
  0.0 106.6 jit_solution(5643675675463363880)
XLA Ops:
  0.6 0.8 pad_maximum_fusion
  1.4 0.0 copy-start.1
  1.4 0.8 broadcast_in_dim.21
  2.3 0.0 copy-start
  2.3 0.0 copy-start.2
  2.3 0.0 copy-start.3
  2.3 0.0 copy-start.6
  2.3 10.5 %all-to-all-start = ((bf16[8,64,512]{2,1,0:T(8,128)(2,1)}), bf16[8,64,512]{2,1,0:T(8,128)(2,1)S(1)}, u32[]{:S(2)}, u32[]{:S(2)}) async-start(bf16[8,64,512]{2,1,0:T(8,128)(2,1)} %broadcast_in_dim.21), calls=%async_computation | async-start | bytes 1048576 | tf_op jit(solution)/shard_map/all_to_all | solution.py:253
  13.4 0.0 copy-done.1
  13.4 0.0 copy-done
  13.4 0.0 copy-done.2
  13.4 0.0 copy-done.3
  13.4 0.0 copy-done.6
  13.4 1.0 shard_map.127
  14.4 0.0 copy-start.4
  14.5 0.6 copy-done.4
  15.1 15.1 %all-to-all-done.near_in = bf16[8,64,512]{2,1,0:T(8,128)(2,1)S(1)} async-done(((bf16[8,64,512]{2,1,0:T(8,128)(2,1)}), bf16[8,64,512]{2,1,0:T(8,128)(2,1)S(1)}, u32[]{:S(2)}, u32[]{:S(2)}) %all-to-all-start) | async-done | bytes 524320 | tf_op jit(solution)/shard_map/all_to_all | solution.py:253
  30.2 0.0 copy-start.5
  30.3 3.5 %collective-permute-start = (bf16[8,64,256]{2,1,0:T(8,128)(2,1)S(1)}, bf16[8,64,256]{2,1,0:T(8,128)(2,1)S(1)}, u32[]{:S(2)}, u32[]{:S(2)}) collective-permute-start(bf16[8,64,256]{2,1,0:T(8,128)(2,1)S(1)} %get-tuple-element.63), channel_id=1, source_target_pairs={{0,8},{8,0},{1,9},{9,1},{2,10},{10,2},{3,11},{11,3},{4,12},{12,4},... | collective-permute-start | bytes 786440 | tf_op jit(solution)/shard_map/ppermute | solution.py:257
  33.8 6.6 %collective-permute-done.far_in = bf16[8,64,256]{2,1,0:T(8,128)(2,1)S(1)} collective-permute-done((bf16[8,64,256]{2,1,0:T(8,128)(2,1)S(1)}, bf16[8,64,256]{2,1,0:T(8,128)(2,1)S(1)}, u32[]{:S(2)}, u32[]{:S(2)}) %collective-permute-start) | collective-permute-done | bytes 262176 | tf_op jit(solution)/shard_map/ppermute | solution.py:257
  40.4 3.5 %collective-permute-start.1 = (bf16[8,64,256]{2,1,0:T(8,128)(2,1)S(1)}, bf16[8,64,256]{2,1,0:T(8,128)(2,1)S(1)}, u32[]{:S(2)}, u32[]{:S(2)}) collective-permute-start(bf16[8,64,256]{2,1,0:T(8,128)(2,1)S(1)} %get-tuple-element.43), channel_id=1, source_target_pairs={{0,8},{8,0},{1,9},{9,1},{2,10},{10,2},{3,11},{11,3},{4,12},{12,4},... | collective-permute-start | bytes 786440 | tf_op jit(solution)/shard_map/ppermute | solution.py:257
  43.9 0.0 copy-done.5
  43.9 5.2 %shard_map.128 = (bf16[4,128,640]{2,1,0:T(8,128)(2,1)S(1)}, bf16[128,512]{1,0:T(8,128)(2,1)}, bf16[128,512]{1,0:T(8,128)(2,1)}, bf16[8,64,512]{2,1,0:T(8,128)(2,...) custom-call(s32[1,1]{1,0:T(1,128)S(6)} %copy.24.length_ref, ...), custom_call_target="tpu_custom_call" | custom-call | flops 1048576000 | bytes 4194304 | tf_op jit(solution)/shard_map/pallas_call | solution.py:164
  49.1 0.6 collective-permute-done.1.far_in
  49.7 5.2 %shard_map.129 = (bf16[4,128,640]{2,1,0:T(8,128)(2,1)S(1)}, bf16[128,512]{1,0:T(8,128)(2,1)}, bf16[128,512]{1,0:T(8,128)(2,1)}, bf16[8,64,512]{2,1,0:T(8,128)(2,...) custom-call(s32[1,1]{1,0:T(1,128)S(6)} %copy.24.length_ref, ...), custom_call_target="tpu_custom_call", output_to_operand_aliasing={{0}: (7, {}), {1}: (8, {}), {2}: (9, {}), {3}: (10, {}), {4... | custom-call | flops 1048576000 | bytes 4194304 | tf_op jit(solution)/shard_map/pallas_call | solution.py:164
  54.9 3.5 %collective-permute-start.2 = (bf16[8,64,512]{2,1,0:T(8,128)(2,1)S(1)}, bf16[8,64,512]{2,1,0:T(8,128)(2,1)S(1)}, u32[]{:S(2)}, u32[]{:S(2)}) collective-permute-start(bf16[8,64,512]{2,1,0:T(8,128)(2,1)S(1)} %get-tuple-element.52), channel_id=1, source_target_pairs={{0,8},{8,0},{1,9},{9,1},{2,10},{10,2},{3,11},{11,3},{4,12},{12,4},... | collective-permute-start | bytes 1572872 | tf_op jit(solution)/shard_map/ppermute | solution.py:257
  58.3 8.3 %all_to_all.20.sums = f32[8,20,128]{2,1,0:T(8,128)S(1)} all-to-all(f32[8,20,128]{2,1,0:T(8,128)S(1)} %get-tuple-element.53), channel_id=1, replica_groups=mesh['yh'=4,'x1'=2,'x0'=2,'core'=2,'yl'=2,'z2'=2,'z1'=2,'z0'=2] {'x1','x..., dimensions={0} | all-to-all | bytes 163840 | tf_op jit(solution)/shard_map/all_to_all | solution.py:279
  66.6 2.3 %collective-permute-done.2.got = bf16[8,64,512]{2,1,0:T(8,128)(2,1)S(1)} collective-permute-done((bf16[8,64,512]{2,1,0:T(8,128)(2,1)S(1)}, bf16[8,64,512]{2,1,0:T(8,128)(2,1)S(1)}, u32[]{:S(2)}, u32[]{:S(2)}) %collective-permute-start.2) | collective-permute-done | bytes 524320 | tf_op jit(solution)/shard_map/ppermute | solution.py:257
  68.9 0.1 shard_map.130
  69.0 20.6 %all_to_all.21.got = bf16[8,80,512]{2,1,0:T(8,128)(2,1)S(1)} all-to-all(bf16[8,80,512]{2,1,0:T(8,128)(2,1)S(1)} %shard_map.130), channel_id=1, replica_groups=mesh['yh'=4,'x1'=2,'x0'=2,'core'=2,'yl'=2,'z2'=2,'z1'=2,'z0'=2] {'z2','z..., dimensions={0} | all-to-all | bytes 1310720 | tf_op jit(solution)/shard_map/all_to_all | solution.py:294
  89.6 0.7 shard_map.132
  90.3 6.9 %all-to-all-start.3 = ((f32[8,20,128]{2,1,0:T(8,128)}), f32[8,20,128]{2,1,0:T(8,128)S(1)}, u32[]{:S(2)}, u32[]{:S(2)}) async-start(f32[8,20,128]{2,1,0:T(8,128)} %get-tuple-element.61), calls=%async_computation.3 | async-start | bytes 196608 | tf_op jit(solution)/shard_map/all_to_all | solution.py:296
  97.2 1.1 shard_map.131
  98.3 7.7 %all-to-all-done.3 = f32[8,20,128]{2,1,0:T(8,128)S(1)} async-done(((f32[8,20,128]{2,1,0:T(8,128)}), f32[8,20,128]{2,1,0:T(8,128)S(1)}, u32[]{:S(2)}, u32[]{:S(2)}) %all-to-all-start.3) | async-done | bytes 81952 | tf_op jit(solution)/shard_map/all_to_all | solution.py:296
  106.0 0.6 multiply_bitcast_fusion
  (2 shorter events, 0.1 us)
Async XLA Ops:
  1.4 12.0 %copy-start.1 = (bf16[1,1,128,2560]{3,2,1,0:T(8,128)(2,1)S(1)}, bf16[1,1,128,2560]{3,2,1,0:T(8,128)(2,1)}, u32[]{:S(2)}) copy-start(bf16[1,1,128,2560]{3,2,1,0:T(8,128)(2,1)} %param.14) | copy-start | bytes 1966084
  2.3 11.1 %copy-start = (bf16[1,1,128,2560]{3,2,1,0:T(8,128)(2,1)S(1)}, bf16[1,1,128,2560]{3,2,1,0:T(8,128)(2,1)}, u32[]{:S(2)}) copy-start(bf16[1,1,128,2560]{3,2,1,0:T(8,128)(2,1)} %param.10) | copy-start | bytes 1966084
  2.3 11.1 %copy-start.2 = (bf16[1,1,128,512]{3,2,1,0:T(8,128)(2,1)S(1)}, bf16[1,1,128,512]{3,2,1,0:T(8,128)(2,1)}, u32[]{:S(2)}) copy-start(bf16[1,1,128,512]{3,2,1,0:T(8,128)(2,1)} %param.11) | copy-start | bytes 393220
  2.3 11.2 %copy-start.3 = (bf16[1,1,128,512]{3,2,1,0:T(8,128)(2,1)S(1)}, bf16[1,1,128,512]{3,2,1,0:T(8,128)(2,1)}, u32[]{:S(2)}) copy-start(bf16[1,1,128,512]{3,2,1,0:T(8,128)(2,1)} %param.12) | copy-start | bytes 393220
  2.3 11.2 %copy-start.6 = (f32[2560]{0:T(1024)S(1)}, f32[2560]{0:T(1024)}, u32[]{:S(2)}) copy-start(f32[2560]{0:T(1024)} %bias_ref.1) | copy-start | bytes 30724
  2.3 28.0 %all-to-all-start = ((bf16[8,64,512]{2,1,0:T(8,128)(2,1)}), bf16[8,64,512]{2,1,0:T(8,128)(2,1)S(1)}, u32[]{:S(2)}, u32[]{:S(2)}) async-start(bf16[8,64,512]{2,1,0:T(8,128)(2,1)} %broadcast_in_dim.21), calls=%async_computation | async-start | bytes 1048576 | tf_op jit(solution)/shard_map/all_to_all | solution.py:253
  14.4 0.7 copy-start.4
  30.2 13.7 %copy-start.5 = (bf16[128,512]{1,0:T(8,128)(2,1)S(1)}, bf16[128,512]{1,0:T(8,128)(2,1)}, u32[]{:S(2)}) copy-start(bf16[128,512]{1,0:T(8,128)(2,1)} %copy-done.4) | copy-start | bytes 393220
  30.3 10.1 %collective-permute-start = (bf16[8,64,256]{2,1,0:T(8,128)(2,1)S(1)}, bf16[8,64,256]{2,1,0:T(8,128)(2,1)S(1)}, u32[]{:S(2)}, u32[]{:S(2)}) collective-permute-start(bf16[8,64,256]{2,1,0:T(8,128)(2,1)S(1)} %get-tuple-element.63), channel_id=1, source_target_pairs={{0,8},{8,0},{1,9},{9,1},{2,10},{10,2},{3,11},{11,3},{4,12},{12,4},... | collective-permute-start | bytes 786440 | tf_op jit(solution)/shard_map/ppermute | solution.py:257
  40.4 9.3 %collective-permute-start.1 = (bf16[8,64,256]{2,1,0:T(8,128)(2,1)S(1)}, bf16[8,64,256]{2,1,0:T(8,128)(2,1)S(1)}, u32[]{:S(2)}, u32[]{:S(2)}) collective-permute-start(bf16[8,64,256]{2,1,0:T(8,128)(2,1)S(1)} %get-tuple-element.43), channel_id=1, source_target_pairs={{0,8},{8,0},{1,9},{9,1},{2,10},{10,2},{3,11},{11,3},{4,12},{12,4},... | collective-permute-start | bytes 786440 | tf_op jit(solution)/shard_map/ppermute | solution.py:257
  54.9 14.0 %collective-permute-start.2 = (bf16[8,64,512]{2,1,0:T(8,128)(2,1)S(1)}, bf16[8,64,512]{2,1,0:T(8,128)(2,1)S(1)}, u32[]{:S(2)}, u32[]{:S(2)}) collective-permute-start(bf16[8,64,512]{2,1,0:T(8,128)(2,1)S(1)} %get-tuple-element.52), channel_id=1, source_target_pairs={{0,8},{8,0},{1,9},{9,1},{2,10},{10,2},{3,11},{11,3},{4,12},{12,4},... | collective-permute-start | bytes 1572872 | tf_op jit(solution)/shard_map/ppermute | solution.py:257
  90.3 15.6 %all-to-all-start.3 = ((f32[8,20,128]{2,1,0:T(8,128)}), f32[8,20,128]{2,1,0:T(8,128)S(1)}, u32[]{:S(2)}, u32[]{:S(2)}) async-start(f32[8,20,128]{2,1,0:T(8,128)} %get-tuple-element.61), calls=%async_computation.3 | async-start | bytes 196608 | tf_op jit(solution)/shard_map/all_to_all | solution.py:296

commit v4 on v3

--- a/solution.py
+++ b/solution.py
@@ -11,7 +11,6 @@
 HD = 128
 GROUP = 5
 KVH = 4
-PER = KVH // 2
 SCALE = 1.0 / math.sqrt(HD)
 LOG2E = 1.4426950408889634
 F32 = jnp.float32
@@ -83,13 +82,15 @@
     )(length, queries, bias, cotangent, resp_keys, resp_values)
 
 
-def attend_kernel(part, length_ref, qs_ref, dos_ref, rk_ref, rv_ref, near_in, far_in, *refs):
-    flat_ref, drk_ref, drv_ref, near_ref, far_ref, sums_ref, columns, probs_s, dscores_s = refs[-9:]
+def attend_kernel(
+    length_ref, qs_ref, dos_ref, rk_ref, rv_ref, near_in, far_in,
+    flat_ref, drk_ref, drv_ref, near_ref, far_ref, sums_ref, columns, probs_s, dscores_s,
+):
     group = pl.program_id(0)
     length = length_ref[0, 0]
     rows = rk_ref.shape[0]
-    shards, shard_rows, _ = near_in.shape
-    shard_rows //= 2
+    shards, both_rows, _ = near_in.shape
+    shard_rows = both_rows // 2
     half = shards * shard_rows
     prefix = 2 * half
     keys, values = (
@@ -108,17 +109,17 @@
     visible = (key_at <= row_at) & (key_at < length)
     for head in range(GROUP):
         span = slice(head * rows, (head + 1) * rows)
-        scores = dot(keys, qs_ref[0, span, :], 1, 1) * (SCALE * LOG2E)
+        scores = dot(keys, qs_ref[0, span, :], 1, 1)
         scores = jnp.concatenate(
             [scores[:prefix], jnp.where(visible, scores[prefix:], -jnp.inf)], 0
         )
-        expd = jnp.exp2(scores - jnp.max(scores, 0, keepdims=True))
+        top = jnp.max(scores, 0, keepdims=True) * (SCALE * LOG2E)
+        expd = jnp.exp2(scores * (SCALE * LOG2E) - top)
         inverse = 1.0 / jnp.sum(expd, 0, keepdims=True)
-        probs = expd * inverse
         dprobs = dot(values, dos_ref[0, span, :], 1, 1)
-        delta = jnp.sum(probs * dprobs, 0, keepdims=True)
-        probs_s[:, span] = probs.astype(BF16)
-        dscores_s[:, span] = (probs * (dprobs - delta) * SCALE).astype(BF16)
+        delta = jnp.sum(expd * dprobs, 0, keepdims=True) * inverse
+        probs_s[:, span] = (expd * inverse).astype(BF16)
+        dscores_s[:, span] = (expd * ((dprobs - delta) * (inverse * SCALE))).astype(BF16)
     dscores = dscores_s[...]
     for at, left, right, own in (
         (0, dscores, qs_ref, drk_ref),
@@ -136,72 +137,56 @@
             dq[:, head * rows : (head + 1) * rows], 1, keepdims=True
         )
 
-    @pl.when(group == PER - 1)
+    @pl.when(group == KVH - 1)
     def _():
-        at = part * PER * GROUP
-        for step in range(PER):
+        for step in range(KVH):
             sums = columns[step].T[:GROUP]
             for copy in range(sums_ref.shape[0]):
-                sums_ref[copy, at + step * GROUP : at + (step + 1) * GROUP, :] = sums
-        if part:
-            for copy in range(sums_ref.shape[0]):
-                sums_ref[copy, :at, :] = refs[5][0, :at, :]
-
-
-def attend(part, length, qs, dos, resp_keys, resp_values, near, far, before, copies):
-    rows = resp_keys.shape[0]
-    shards, both_rows, width = near.shape
+                sums_ref[copy, step * GROUP : (step + 1) * GROUP, :] = sums
+
+
+def attend(length, qs, dos, resp_keys, resp_values, near, far, copies):
+    rows, width = resp_keys.shape
+    shards, both_rows, _ = near.shape
     key_count = shards * both_rows + rows
     columns = qs.shape[1]
-    group_at = lambda g: part * PER + g
-    column = lambda g: (0, group_at(g))
-    stacked = lambda g: (group_at(g), 0, 0)
-    blocked = lambda g: (0, 0, group_at(g))
-    block = (shards, both_rows, HD)
-    sums = lambda count: pl.BlockSpec((count, KVH * GROUP, HD), lambda g: (0, 0, 0))
-    tall = (1, columns, HD)
-    flat = (1, HD, columns)
+    stacked = lambda g: (g, 0, 0)
+    own = pl.BlockSpec((rows, HD), lambda g: (0, g))
+    block = pl.BlockSpec((shards, both_rows, HD), lambda g: (0, 0, g))
+    tall = pl.BlockSpec((1, columns, HD), stacked)
+    sums = (copies, KVH * GROUP, HD)
     return pl.pallas_call(
-        functools.partial(attend_kernel, part),
-        grid=(PER,),
+        attend_kernel,
+        grid=(KVH,),
         out_shape=(
-            jax.ShapeDtypeStruct((KVH, *flat[1:]), BF16),
+            jax.ShapeDtypeStruct((KVH, HD, columns), BF16),
             *[jax.ShapeDtypeStruct((rows, width), BF16)] * 2,
             *[jax.ShapeDtypeStruct((shards, both_rows, width), BF16)] * 2,
-            jax.ShapeDtypeStruct((copies, KVH * GROUP, HD), F32),
-        ),
-        in_specs=[
-            pl.BlockSpec(memory_space=pltpu.SMEM),
-            pl.BlockSpec(tall, stacked),
-            pl.BlockSpec(tall, stacked),
-            pl.BlockSpec((rows, HD), column),
-            pl.BlockSpec((rows, HD), column),
-            pl.BlockSpec(block, blocked),
-            pl.BlockSpec(block, lambda g: (0, 0, g)),
-            *[pl.BlockSpec(memory_space=pl.ANY)] * 5 * part,
-            *[sums(1)] * part,
-        ],
+            jax.ShapeDtypeStruct(sums, F32),
+        ),
+        in_specs=[pl.BlockSpec(memory_space=pltpu.SMEM), tall, tall, own, own, block, block],
         out_specs=(
-            pl.BlockSpec(flat, stacked),
-            *[pl.BlockSpec((rows, HD), column)] * 2,
-            *[pl.BlockSpec(block, blocked)] * 2,
-            sums(copies),
+            pl.BlockSpec((1, HD, columns), stacked),
+            own,
+            own,
+            block,
+            block,
+            pl.BlockSpec(sums, lambda g: (0, 0, 0)),
         ),
         scratch_shapes=[
-            pltpu.VMEM((PER, HD, HD), F32),
+            pltpu.VMEM((KVH, HD, HD), F32),
             pltpu.VMEM((key_count, columns), BF16),
             pltpu.VMEM((key_count, columns), BF16),
         ],
-        input_output_aliases={7 + i: i for i in range(5 * part)},
         compiler_params=pltpu.CompilerParams(
             dimension_semantics=("arbitrary",), vmem_limit_bytes=32 * 1024 * 1024
         ),
         cost_estimate=pl.CostEstimate(
-            flops=10 * PER * columns * key_count * HD,
-            transcendentals=PER * columns * key_count,
-            bytes_accessed=4 * 1024 * 1024,
-        ),
-    )(length, qs, dos, resp_keys, resp_values, near, far, *before)
+            flops=10 * KVH * columns * key_count * HD,
+            transcendentals=KVH * columns * key_count,
+            bytes_accessed=6 * 1024 * 1024,
+        ),
+    )(length, qs, dos, resp_keys, resp_values, near, far)
 
 
 def turn_kernel(flat_ref, out_ref):
@@ -210,6 +195,14 @@
         for head in range(GROUP):
             at = (group * GROUP + head) * HD
             out_ref[:, at : at + HD] = flat_ref[group, :, head * rows : (head + 1) * rows].T
+
+
+def total_kernel(got, out):
+    total = got[0]
+    for copy in range(1, got.shape[0]):
+        total = total + got[copy]
+    for copy in range(out.shape[0]):
+        out[copy] = total
 
 
 def pair_kernel(near, got, sums, out):
@@ -227,7 +220,7 @@
         out[shard, both_rows:, :] = terms
 
 
-def finish_kernel(got, dk_ref, dv_ref, sums_ref):
+def finish_kernel(divisor, got, dk_ref, dv_ref, sums_ref):
     rows = dk_ref.shape[0]
     total = got[0].astype(F32)
     for shard in range(1, got.shape[0]):
@@ -235,9 +228,8 @@
     dk_ref[...] = total[:rows].astype(BF16)
     dv_ref[...] = total[rows : 2 * rows].astype(BF16)
     terms = total[2 * rows :, : 2 * HD] + total[2 * rows :, 2 * HD :]
-    sums = jnp.concatenate([terms[:, :HD], terms[:, HD:]], 0)[: sums_ref.shape[1]]
-    for copy in range(sums_ref.shape[0]):
-        sums_ref[copy] = sums
+    sums = jnp.concatenate([terms[:, :HD], terms[:, HD:]], 0)[: sums_ref.shape[0]]
+    sums_ref[...] = sums / divisor
 
 
 def small_call(kernel, out_shape, *operands):
@@ -266,41 +258,40 @@
     qs, dos, rk, rv = prepared(
         lengths, resp_queries[0, 0], query_bias, out_grad[0, 0], resp_keys[0, 0], resp_values[0, 0]
     )
-    near, qs, dos, rk, rv = lax.optimization_barrier((near, qs, dos, rk, rv))
-    operands = (lengths, qs, dos, rk, rv, near)
-    wide = PER * HD
-    far_a = swap(near[:, :, :wide], "yl")
-    far_a, near_b = lax.optimization_barrier((far_a, near[:, :, wide:]))
-    far_b = swap(near_b, "yl")
-    first, last = ("x1", "x0", "core"), ("yh", "yl")
-    held = attend(0, *operands, far_a, (), 1)
-    flat, drk, drv, mine, others, sums = attend(1, *operands, far_b, held, lax.axis_size(first))
+    first, second = ("x1", "x0", "core"), ("yh", "yl")
+    flat, drk, drv, mine, others, sums = attend(
+        lengths, qs, dos, rk, rv, near, swap(near, "yl"), lax.axis_size(first)
+    )
     got = swap(others, "yl")
-    sums = lax.all_to_all(sums, first, 0, 0)
+    sums = small_call(
+        total_kernel,
+        jax.ShapeDtypeStruct((lax.axis_size(second), *sums.shape[1:]), F32),
+        lax.all_to_all(sums, first, 0, 0),
+    )
     pairs = small_call(
         pair_kernel,
         jax.ShapeDtypeStruct((near.shape[0], 2 * shard_rows + 16, kv_width), BF16),
-        mine, got, sums,
+        mine, got, lax.all_to_all(sums, second, 0, 0),
     )
     pairs, flat = lax.optimization_barrier((pairs, flat))
     dq = small_call(turn_kernel, jax.ShapeDtypeStruct((rows, width), BF16), flat)
+    summed, dq = lax.optimization_barrier((lax.all_to_all(pairs, Z, 0, 0), dq))
     prefix_dk, prefix_dv, sums = small_call(
-        finish_kernel,
+        functools.partial(finish_kernel, math.sqrt(math.prod(SIZES) * rows)),
         (
             jax.ShapeDtypeStruct((shard_rows, kv_width), BF16),
             jax.ShapeDtypeStruct((shard_rows, kv_width), BF16),
-            jax.ShapeDtypeStruct((lax.axis_size(last), KVH * GROUP, HD), F32),
-        ),
-        lax.all_to_all(pairs, Z, 0, 0),
-    )
-    sums = jnp.sum(lax.all_to_all(sums, last, 0, 0), 0).reshape(width)
+            jax.ShapeDtypeStruct((KVH * GROUP, HD), F32),
+        ),
+        summed,
+    )
     return (
         dq[None, None],
         drk[None, None],
         drv[None, None],
         prefix_dk[None],
         prefix_dv[None],
-        sums / math.sqrt(math.prod(SIZES) * rows),
+        sums.reshape(width),
     )
 
 

time: 107 us -> 105 us (0.981); the launches traced: 107 us -> 103 us
  blocking collectives: 28.9 us -> 50.8 us
  starting transfers between devices: 27.8 us -> 10.5 us
  waiting for transfers between devices: 32.2 us -> 26.5 us
  local copies, waits for them, and re-layouts: 1.55 us -> 0.06 us
    all_to_all x2 -> x3, blocking collectives: 28.9 us -> 50.8 us  [the longest x1 27.7 us: spread(): return lax.all_to_all(copies, axis, 0, 0)]
    all_to_all x2 -> x1, starting transfers between devices: 17.4 us -> 3.54 us  [body(): summed, dq = lax.optimization_barrier((lax.all_to_all(pairs, Z, 0, 0), dq))]
    all_to_all x2 -> x1, waiting for transfers between devices: 22.8 us -> 18 us  [body(): summed, dq = lax.optimization_barrier((lax.all_to_all(pairs, Z, 0, 0), dq))]
    ppermute x3 -> x2, starting transfers between devices: 10.4 us -> 6.94 us  [swap(): return lax.ppermute(block, axis, [(0, 1), (1, 0)])]
    ppermute x3 -> x2, waiting for transfers between devices: 9.46 us -> 8.57 us  [swap(): return lax.ppermute(block, axis, [(0, 1), (1, 0)])]
    pallas_call x3 -> x4, Pallas kernels: 1.92 us -> 2.74 us  [small_call(): pl.pallas_call(kernel, out_shape=out_shape, compiler_params=pltpu.Compile...]
    pallas_call x2 -> x1, Pallas kernels: 10.4 us -> 9.66 us  [attend(): pl.pallas_call(attend_kernel, grid=(KVH,), out_shape=(jax.ShapeDtypeStruc...]
  transfers between devices with their start and end apart: 5 -> 3, of which waited for: 5 -> 2; matrix products, arithmetic and copies ran while one was open for 0% -> 0% of each run, Pallas kernels for 7% -> 2%
where the time goes in v4:
time: 105 us; the launch traced here: 103 us
  blocking collectives  50.8 us (48%)
  waiting for transfers between devices  26.5 us (25%)
  Pallas kernels  13.4 us (13%)
  starting transfers between devices  10.5 us (10%)
  between operations  1.4 us (1%)
    all_to_all x1, blocking collectives, spread(): return lax.all_to_all(copies, axis, 0, 0)  27.7 us
    all_to_all x1, waiting for transfers between devices, body(): summed, dq = lax.optimization_barrier((lax.all_to_all(pairs, Z, 0, 0), dq))  18 us
    all_to_all x1, blocking collectives, body(): lax.all_to_all(sums, second, 0, 0)  14.7 us
    pallas_call x1, Pallas kernels, attend(): pl.pallas_call(attend_kernel, grid=(KVH,), out_shape=(jax.ShapeDtypeStruc...  9.66 us
    ppermute x2, waiting for transfers between devices, swap(): return lax.ppermute(block, axis, [(0, 1), (1, 0)])  8.57 us
    all_to_all x1, blocking collectives, body(): lax.all_to_all(sums, first, 0, 0)  8.3 us
    ppermute x2, starting transfers between devices, swap(): return lax.ppermute(block, axis, [(0, 1), (1, 0)])  6.94 us
    all_to_all x1, starting transfers between devices, body(): summed, dq = lax.optimization_barrier((lax.all_to_all(pairs, Z, 0, 0), dq))  3.54 us
  transfers between devices with their start and end apart: 3, of which 2 were waited for; matrix products, arithmetic and copies ran while one was open for 0% of the time, Pallas kernels for 2%

profile of v4, /device:TPU:6, one launch (start us, length us, event | category | flops | bytes accessed | tf_op | source)
XLA Modules:
  0.0 103.5 jit_solution(15625420262212674033)
XLA Ops:
  0.6 0.8 pad_maximum_fusion
  1.4 0.0 copy-start.1
  1.5 0.0 copy-start
  1.5 0.0 copy-start.2
  1.5 0.0 copy-start.3
  1.5 0.0 copy-start.4
  1.5 27.7 %all_to_all.20.near_in = bf16[8,64,512]{2,1,0:T(8,128)(2,1)S(1)} all-to-all(bf16[8,64,512]{2,1,0:T(8,128)(2,1)S(1)} %broadcast_in_dim.21), channel_id=1, replica_groups=mesh['yh'=4,'x1'=2,'x0'=2,'core'=2,'yl'=2,'z2'=2,'z1'=2,'z0'=2] {'z2','z..., dimensions={0} | all-to-all | bytes 1048576 | tf_op jit(solution)/shard_map/all_to_all | solution.py:245
  29.2 3.5 %collective-permute-start = (bf16[8,64,512]{2,1,0:T(8,128)(2,1)S(1)}, bf16[8,64,512]{2,1,0:T(8,128)(2,1)S(1)}, u32[]{:S(2)}, u32[]{:S(2)}) collective-permute-start(bf16[8,64,512]{2,1,0:T(8,128)(2,1)S(1)} %all_to_all.20.near_in), channel_id=1, source_target_pairs={{0,8},{8,0},{1,9},{9,1},{2,10},{10,2},{3,11},{11,3},{4,12},{12,4},... | collective-permute-start | bytes 1572872 | tf_op jit(solution)/shard_map/ppermute | solution.py:249
  33.4 0.0 copy-done.1
  33.4 0.0 copy-done
  33.4 0.0 copy-done.2
  33.4 0.0 copy-done.3
  33.4 0.0 copy-done.4
  33.4 1.0 shard_map.127
  34.4 8.6 %collective-permute-done.far_in = bf16[8,64,512]{2,1,0:T(8,128)(2,1)S(1)} collective-permute-done((bf16[8,64,512]{2,1,0:T(8,128)(2,1)S(1)}, bf16[8,64,512]{2,1,0:T(8,128)(2,1)S(1)}, u32[]{:S(2)}, u32[]{:S(2)}) %collective-permute-start) | collective-permute-done | bytes 524320 | tf_op jit(solution)/shard_map/ppermute | solution.py:249
  43.0 9.7 %shard_map.128 = (bf16[4,128,640]{2,1,0:T(8,128)(2,1)S(1)}, bf16[128,512]{1,0:T(8,128)(2,1)}, bf16[128,512]{1,0:T(8,128)(2,1)}, bf16[8,64,512]{2,1,0:T(8,128)(2,...) custom-call(s32[1,1]{1,0:T(1,128)S(6)} %copy.14.length_ref, ...), custom_call_target="tpu_custom_call" | custom-call | flops 2097152000 | bytes 6291456 | tf_op jit(solution)/shard_map/pallas_call | solution.py:158
  52.7 3.5 %collective-permute-start.1 = (bf16[8,64,512]{2,1,0:T(8,128)(2,1)S(1)}, bf16[8,64,512]{2,1,0:T(8,128)(2,1)S(1)}, u32[]{:S(2)}, u32[]{:S(2)}) collective-permute-start(bf16[8,64,512]{2,1,0:T(8,128)(2,1)S(1)} %get-tuple-element.28), channel_id=1, source_target_pairs={{0,8},{8,0},{1,9},{9,1},{2,10},{10,2},{3,11},{11,3},{4,12},{12,4},... | collective-permute-start | bytes 1572872 | tf_op jit(solution)/shard_map/ppermute | solution.py:249
  56.2 8.3 %all_to_all.21.got = f32[8,20,128]{2,1,0:T(8,128)S(1)} all-to-all(f32[8,20,128]{2,1,0:T(8,128)S(1)} %get-tuple-element.29), channel_id=1, replica_groups=mesh['yh'=4,'x1'=2,'x0'=2,'core'=2,'yl'=2,'z2'=2,'z1'=2,'z0'=2] {'x1','x..., dimensions={0} | all-to-all | bytes 163840 | tf_op jit(solution)/shard_map/all_to_all | solution.py:269
  64.5 14.7 %all_to_all.22.sums = f32[8,20,128]{2,1,0:T(8,128)S(1)} all-to-all(f32[8,20,128]{2,1,0:T(8,128)S(1)} %shard_map.129), channel_id=1, replica_groups=mesh['yh'=4,'x1'=2,'x0'=2,'core'=2,'yl'=2,'z2'=2,'z1'=2,'z0'=2] {'yh','yl'}, dimensions={0} | all-to-all | bytes 163840 | tf_op jit(solution)/shard_map/all_to_all | solution.py:274
  79.2 0.0 collective-permute-done.1.got
  79.2 1.0 shard_map.130
  80.2 3.5 %all-to-all-start.3 = ((bf16[8,80,512]{2,1,0:T(8,128)(2,1)}), bf16[8,80,512]{2,1,0:T(8,128)(2,1)S(1)}, u32[]{:S(2)}, u32[]{:S(2)}) async-start(bf16[8,80,512]{2,1,0:T(8,128)(2,1)} %shard_map.130), calls=%async_computation.3 | async-start | bytes 1310720 | tf_op jit(solution)/shard_map/all_to_all | solution.py:278
  83.7 1.1 %shard_map.131 = bf16[128,2560]{1,0:T(8,128)(2,1)} custom-call(bf16[4,128,640]{2,1,0:T(8,128)(2,1)S(1)} %get-tuple-element.32.flat_ref), custom_call_target="tpu_custom_call" | custom-call | tf_op jit(solution)/shard_map/pallas_call | solution.py:236
  84.8 18.0 %all-to-all-done.3.got = bf16[8,80,512]{2,1,0:T(8,128)(2,1)S(1)} async-done(((bf16[8,80,512]{2,1,0:T(8,128)(2,1)}), bf16[8,80,512]{2,1,0:T(8,128)(2,1)S(1)}, u32[]{:S(2)}, u32[]{:S(2)}) %all-to-all-start.3) | async-done | bytes 655392 | tf_op jit(solution)/shard_map/all_to_all | solution.py:278
  102.8 0.7 shard_map.132
  (2 shorter events, 0.1 us)
Async XLA Ops:
  1.4 32.0 %copy-start.1 = (bf16[1,1,128,2560]{3,2,1,0:T(8,128)(2,1)S(1)}, bf16[1,1,128,2560]{3,2,1,0:T(8,128)(2,1)}, u32[]{:S(2)}) copy-start(bf16[1,1,128,2560]{3,2,1,0:T(8,128)(2,1)} %param.14) | copy-start | bytes 1966084
  1.5 31.9 %copy-start = (bf16[1,1,128,2560]{3,2,1,0:T(8,128)(2,1)S(1)}, bf16[1,1,128,2560]{3,2,1,0:T(8,128)(2,1)}, u32[]{:S(2)}) copy-start(bf16[1,1,128,2560]{3,2,1,0:T(8,128)(2,1)} %param.10) | copy-start | bytes 1966084
  1.5 31.9 %copy-start.2 = (bf16[1,1,128,512]{3,2,1,0:T(8,128)(2,1)S(1)}, bf16[1,1,128,512]{3,2,1,0:T(8,128)(2,1)}, u32[]{:S(2)}) copy-start(bf16[1,1,128,512]{3,2,1,0:T(8,128)(2,1)} %param.11) | copy-start | bytes 393220
  1.5 31.9 %copy-start.3 = (bf16[1,1,128,512]{3,2,1,0:T(8,128)(2,1)S(1)}, bf16[1,1,128,512]{3,2,1,0:T(8,128)(2,1)}, u32[]{:S(2)}) copy-start(bf16[1,1,128,512]{3,2,1,0:T(8,128)(2,1)} %param.12) | copy-start | bytes 393220
  1.5 31.9 %copy-start.4 = (f32[2560]{0:T(1024)S(1)}, f32[2560]{0:T(1024)}, u32[]{:S(2)}) copy-start(f32[2560]{0:T(1024)} %bias_ref.1) | copy-start | bytes 30724
  29.2 13.8 %collective-permute-start = (bf16[8,64,512]{2,1,0:T(8,128)(2,1)S(1)}, bf16[8,64,512]{2,1,0:T(8,128)(2,1)S(1)}, u32[]{:S(2)}, u32[]{:S(2)}) collective-permute-start(bf16[8,64,512]{2,1,0:T(8,128)(2,1)S(1)} %all_to_all.20.near_in), channel_id=1, source_target_pairs={{0,8},{8,0},{1,9},{9,1},{2,10},{10,2},{3,11},{11,3},{4,12},{12,4},... | collective-permute-start | bytes 1572872 | tf_op jit(solution)/shard_map/ppermute | solution.py:249
  52.7 26.5 %collective-permute-start.1 = (bf16[8,64,512]{2,1,0:T(8,128)(2,1)S(1)}, bf16[8,64,512]{2,1,0:T(8,128)(2,1)S(1)}, u32[]{:S(2)}, u32[]{:S(2)}) collective-permute-start(bf16[8,64,512]{2,1,0:T(8,128)(2,1)S(1)} %get-tuple-element.28), channel_id=1, source_target_pairs={{0,8},{8,0},{1,9},{9,1},{2,10},{10,2},{3,11},{11,3},{4,12},{12,4},... | collective-permute-start | bytes 1572872 | tf_op jit(solution)/shard_map/ppermute | solution.py:249
  80.2 22.6 %all-to-all-start.3 = ((bf16[8,80,512]{2,1,0:T(8,128)(2,1)}), bf16[8,80,512]{2,1,0:T(8,128)(2,1)S(1)}, u32[]{:S(2)}, u32[]{:S(2)}) async-start(bf16[8,80,512]{2,1,0:T(8,128)(2,1)} %shard_map.130), calls=%async_computation.3 | async-start | bytes 1310720 | tf_op jit(solution)/shard_map/all_to_all | solution.py:278

commit v5 on v4

--- a/solution.py
+++ b/solution.py
@@ -82,111 +82,148 @@
     )(length, queries, bias, cotangent, resp_keys, resp_values)
 
 
-def attend_kernel(
-    length_ref, qs_ref, dos_ref, rk_ref, rv_ref, near_in, far_in,
-    flat_ref, drk_ref, drv_ref, near_ref, far_ref, sums_ref, columns, probs_s, dscores_s,
+def near_kernel(
+    length_ref, qs_ref, dos_ref, rk_ref, rv_ref, near_in, expd_ref, dprobs_ref, stats_ref
 ):
-    group = pl.program_id(0)
     length = length_ref[0, 0]
     rows = rk_ref.shape[0]
     shards, both_rows, _ = near_in.shape
     shard_rows = both_rows // 2
     half = shards * shard_rows
-    prefix = 2 * half
-    keys, values = (
-        jnp.concatenate(
-            [
-                near_in[:, at : at + shard_rows, :].reshape(half, HD),
-                far_in[:, at : at + shard_rows, :].reshape(half, HD),
-                own[...],
-            ],
-            0,
-        )
-        for at, own in ((0, rk_ref), (shard_rows, rv_ref))
-    )
     key_at = lax.broadcasted_iota(jnp.int32, (rows, rows), 0)
     row_at = lax.broadcasted_iota(jnp.int32, (rows, rows), 1)
     visible = (key_at <= row_at) & (key_at < length)
-    for head in range(GROUP):
-        span = slice(head * rows, (head + 1) * rows)
-        scores = dot(keys, qs_ref[0, span, :], 1, 1)
-        scores = jnp.concatenate(
-            [scores[:prefix], jnp.where(visible, scores[prefix:], -jnp.inf)], 0
+    for group in range(KVH):
+        cols = slice(group * HD, (group + 1) * HD)
+        keys, values = (
+            jnp.concatenate(
+                [near_in[:, at : at + shard_rows, cols].reshape(half, HD), own[:, cols]], 0
+            )
+            for at, own in ((0, rk_ref), (shard_rows, rv_ref))
         )
-        top = jnp.max(scores, 0, keepdims=True) * (SCALE * LOG2E)
-        expd = jnp.exp2(scores * (SCALE * LOG2E) - top)
-        inverse = 1.0 / jnp.sum(expd, 0, keepdims=True)
-        dprobs = dot(values, dos_ref[0, span, :], 1, 1)
-        delta = jnp.sum(expd * dprobs, 0, keepdims=True) * inverse
-        probs_s[:, span] = (expd * inverse).astype(BF16)
-        dscores_s[:, span] = (expd * ((dprobs - delta) * (inverse * SCALE))).astype(BF16)
-    dscores = dscores_s[...]
-    for at, left, right, own in (
-        (0, dscores, qs_ref, drk_ref),
-        (shard_rows, probs_s[...], dos_ref, drv_ref),
-    ):
-        grad = dot(left, right[0], 1, 0).astype(BF16)
-        own[...] = grad[prefix:]
-        halves = grad[:prefix].reshape(2, shards, shard_rows, HD)
-        near_ref[:, at : at + shard_rows, :] = halves[0]
-        far_ref[:, at : at + shard_rows, :] = halves[1]
-    dq = dot(keys, dscores, 0, 0)
-    flat_ref[0] = dq.astype(BF16)
-    for head in range(GROUP):
-        columns[group, :, head : head + 1] = jnp.sum(
-            dq[:, head * rows : (head + 1) * rows], 1, keepdims=True
-        )
-
-    @pl.when(group == KVH - 1)
-    def _():
-        for step in range(KVH):
-            sums = columns[step].T[:GROUP]
-            for copy in range(sums_ref.shape[0]):
-                sums_ref[copy, step * GROUP : (step + 1) * GROUP, :] = sums
-
-
-def attend(length, qs, dos, resp_keys, resp_values, near, far, copies):
+        for head in range(GROUP):
+            span = slice(head * rows, (head + 1) * rows)
+            scores = dot(keys, qs_ref[group, span, :], 1, 1)
+            scores = jnp.concatenate(
+                [scores[:half], jnp.where(visible, scores[half:], -jnp.inf)], 0
+            )
+            top = jnp.max(scores, 0, keepdims=True) * (SCALE * LOG2E)
+            expd = jnp.exp2(scores * (SCALE * LOG2E) - top)
+            dprobs = dot(values, dos_ref[group, span, :], 1, 1)
+            expd_ref[group, :, span] = expd
+            dprobs_ref[group, :, span] = dprobs
+            stats_ref[group, 0:1, span] = top
+            stats_ref[group, 1:2, span] = jnp.sum(expd, 0, keepdims=True)
+            stats_ref[group, 2:3, span] = jnp.sum(expd * dprobs, 0, keepdims=True)
+
+
+def near_scores(length, qs, dos, resp_keys, resp_values, near):
+    shards, both_rows, _ = near.shape
+    columns = qs.shape[1]
+    square = (KVH, shards * both_rows // 2 + resp_keys.shape[0], columns)
+    vmem = pl.BlockSpec(memory_space=pltpu.VMEM)
+    return pl.pallas_call(
+        near_kernel,
+        out_shape=(
+            jax.ShapeDtypeStruct(square, F32),
+            jax.ShapeDtypeStruct(square, F32),
+            jax.ShapeDtypeStruct((KVH, 8, columns), F32),
+        ),
+        in_specs=[pl.BlockSpec(memory_space=pltpu.SMEM), *[vmem] * 5],
+        out_specs=(vmem,) * 3,
+        compiler_params=pltpu.CompilerParams(vmem_limit_bytes=16 * 1024 * 1024),
+        cost_estimate=pl.CostEstimate(
+            flops=4 * KVH * columns * square[1] * HD,
+            transcendentals=KVH * columns * square[1],
+            bytes_accessed=2 * 1024 * 1024,
+        ),
+    )(length, qs, dos, resp_keys, resp_values, near)
+
+
+def attend_kernel(
+    qs_ref, dos_ref, rk_ref, near_in, far_in, expd_in, dprobs_in, stats_in,
+    flat_ref, drk_ref, drv_ref, near_ref, far_ref, sums_ref, probs_s, dscores_s,
+):
+    rows = rk_ref.shape[0]
+    shards, both_rows, _ = near_in.shape
+    shard_rows = both_rows // 2
+    half = shards * shard_rows
+    first = half + rows
+    for group in range(KVH):
+        cols = slice(group * HD, (group + 1) * HD)
+        far_keys = far_in[:, :shard_rows, cols].reshape(half, HD)
+        far_values = far_in[:, shard_rows:, cols].reshape(half, HD)
+        for head in range(GROUP):
+            span = slice(head * rows, (head + 1) * rows)
+            scores = dot(far_keys, qs_ref[group, span, :], 1, 1)
+            near_top = stats_in[group, 0:1, span]
+            top = jnp.max(scores, 0, keepdims=True) * (SCALE * LOG2E)
+            top = jnp.maximum(top, near_top)
+            shrink = jnp.exp2(near_top - top)
+            expd = jnp.exp2(scores * (SCALE * LOG2E) - top)
+            total = stats_in[group, 1:2, span] * shrink + jnp.sum(expd, 0, keepdims=True)
+            inverse = 1.0 / total
+            dprobs = dot(far_values, dos_ref[group, span, :], 1, 1)
+            delta = stats_in[group, 2:3, span] * shrink + jnp.sum(expd * dprobs, 0, keepdims=True)
+            delta = delta * inverse
+            probs_s[group, first:, span] = (expd * inverse).astype(BF16)
+            dscores_s[group, first:, span] = (
+                expd * ((dprobs - delta) * (inverse * SCALE))
+            ).astype(BF16)
+            factor = shrink * inverse
+            expd = expd_in[group, :, span]
+            dprobs = dprobs_in[group, :, span]
+            probs_s[group, :first, span] = (expd * factor).astype(BF16)
+            dscores_s[group, :first, span] = (
+                expd * ((dprobs - delta) * (factor * SCALE))
+            ).astype(BF16)
+        dscores = dscores_s[group]
+        for at, left, right, own in (
+            (0, dscores, qs_ref, drk_ref),
+            (shard_rows, probs_s[group], dos_ref, drv_ref),
+        ):
+            grad = dot(left, right[group], 1, 0).astype(BF16)
+            own[:, cols] = grad[half:first]
+            for ref, part in ((near_ref, grad[:half]), (far_ref, grad[first:])):
+                ref[:, at : at + shard_rows, cols] = part.reshape(shards, shard_rows, HD)
+        near_keys = near_in[:, :shard_rows, cols].reshape(half, HD)
+        keys = jnp.concatenate([near_keys, rk_ref[:, cols], far_keys], 0)
+        dq = dot(keys, dscores, 0, 0)
+        flat_ref[group] = dq.astype(BF16)
+        columns = [
+            jnp.sum(dq[:, head * rows : (head + 1) * rows], 1, keepdims=True)
+            for head in range(GROUP)
+        ]
+        columns.append(jnp.zeros((HD, HD - GROUP), F32))
+        sums = jnp.concatenate(columns, 1).T[:GROUP]
+        for copy in range(sums_ref.shape[0]):
+            sums_ref[copy, group * GROUP : (group + 1) * GROUP, :] = sums
+
+
+def attend(qs, dos, resp_keys, near, far, expd, dprobs, stats, copies):
     rows, width = resp_keys.shape
     shards, both_rows, _ = near.shape
     key_count = shards * both_rows + rows
     columns = qs.shape[1]
-    stacked = lambda g: (g, 0, 0)
-    own = pl.BlockSpec((rows, HD), lambda g: (0, g))
-    block = pl.BlockSpec((shards, both_rows, HD), lambda g: (0, 0, g))
-    tall = pl.BlockSpec((1, columns, HD), stacked)
-    sums = (copies, KVH * GROUP, HD)
+    vmem = pl.BlockSpec(memory_space=pltpu.VMEM)
     return pl.pallas_call(
         attend_kernel,
-        grid=(KVH,),
         out_shape=(
             jax.ShapeDtypeStruct((KVH, HD, columns), BF16),
             *[jax.ShapeDtypeStruct((rows, width), BF16)] * 2,
             *[jax.ShapeDtypeStruct((shards, both_rows, width), BF16)] * 2,
-            jax.ShapeDtypeStruct(sums, F32),
-        ),
-        in_specs=[pl.BlockSpec(memory_space=pltpu.SMEM), tall, tall, own, own, block, block],
-        out_specs=(
-            pl.BlockSpec((1, HD, columns), stacked),
-            own,
-            own,
-            block,
-            block,
-            pl.BlockSpec(sums, lambda g: (0, 0, 0)),
-        ),
-        scratch_shapes=[
-            pltpu.VMEM((KVH, HD, HD), F32),
-            pltpu.VMEM((key_count, columns), BF16),
-            pltpu.VMEM((key_count, columns), BF16),
-        ],
-        compiler_params=pltpu.CompilerParams(
-            dimension_semantics=("arbitrary",), vmem_limit_bytes=32 * 1024 * 1024
-        ),
+            jax.ShapeDtypeStruct((copies, KVH * GROUP, HD), F32),
+        ),
+        in_specs=[vmem] * 8,
+        out_specs=(vmem,) * 6,
+        scratch_shapes=[pltpu.VMEM((KVH, key_count, columns), BF16)] * 2,
+        compiler_params=pltpu.CompilerParams(vmem_limit_bytes=32 * 1024 * 1024),
         cost_estimate=pl.CostEstimate(
-            flops=10 * KVH * columns * key_count * HD,
-            transcendentals=KVH * columns * key_count,
+            flops=8 * KVH * columns * key_count * HD,
+            transcendentals=KVH * columns * key_count // 2,
             bytes_accessed=6 * 1024 * 1024,
         ),
-    )(length, qs, dos, resp_keys, resp_values, near, far)
+    )(qs, dos, resp_keys, near, far, expd, dprobs, stats)
 
 
 def turn_kernel(flat_ref, out_ref):
@@ -259,8 +296,10 @@
         lengths, resp_queries[0, 0], query_bias, out_grad[0, 0], resp_keys[0, 0], resp_values[0, 0]
     )
     first, second = ("x1", "x0", "core"), ("yh", "yl")
+    far = swap(near, "yl")
+    held = near_scores(lengths, qs, dos, rk, rv, near)
     flat, drk, drv, mine, others, sums = attend(
-        lengths, qs, dos, rk, rv, near, swap(near, "yl"), lax.axis_size(first)
+        qs, dos, rk, near, far, *held, lax.axis_size(first)
     )
     got = swap(others, "yl")
     sums = small_call(
@@ -268,14 +307,15 @@
         jax.ShapeDtypeStruct((lax.axis_size(second), *sums.shape[1:]), F32),
         lax.all_to_all(sums, first, 0, 0),
     )
+    sums, flat = lax.optimization_barrier((sums, flat))
+    dq = small_call(turn_kernel, jax.ShapeDtypeStruct((rows, width), BF16), flat)
+    sums, dq = lax.optimization_barrier((lax.all_to_all(sums, second, 0, 0), dq))
     pairs = small_call(
         pair_kernel,
         jax.ShapeDtypeStruct((near.shape[0], 2 * shard_rows + 16, kv_width), BF16),
-        mine, got, lax.all_to_all(sums, second, 0, 0),
-    )
-    pairs, flat = lax.optimization_barrier((pairs, flat))
-    dq = small_call(turn_kernel, jax.ShapeDtypeStruct((rows, width), BF16), flat)
-    summed, dq = lax.optimization_barrier((lax.all_to_all(pairs, Z, 0, 0), dq))
+        mine, got, sums,
+    )
+    summed = lax.all_to_all(pairs, Z, 0, 0)
     prefix_dk, prefix_dv, sums = small_call(
         functools.partial(finish_kernel, math.sqrt(math.prod(SIZES) * rows)),
         (

time: 105 us -> 99.4 us (0.947)
  waiting for transfers between devices: 26.5 us -> 10 us
  blocking collectives: 50.8 us -> 57.5 us
  local copies, waits for them, and re-layouts: 0.06 us -> 4.72 us
  Pallas kernels: 13.4 us -> 10.7 us
  starting transfers between devices: 10.5 us -> 13.2 us
    all_to_all x1, waiting for transfers between devices: 18 us -> 7.67 us  [body(): lax.all_to_all(sums, second, 0, 0)]
    all_to_all x1, blocking collectives: 14.7 us -> 21.6 us  [body(): summed = lax.all_to_all(pairs, Z, 0, 0)]
    ppermute x2, waiting for transfers between devices: 8.57 us -> 2.33 us  [swap(): return lax.ppermute(block, axis, [(0, 1), (1, 0)])]
    unnamed x10, local copies, waits for them, and re-layouts: 0.03 us -> 4.68 us
    all_to_all x1, starting transfers between devices: 3.54 us -> 6.2 us  [body(): lax.all_to_all(sums, second, 0, 0)]
    pallas_call x1 -> x2, Pallas kernels: 9.66 us -> 7.16 us  [the longest x1 5.56 us: attend(): pl.pallas_call(attend_kernel, out_shape=(jax.ShapeDtypeStruct((KVH, HD, c...]
  transfers between devices with their start and end apart: 3 -> 3, of which waited for: 2 -> 2; matrix products, arithmetic and copies ran while one was open for 0% -> 0% of each run, Pallas kernels for 2% -> 4%
where the time goes in v5:
time: 99.4 us; the launch traced here: 98.2 us
  blocking collectives  57.5 us (58%)
  starting transfers between devices  13.2 us (13%)
  Pallas kernels  10.7 us (11%)
  waiting for transfers between devices  10 us (10%)
  local copies, waits for them, and re-layouts  4.72 us (5%)
  between operations  1.33 us (1%)
    all_to_all x1, blocking collectives, spread(): return lax.all_to_all(copies, axis, 0, 0)  27.6 us
    all_to_all x1, blocking collectives, body(): summed = lax.all_to_all(pairs, Z, 0, 0)  21.6 us
    all_to_all x1, blocking collectives, body(): lax.all_to_all(sums, first, 0, 0)  8.31 us
    all_to_all x1, waiting for transfers between devices, body(): lax.all_to_all(sums, second, 0, 0)  7.67 us
    ppermute x2, starting transfers between devices, swap(): return lax.ppermute(block, axis, [(0, 1), (1, 0)])  6.95 us
    all_to_all x1, starting transfers between devices, body(): lax.all_to_all(sums, second, 0, 0)  6.2 us
    pallas_call x1, Pallas kernels, attend(): pl.pallas_call(attend_kernel, out_shape=(jax.ShapeDtypeStruct((KVH, HD, c...  5.56 us
    unnamed x10, local copies, waits for them, and re-layouts  4.68 us
  transfers between devices with their start and end apart: 3, of which 2 were waited for; matrix products, arithmetic and copies ran while one was open for 0% of the time, Pallas kernels for 4%

profile of v5, /device:TPU:6, one launch (start us, length us, event | category | flops | bytes accessed | tf_op | source)
XLA Modules:
  0.0 98.2 jit_solution(6406023942215785173)
XLA Ops:
  0.6 0.8 pad_maximum_fusion
  1.5 27.6 %all_to_all.20.near_in = bf16[8,64,512]{2,1,0:T(8,128)(2,1)S(1)} all-to-all(bf16[8,64,512]{2,1,0:T(8,128)(2,1)S(1)} %broadcast_in_dim.21), channel_id=1, replica_groups=mesh['yh'=4,'x1'=2,'x0'=2,'core'=2,'yl'=2,'z2'=2,'z1'=2,'z0'=2] {'z2','z..., dimensions={0} | all-to-all | bytes 1048576 | tf_op jit(solution)/shard_map/all_to_all | solution.py:282
  29.1 3.5 %collective-permute-start = (bf16[8,64,512]{2,1,0:T(8,128)(2,1)S(1)}, bf16[8,64,512]{2,1,0:T(8,128)(2,1)S(1)}, u32[]{:S(2)}, u32[]{:S(2)}) collective-permute-start(bf16[8,64,512]{2,1,0:T(8,128)(2,1)S(1)} %all_to_all.20.near_in), channel_id=1, source_target_pairs={{0,8},{8,0},{1,9},{9,1},{2,10},{10,2},{3,11},{11,3},{4,12},{12,4},... | collective-permute-start | bytes 1572872 | tf_op jit(solution)/shard_map/ppermute | solution.py:286
  33.2 0.0 copy-start
  33.2 1.1 %copy-done = bf16[1,1,128,2560]{3,2,1,0:T(8,128)(2,1)S(1)} copy-done((bf16[1,1,128,2560]{3,2,1,0:T(8,128)(2,1)S(1)}, bf16[1,1,128,2560]{3,2,1,0:T(8,128)(2,1)}, u32[]{:S(2)}) %copy-start) | copy-done | bytes 655384
  34.3 0.0 copy-start.1
  34.3 1.1 %copy-done.1 = bf16[1,1,128,2560]{3,2,1,0:T(8,128)(2,1)S(1)} copy-done((bf16[1,1,128,2560]{3,2,1,0:T(8,128)(2,1)S(1)}, bf16[1,1,128,2560]{3,2,1,0:T(8,128)(2,1)}, u32[]{:S(2)}) %copy-start.1) | copy-done | bytes 655384
  35.4 0.0 copy-start.2
  35.4 0.9 copy-done.2
  36.3 0.0 copy-start.3
  36.3 0.9 copy-done.3
  37.2 0.0 copy-start.4
  37.2 0.7 copy-done.4
  37.9 1.0 %shard_map.127 = (bf16[4,640,128]{2,1,0:T(8,128)(2,1)S(1)}, bf16[4,640,128]{2,1,0:T(8,128)(2,1)S(1)}, bf16[128,512]{1,0:T(8,128)(2,1)S(1)}, bf16[128,512]{1,0:T(8,128)(2,1)S(1)}) custom-call(s32[1,1]{1,0:T(1,128)S(6)} %copy.14.length_ref, bf16[128,2560]{1,0:T(8,128)(2,1)S(1)} %bitcast.12, f32[2560]{0:T(1024)S(1)} %copy-done.4, ...), custom_call_target="tpu_custom_call" | custom-call | flops 327680 | bytes 4194304 | tf_op jit(solution)/shard_map/pallas_call | solution.py:62
  38.9 1.6 %shard_map.128 = (f32[4,384,640]{2,1,0:T(8,128)S(1)}, f32[4,384,640]{2,1,0:T(8,128)S(1)}, f32[4,8,640]{2,1,0:T(8,128)S(1)}) custom-call(s32[1,1]{1,0:T(1,128)S(6)} %copy.14.length_ref, bf16[4,640,128]{2,1,0:T(8,128)(2,1)S(1)} %get-tuple-element.26.qs_ref, bf16[4,640,128]{2,1,0:T(8,128)(2,1)S(1)} %get-tuple-element.27.dos_ref, ...), custom_call_target="tpu_custom_call" | custom-call | flops 503316480 | bytes 2097152 | tf_op jit(solution)/shard_map/pallas_call | solution.py:125
  40.5 2.3 %collective-permute-done.far_in = bf16[8,64,512]{2,1,0:T(8,128)(2,1)S(1)} collective-permute-done((bf16[8,64,512]{2,1,0:T(8,128)(2,1)S(1)}, bf16[8,64,512]{2,1,0:T(8,128)(2,1)S(1)}, u32[]{:S(2)}, u32[]{:S(2)}) %collective-permute-start) | collective-permute-done | bytes 524320 | tf_op jit(solution)/shard_map/ppermute | solution.py:286
  42.8 5.6 %shard_map.129 = (bf16[4,128,640]{2,1,0:T(8,128)(2,1)S(1)}, bf16[128,512]{1,0:T(8,128)(2,1)}, bf16[128,512]{1,0:T(8,128)(2,1)}, bf16[8,64,512]{2,1,0:T(8,128)(2,...) custom-call(bf16[4,640,128]{2,1,0:T(8,128)(2,1)S(1)} %get-tuple-element.26.qs_ref, ...), custom_call_target="tpu_custom_call" | custom-call | flops 1677721600 | bytes 6291456 | tf_op jit(solution)/shard_map/pallas_call | solution.py:209
  48.4 3.5 %collective-permute-start.1 = (bf16[8,64,512]{2,1,0:T(8,128)(2,1)S(1)}, bf16[8,64,512]{2,1,0:T(8,128)(2,1)S(1)}, u32[]{:S(2)}, u32[]{:S(2)}) collective-permute-start(bf16[8,64,512]{2,1,0:T(8,128)(2,1)S(1)} %get-tuple-element.41), channel_id=1, source_target_pairs={{0,8},{8,0},{1,9},{9,1},{2,10},{10,2},{3,11},{11,3},{4,12},{12,4},... | collective-permute-start | bytes 1572872 | tf_op jit(solution)/shard_map/ppermute | solution.py:286
  51.9 8.3 %all_to_all.21.got = f32[8,20,128]{2,1,0:T(8,128)S(1)} all-to-all(f32[8,20,128]{2,1,0:T(8,128)S(1)} %get-tuple-element.33), channel_id=1, replica_groups=mesh['yh'=4,'x1'=2,'x0'=2,'core'=2,'yl'=2,'z2'=2,'z1'=2,'z0'=2] {'x1','x..., dimensions={0} | all-to-all | bytes 163840 | tf_op jit(solution)/shard_map/all_to_all | solution.py:308
  60.2 0.6 shard_map.130
  60.8 6.2 %all-to-all-start.2 = ((f32[8,20,128]{2,1,0:T(8,128)}), f32[8,20,128]{2,1,0:T(8,128)S(1)}, u32[]{:S(2)}, u32[]{:S(2)}) async-start(f32[8,20,128]{2,1,0:T(8,128)} %shard_map.130), calls=%async_computation.2 | async-start | bytes 196608 | tf_op jit(solution)/shard_map/all_to_all | solution.py:312
  67.0 1.1 %shard_map.131 = bf16[128,2560]{1,0:T(8,128)(2,1)} custom-call(bf16[4,128,640]{2,1,0:T(8,128)(2,1)S(1)} %get-tuple-element.36.flat_ref), custom_call_target="tpu_custom_call" | custom-call | tf_op jit(solution)/shard_map/pallas_call | solution.py:273
  68.1 7.7 %all-to-all-done.2.sums = f32[8,20,128]{2,1,0:T(8,128)S(1)} async-done(((f32[8,20,128]{2,1,0:T(8,128)}), f32[8,20,128]{2,1,0:T(8,128)S(1)}, u32[]{:S(2)}, u32[]{:S(2)}) %all-to-all-start.2) | async-done | bytes 81952 | tf_op jit(solution)/shard_map/all_to_all | solution.py:312
  75.8 0.0 collective-permute-done.1.got
  75.8 0.1 shard_map.132
  75.9 21.6 %all_to_all.22.got = bf16[8,80,512]{2,1,0:T(8,128)(2,1)S(1)} all-to-all(bf16[8,80,512]{2,1,0:T(8,128)(2,1)S(1)} %shard_map.132), channel_id=1, replica_groups=mesh['yh'=4,'x1'=2,'x0'=2,'core'=2,'yl'=2,'z2'=2,'z1'=2,'z0'=2] {'z2','z..., dimensions={0} | all-to-all | bytes 1310720 | tf_op jit(solution)/shard_map/all_to_all | solution.py:318
  97.5 0.7 shard_map.133
  (1 shorter events, 0.0 us)
Async XLA Ops:
  29.1 13.8 %collective-permute-start = (bf16[8,64,512]{2,1,0:T(8,128)(2,1)S(1)}, bf16[8,64,512]{2,1,0:T(8,128)(2,1)S(1)}, u32[]{:S(2)}, u32[]{:S(2)}) collective-permute-start(bf16[8,64,512]{2,1,0:T(8,128)(2,1)S(1)} %all_to_all.20.near_in), channel_id=1, source_target_pairs={{0,8},{8,0},{1,9},{9,1},{2,10},{10,2},{3,11},{11,3},{4,12},{12,4},... | collective-permute-start | bytes 1572872 | tf_op jit(solution)/shard_map/ppermute | solution.py:286
  33.2 1.1 %copy-start = (bf16[1,1,128,2560]{3,2,1,0:T(8,128)(2,1)S(1)}, bf16[1,1,128,2560]{3,2,1,0:T(8,128)(2,1)}, u32[]{:S(2)}) copy-start(bf16[1,1,128,2560]{3,2,1,0:T(8,128)(2,1)} %param.10) | copy-start | bytes 1966084
  34.3 1.1 %copy-start.1 = (bf16[1,1,128,2560]{3,2,1,0:T(8,128)(2,1)S(1)}, bf16[1,1,128,2560]{3,2,1,0:T(8,128)(2,1)}, u32[]{:S(2)}) copy-start(bf16[1,1,128,2560]{3,2,1,0:T(8,128)(2,1)} %param.14) | copy-start | bytes 1966084
  35.4 0.9 copy-start.2
  36.3 0.9 copy-start.3
  37.2 0.7 copy-start.4
  48.4 27.4 %collective-permute-start.1 = (bf16[8,64,512]{2,1,0:T(8,128)(2,1)S(1)}, bf16[8,64,512]{2,1,0:T(8,128)(2,1)S(1)}, u32[]{:S(2)}, u32[]{:S(2)}) collective-permute-start(bf16[8,64,512]{2,1,0:T(8,128)(2,1)S(1)} %get-tuple-element.41), channel_id=1, source_target_pairs={{0,8},{8,0},{1,9},{9,1},{2,10},{10,2},{3,11},{11,3},{4,12},{12,4},... | collective-permute-start | bytes 1572872 | tf_op jit(solution)/shard_map/ppermute | solution.py:286
  60.8 14.9 %all-to-all-start.2 = ((f32[8,20,128]{2,1,0:T(8,128)}), f32[8,20,128]{2,1,0:T(8,128)S(1)}, u32[]{:S(2)}, u32[]{:S(2)}) async-start(f32[8,20,128]{2,1,0:T(8,128)} %shard_map.130), calls=%async_computation.2 | async-start | bytes 196608 | tf_op jit(solution)/shard_map/all_to_all | solution.py:312

commit v6 on v5

--- a/solution.py
+++ b/solution.py
@@ -178,14 +178,15 @@
                 expd * ((dprobs - delta) * (factor * SCALE))
             ).astype(BF16)
         dscores = dscores_s[group]
-        for at, left, right, own in (
-            (0, dscores, qs_ref, drk_ref),
-            (shard_rows, probs_s[group], dos_ref, drv_ref),
+        for block, left, right, own in (
+            (group, dscores, qs_ref, drk_ref),
+            (KVH + group, probs_s[group], dos_ref, drv_ref),
         ):
             grad = dot(left, right[group], 1, 0).astype(BF16)
             own[:, cols] = grad[half:first]
+            at = slice(block * shard_rows, (block + 1) * shard_rows)
             for ref, part in ((near_ref, grad[:half]), (far_ref, grad[first:])):
-                ref[:, at : at + shard_rows, cols] = part.reshape(shards, shard_rows, HD)
+                ref[:, at, :] = part.reshape(shards, shard_rows, HD)
         near_keys = near_in[:, :shard_rows, cols].reshape(half, HD)
         keys = jnp.concatenate([near_keys, rk_ref[:, cols], far_keys], 0)
         dq = dot(keys, dscores, 0, 0)
@@ -211,7 +212,7 @@
         out_shape=(
             jax.ShapeDtypeStruct((KVH, HD, columns), BF16),
             *[jax.ShapeDtypeStruct((rows, width), BF16)] * 2,
-            *[jax.ShapeDtypeStruct((shards, both_rows, width), BF16)] * 2,
+            *[jax.ShapeDtypeStruct((shards, both_rows * KVH, HD), BF16)] * 2,
             jax.ShapeDtypeStruct((copies, KVH * GROUP, HD), F32),
         ),
         in_specs=[vmem] * 8,
@@ -243,30 +244,32 @@
 
 
 def pair_kernel(near, got, sums, out):
-    shards, both_rows, width = near.shape
-    more = out.shape[1] - both_rows
-    out[:, :both_rows, :] = (near[...].astype(F32) + got[...].astype(F32)).astype(BF16)
+    shards, data_rows, _ = near.shape
+    room = (out.shape[1] - data_rows) // 2
+    out[:, :data_rows, :] = (near[...].astype(F32) + got[...].astype(F32)).astype(BF16)
     total = sums[0]
     for copy in range(1, sums.shape[0]):
         total = total + sums[copy]
-    total = jnp.concatenate([total, jnp.zeros((2 * more - total.shape[0], HD), F32)], 0)
-    high = total.astype(BF16)
-    low = (total - high.astype(F32)).astype(BF16)
-    terms = jnp.concatenate([high[:more], high[more:], low[:more], low[more:]], 1)
+    total = jnp.concatenate([total, jnp.zeros((room - total.shape[0], HD), F32)], 0)
+    high = total.astype(BF16).astype(F32)
+    terms = jnp.concatenate([high, total - high], 0).astype(BF16)
     for shard in range(shards):
-        out[shard, both_rows:, :] = terms
+        out[shard, data_rows:, :] = terms
 
 
 def finish_kernel(divisor, got, dk_ref, dv_ref, sums_ref):
     rows = dk_ref.shape[0]
+    data_rows = 2 * KVH * rows
+    room = (got.shape[1] - data_rows) // 2
     total = got[0].astype(F32)
     for shard in range(1, got.shape[0]):
         total = total + got[shard].astype(F32)
-    dk_ref[...] = total[:rows].astype(BF16)
-    dv_ref[...] = total[rows : 2 * rows].astype(BF16)
-    terms = total[2 * rows :, : 2 * HD] + total[2 * rows :, 2 * HD :]
-    sums = jnp.concatenate([terms[:, :HD], terms[:, HD:]], 0)[: sums_ref.shape[0]]
-    sums_ref[...] = sums / divisor
+    for group in range(KVH):
+        cols = slice(group * HD, (group + 1) * HD)
+        for ref, block in ((dk_ref, group), (dv_ref, KVH + group)):
+            ref[:, cols] = total[block * rows : (block + 1) * rows].astype(BF16)
+    sums = total[data_rows : data_rows + room] + total[data_rows + room :]
+    sums_ref[...] = sums[: sums_ref.shape[0]] / divisor
 
 
 def small_call(kernel, out_shape, *operands):
@@ -312,7 +315,7 @@
     sums, dq = lax.optimization_barrier((lax.all_to_all(sums, second, 0, 0), dq))
     pairs = small_call(
         pair_kernel,
-        jax.ShapeDtypeStruct((near.shape[0], 2 * shard_rows + 16, kv_width), BF16),
+        jax.ShapeDtypeStruct((mine.shape[0], mine.shape[1] + 48, HD), BF16),
         mine, got, sums,
     )
     summed = lax.all_to_all(pairs, Z, 0, 0)

time: 99.4 us -> 98.7 us (level)
  no operation moved by 1% of the time
where the time goes in v6:
time: 98.7 us; the launch traced here: 97.4 us
  blocking collectives  56.8 us (58%)
  starting transfers between devices  13.2 us (13%)
  Pallas kernels  10.7 us (11%)
  waiting for transfers between devices  10 us (10%)
  local copies, waits for them, and re-layouts  4.72 us (5%)
  between operations  1.33 us (1%)
    all_to_all x1, blocking collectives, spread(): return lax.all_to_all(copies, axis, 0, 0)  27.6 us
    all_to_all x1, blocking collectives, body(): summed = lax.all_to_all(pairs, Z, 0, 0)  20.8 us
    all_to_all x1, blocking collectives, body(): lax.all_to_all(sums, first, 0, 0)  8.3 us
    all_to_all x1, waiting for transfers between devices, body(): lax.all_to_all(sums, second, 0, 0)  7.67 us
    ppermute x2, starting transfers between devices, swap(): return lax.ppermute(block, axis, [(0, 1), (1, 0)])  6.95 us
    all_to_all x1, starting transfers between devices, body(): lax.all_to_all(sums, second, 0, 0)  6.21 us
    pallas_call x1, Pallas kernels, attend(): pl.pallas_call(attend_kernel, out_shape=(jax.ShapeDtypeStruct((KVH, HD, c...  5.57 us
    unnamed x10, local copies, waits for them, and re-layouts  4.68 us
  transfers between devices with their start and end apart: 3, of which 2 were waited for; matrix products, arithmetic and copies ran while one was open for 0% of the time, Pallas kernels for 4%

profile of v6, /device:TPU:6, one launch (start us, length us, event | category | flops | bytes accessed | tf_op | source)
XLA Modules:
  0.0 97.4 jit_solution(5950616033968424463)
XLA Ops:
  0.6 0.8 pad_maximum_fusion
  1.5 27.6 %all_to_all.20.near_in = bf16[8,64,512]{2,1,0:T(8,128)(2,1)S(1)} all-to-all(bf16[8,64,512]{2,1,0:T(8,128)(2,1)S(1)} %broadcast_in_dim.21), channel_id=1, replica_groups=mesh['yh'=4,'x1'=2,'x0'=2,'core'=2,'yl'=2,'z2'=2,'z1'=2,'z0'=2] {'z2','z..., dimensions={0} | all-to-all | bytes 1048576 | tf_op jit(solution)/shard_map/all_to_all | solution.py:285
  29.1 3.5 %collective-permute-start = (bf16[8,64,512]{2,1,0:T(8,128)(2,1)S(1)}, bf16[8,64,512]{2,1,0:T(8,128)(2,1)S(1)}, u32[]{:S(2)}, u32[]{:S(2)}) collective-permute-start(bf16[8,64,512]{2,1,0:T(8,128)(2,1)S(1)} %all_to_all.20.near_in), channel_id=1, source_target_pairs={{0,8},{8,0},{1,9},{9,1},{2,10},{10,2},{3,11},{11,3},{4,12},{12,4},... | collective-permute-start | bytes 1572872 | tf_op jit(solution)/shard_map/ppermute | solution.py:289
  33.2 0.0 copy-start
  33.2 1.1 %copy-done = bf16[1,1,128,2560]{3,2,1,0:T(8,128)(2,1)S(1)} copy-done((bf16[1,1,128,2560]{3,2,1,0:T(8,128)(2,1)S(1)}, bf16[1,1,128,2560]{3,2,1,0:T(8,128)(2,1)}, u32[]{:S(2)}) %copy-start) | copy-done | bytes 655384
  34.3 0.0 copy-start.1
  34.3 1.1 %copy-done.1 = bf16[1,1,128,2560]{3,2,1,0:T(8,128)(2,1)S(1)} copy-done((bf16[1,1,128,2560]{3,2,1,0:T(8,128)(2,1)S(1)}, bf16[1,1,128,2560]{3,2,1,0:T(8,128)(2,1)}, u32[]{:S(2)}) %copy-start.1) | copy-done | bytes 655384
  35.4 0.0 copy-start.2
  35.4 0.9 copy-done.2
  36.3 0.0 copy-start.3
  36.3 0.9 copy-done.3
  37.2 0.0 copy-start.4
  37.2 0.7 copy-done.4
  37.9 1.0 %shard_map.127 = (bf16[4,640,128]{2,1,0:T(8,128)(2,1)S(1)}, bf16[4,640,128]{2,1,0:T(8,128)(2,1)S(1)}, bf16[128,512]{1,0:T(8,128)(2,1)S(1)}, bf16[128,512]{1,0:T(8,128)(2,1)S(1)}) custom-call(s32[1,1]{1,0:T(1,128)S(6)} %copy.14.length_ref, bf16[128,2560]{1,0:T(8,128)(2,1)S(1)} %bitcast.12, f32[2560]{0:T(1024)S(1)} %copy-done.4, ...), custom_call_target="tpu_custom_call" | custom-call | flops 327680 | bytes 4194304 | tf_op jit(solution)/shard_map/pallas_call | solution.py:62
  38.9 1.6 %shard_map.128 = (f32[4,384,640]{2,1,0:T(8,128)S(1)}, f32[4,384,640]{2,1,0:T(8,128)S(1)}, f32[4,8,640]{2,1,0:T(8,128)S(1)}) custom-call(s32[1,1]{1,0:T(1,128)S(6)} %copy.14.length_ref, bf16[4,640,128]{2,1,0:T(8,128)(2,1)S(1)} %get-tuple-element.26.qs_ref, bf16[4,640,128]{2,1,0:T(8,128)(2,1)S(1)} %get-tuple-element.27.dos_ref, ...), custom_call_target="tpu_custom_call" | custom-call | flops 503316480 | bytes 2097152 | tf_op jit(solution)/shard_map/pallas_call | solution.py:125
  40.5 2.3 %collective-permute-done.far_in = bf16[8,64,512]{2,1,0:T(8,128)(2,1)S(1)} collective-permute-done((bf16[8,64,512]{2,1,0:T(8,128)(2,1)S(1)}, bf16[8,64,512]{2,1,0:T(8,128)(2,1)S(1)}, u32[]{:S(2)}, u32[]{:S(2)}) %collective-permute-start) | collective-permute-done | bytes 524320 | tf_op jit(solution)/shard_map/ppermute | solution.py:289
  42.8 5.6 %shard_map.129 = (bf16[4,128,640]{2,1,0:T(8,128)(2,1)S(1)}, bf16[128,512]{1,0:T(8,128)(2,1)}, bf16[128,512]{1,0:T(8,128)(2,1)}, bf16[8,256,128]{2,1,0:T(8,128)(2...) custom-call(bf16[4,640,128]{2,1,0:T(8,128)(2,1)S(1)} %get-tuple-element.26.qs_ref, ...), custom_call_target="tpu_custom_call" | custom-call | flops 1677721600 | bytes 6291456 | tf_op jit(solution)/shard_map/pallas_call | solution.py:210
  48.4 3.5 %collective-permute-start.1 = (bf16[8,256,128]{2,1,0:T(8,128)(2,1)S(1)}, bf16[8,256,128]{2,1,0:T(8,128)(2,1)S(1)}, u32[]{:S(2)}, u32[]{:S(2)}) collective-permute-start(bf16[8,256,128]{2,1,0:T(8,128)(2,1)S(1)} %get-tuple-element.41), channel_id=1, source_target_pairs={{0,8},{8,0},{1,9},{9,1},{2,10},{10,2},{3,11},{11,3},{4,12},{12,4},... | collective-permute-start | bytes 1572872 | tf_op jit(solution)/shard_map/ppermute | solution.py:289
  51.9 8.3 %all_to_all.21.got = f32[8,20,128]{2,1,0:T(8,128)S(1)} all-to-all(f32[8,20,128]{2,1,0:T(8,128)S(1)} %get-tuple-element.33), channel_id=1, replica_groups=mesh['yh'=4,'x1'=2,'x0'=2,'core'=2,'yl'=2,'z2'=2,'z1'=2,'z0'=2] {'x1','x..., dimensions={0} | all-to-all | bytes 163840 | tf_op jit(solution)/shard_map/all_to_all | solution.py:311
  60.2 0.6 shard_map.130
  60.8 6.2 %all-to-all-start.2 = ((f32[8,20,128]{2,1,0:T(8,128)}), f32[8,20,128]{2,1,0:T(8,128)S(1)}, u32[]{:S(2)}, u32[]{:S(2)}) async-start(f32[8,20,128]{2,1,0:T(8,128)} %shard_map.130), calls=%async_computation.2 | async-start | bytes 196608 | tf_op jit(solution)/shard_map/all_to_all | solution.py:315
  67.0 1.1 %shard_map.131 = bf16[128,2560]{1,0:T(8,128)(2,1)} custom-call(bf16[4,128,640]{2,1,0:T(8,128)(2,1)S(1)} %get-tuple-element.36.flat_ref), custom_call_target="tpu_custom_call" | custom-call | tf_op jit(solution)/shard_map/pallas_call | solution.py:276
  68.1 7.7 %all-to-all-done.2.sums = f32[8,20,128]{2,1,0:T(8,128)S(1)} async-done(((f32[8,20,128]{2,1,0:T(8,128)}), f32[8,20,128]{2,1,0:T(8,128)S(1)}, u32[]{:S(2)}, u32[]{:S(2)}) %all-to-all-start.2) | async-done | bytes 81952 | tf_op jit(solution)/shard_map/all_to_all | solution.py:315
  75.8 0.0 collective-permute-done.1.got
  75.8 0.1 shard_map.132
  75.9 20.8 %all_to_all.22.got = bf16[8,304,128]{2,1,0:T(8,128)(2,1)S(1)} all-to-all(bf16[8,304,128]{2,1,0:T(8,128)(2,1)S(1)} %shard_map.132), channel_id=1, replica_groups=mesh['yh'=4,'x1'=2,'x0'=2,'core'=2,'yl'=2,'z2'=2,'z1'=2,'z0'=2] {'z2','z..., dimensions={0} | all-to-all | bytes 1245184 | tf_op jit(solution)/shard_map/all_to_all | solution.py:321
  96.8 0.7 shard_map.133
  (1 shorter events, 0.0 us)
Async XLA Ops:
  29.1 13.8 %collective-permute-start = (bf16[8,64,512]{2,1,0:T(8,128)(2,1)S(1)}, bf16[8,64,512]{2,1,0:T(8,128)(2,1)S(1)}, u32[]{:S(2)}, u32[]{:S(2)}) collective-permute-start(bf16[8,64,512]{2,1,0:T(8,128)(2,1)S(1)} %all_to_all.20.near_in), channel_id=1, source_target_pairs={{0,8},{8,0},{1,9},{9,1},{2,10},{10,2},{3,11},{11,3},{4,12},{12,4},... | collective-permute-start | bytes 1572872 | tf_op jit(solution)/shard_map/ppermute | solution.py:289
  33.2 1.1 %copy-start = (bf16[1,1,128,2560]{3,2,1,0:T(8,128)(2,1)S(1)}, bf16[1,1,128,2560]{3,2,1,0:T(8,128)(2,1)}, u32[]{:S(2)}) copy-start(bf16[1,1,128,2560]{3,2,1,0:T(8,128)(2,1)} %param.10) | copy-start | bytes 1966084
  34.3 1.1 %copy-start.1 = (bf16[1,1,128,2560]{3,2,1,0:T(8,128)(2,1)S(1)}, bf16[1,1,128,2560]{3,2,1,0:T(8,128)(2,1)}, u32[]{:S(2)}) copy-start(bf16[1,1,128,2560]{3,2,1,0:T(8,128)(2,1)} %param.14) | copy-start | bytes 1966084
  35.4 0.9 copy-start.2
  36.3 0.9 copy-start.3
  37.2 0.7 copy-start.4
  48.4 27.4 %collective-permute-start.1 = (bf16[8,256,128]{2,1,0:T(8,128)(2,1)S(1)}, bf16[8,256,128]{2,1,0:T(8,128)(2,1)S(1)}, u32[]{:S(2)}, u32[]{:S(2)}) collective-permute-start(bf16[8,256,128]{2,1,0:T(8,128)(2,1)S(1)} %get-tuple-element.41), channel_id=1, source_target_pairs={{0,8},{8,0},{1,9},{9,1},{2,10},{10,2},{3,11},{11,3},{4,12},{12,4},... | collective-permute-start | bytes 1572872 | tf_op jit(solution)/shard_map/ppermute | solution.py:289
  60.8 14.9 %all-to-all-start.2 = ((f32[8,20,128]{2,1,0:T(8,128)}), f32[8,20,128]{2,1,0:T(8,128)S(1)}, u32[]{:S(2)}, u32[]{:S(2)}) async-start(f32[8,20,128]{2,1,0:T(8,128)} %shard_map.130), calls=%async_computation.2 | async-start | bytes 196608 | tf_op jit(solution)/shard_map/all_to_all | solution.py:315

commit v7 on v6

--- a/solution.py
+++ b/solution.py
@@ -177,6 +177,8 @@
             dscores_s[group, :first, span] = (
                 expd * ((dprobs - delta) * (factor * SCALE))
             ).astype(BF16)
+    for group in range(KVH):
+        cols = slice(group * HD, (group + 1) * HD)
         dscores = dscores_s[group]
         for block, left, right, own in (
             (group, dscores, qs_ref, drk_ref),
@@ -187,7 +189,7 @@
             at = slice(block * shard_rows, (block + 1) * shard_rows)
             for ref, part in ((near_ref, grad[:half]), (far_ref, grad[first:])):
                 ref[:, at, :] = part.reshape(shards, shard_rows, HD)
-        near_keys = near_in[:, :shard_rows, cols].reshape(half, HD)
+        near_keys, far_keys = (ref[:, :shard_rows, cols].reshape(half, HD) for ref in (near_in, far_in))
         keys = jnp.concatenate([near_keys, rk_ref[:, cols], far_keys], 0)
         dq = dot(keys, dscores, 0, 0)
         flat_ref[group] = dq.astype(BF16)

time: 98.7 us -> 98.1 us (level)
  no operation moved by 1% of the time
where the time goes in v7:
time: 98.1 us; the launch traced here: 96.8 us
  blocking collectives  56.8 us (58%)
  starting transfers between devices  13.1 us (13%)
  Pallas kernels  10.1 us (10%)
  waiting for transfers between devices  10 us (10%)
  local copies, waits for them, and re-layouts  4.72 us (5%)
  between operations  1.33 us (1%)
    all_to_all x1, blocking collectives, spread(): return lax.all_to_all(copies, axis, 0, 0)  27.6 us
    all_to_all x1, blocking collectives, body(): summed = lax.all_to_all(pairs, Z, 0, 0)  20.9 us
    all_to_all x1, blocking collectives, body(): lax.all_to_all(sums, first, 0, 0)  8.3 us
    all_to_all x1, waiting for transfers between devices, body(): lax.all_to_all(sums, second, 0, 0)  7.67 us
    ppermute x2, starting transfers between devices, swap(): return lax.ppermute(block, axis, [(0, 1), (1, 0)])  6.95 us
    all_to_all x1, starting transfers between devices, body(): lax.all_to_all(sums, second, 0, 0)  6.2 us
    pallas_call x1, Pallas kernels, attend(): pl.pallas_call(attend_kernel, out_shape=(jax.ShapeDtypeStruct((KVH, HD, c...  4.95 us
    unnamed x10, local copies, waits for them, and re-layouts  4.68 us
  transfers between devices with their start and end apart: 3, of which 2 were waited for; matrix products, arithmetic and copies ran while one was open for 0% of the time, Pallas kernels for 4%

profile of v7, /device:TPU:6, one launch (start us, length us, event | category | flops | bytes accessed | tf_op | source)
XLA Modules:
  0.0 96.8 jit_solution(5289958140600946529)
XLA Ops:
  0.6 0.8 pad_maximum_fusion
  1.5 27.6 %all_to_all.20.near_in = bf16[8,64,512]{2,1,0:T(8,128)(2,1)S(1)} all-to-all(bf16[8,64,512]{2,1,0:T(8,128)(2,1)S(1)} %broadcast_in_dim.21), channel_id=1, replica_groups=mesh['yh'=4,'x1'=2,'x0'=2,'core'=2,'yl'=2,'z2'=2,'z1'=2,'z0'=2] {'z2','z..., dimensions={0} | all-to-all | bytes 1048576 | tf_op jit(solution)/shard_map/all_to_all | solution.py:287
  29.1 3.5 %collective-permute-start = (bf16[8,64,512]{2,1,0:T(8,128)(2,1)S(1)}, bf16[8,64,512]{2,1,0:T(8,128)(2,1)S(1)}, u32[]{:S(2)}, u32[]{:S(2)}) collective-permute-start(bf16[8,64,512]{2,1,0:T(8,128)(2,1)S(1)} %all_to_all.20.near_in), channel_id=1, source_target_pairs={{0,8},{8,0},{1,9},{9,1},{2,10},{10,2},{3,11},{11,3},{4,12},{12,4},... | collective-permute-start | bytes 1572872 | tf_op jit(solution)/shard_map/ppermute | solution.py:291
  33.2 0.0 copy-start
  33.2 1.1 %copy-done = bf16[1,1,128,2560]{3,2,1,0:T(8,128)(2,1)S(1)} copy-done((bf16[1,1,128,2560]{3,2,1,0:T(8,128)(2,1)S(1)}, bf16[1,1,128,2560]{3,2,1,0:T(8,128)(2,1)}, u32[]{:S(2)}) %copy-start) | copy-done | bytes 655384
  34.3 0.0 copy-start.1
  34.3 1.1 %copy-done.1 = bf16[1,1,128,2560]{3,2,1,0:T(8,128)(2,1)S(1)} copy-done((bf16[1,1,128,2560]{3,2,1,0:T(8,128)(2,1)S(1)}, bf16[1,1,128,2560]{3,2,1,0:T(8,128)(2,1)}, u32[]{:S(2)}) %copy-start.1) | copy-done | bytes 655384
  35.4 0.0 copy-start.2
  35.4 0.9 copy-done.2
  36.3 0.0 copy-start.3
  36.3 0.9 copy-done.3
  37.2 0.0 copy-start.4
  37.2 0.7 copy-done.4
  37.9 1.0 %shard_map.127 = (bf16[4,640,128]{2,1,0:T(8,128)(2,1)S(1)}, bf16[4,640,128]{2,1,0:T(8,128)(2,1)S(1)}, bf16[128,512]{1,0:T(8,128)(2,1)S(1)}, bf16[128,512]{1,0:T(8,128)(2,1)S(1)}) custom-call(s32[1,1]{1,0:T(1,128)S(6)} %copy.14.length_ref, bf16[128,2560]{1,0:T(8,128)(2,1)S(1)} %bitcast.12, f32[2560]{0:T(1024)S(1)} %copy-done.4, ...), custom_call_target="tpu_custom_call" | custom-call | flops 327680 | bytes 4194304 | tf_op jit(solution)/shard_map/pallas_call | solution.py:62
  38.9 1.6 %shard_map.128 = (f32[4,384,640]{2,1,0:T(8,128)S(1)}, f32[4,384,640]{2,1,0:T(8,128)S(1)}, f32[4,8,640]{2,1,0:T(8,128)S(1)}) custom-call(s32[1,1]{1,0:T(1,128)S(6)} %copy.14.length_ref, bf16[4,640,128]{2,1,0:T(8,128)(2,1)S(1)} %get-tuple-element.26.qs_ref, bf16[4,640,128]{2,1,0:T(8,128)(2,1)S(1)} %get-tuple-element.27.dos_ref, ...), custom_call_target="tpu_custom_call" | custom-call | flops 503316480 | bytes 2097152 | tf_op jit(solution)/shard_map/pallas_call | solution.py:125
  40.5 2.3 %collective-permute-done.far_in = bf16[8,64,512]{2,1,0:T(8,128)(2,1)S(1)} collective-permute-done((bf16[8,64,512]{2,1,0:T(8,128)(2,1)S(1)}, bf16[8,64,512]{2,1,0:T(8,128)(2,1)S(1)}, u32[]{:S(2)}, u32[]{:S(2)}) %collective-permute-start) | collective-permute-done | bytes 524320 | tf_op jit(solution)/shard_map/ppermute | solution.py:291
  42.8 4.9 %shard_map.129 = (bf16[4,128,640]{2,1,0:T(8,128)(2,1)S(1)}, bf16[128,512]{1,0:T(8,128)(2,1)}, bf16[128,512]{1,0:T(8,128)(2,1)}, bf16[8,256,128]{2,1,0:T(8,128)(2...) custom-call(bf16[4,640,128]{2,1,0:T(8,128)(2,1)S(1)} %get-tuple-element.26.qs_ref, ...), custom_call_target="tpu_custom_call" | custom-call | flops 1677721600 | bytes 6291456 | tf_op jit(solution)/shard_map/pallas_call | solution.py:212
  47.8 3.5 %collective-permute-start.1 = (bf16[8,256,128]{2,1,0:T(8,128)(2,1)S(1)}, bf16[8,256,128]{2,1,0:T(8,128)(2,1)S(1)}, u32[]{:S(2)}, u32[]{:S(2)}) collective-permute-start(bf16[8,256,128]{2,1,0:T(8,128)(2,1)S(1)} %get-tuple-element.41), channel_id=1, source_target_pairs={{0,8},{8,0},{1,9},{9,1},{2,10},{10,2},{3,11},{11,3},{4,12},{12,4},... | collective-permute-start | bytes 1572872 | tf_op jit(solution)/shard_map/ppermute | solution.py:291
  51.3 8.3 %all_to_all.21.got = f32[8,20,128]{2,1,0:T(8,128)S(1)} all-to-all(f32[8,20,128]{2,1,0:T(8,128)S(1)} %get-tuple-element.33), channel_id=1, replica_groups=mesh['yh'=4,'x1'=2,'x0'=2,'core'=2,'yl'=2,'z2'=2,'z1'=2,'z0'=2] {'x1','x..., dimensions={0} | all-to-all | bytes 163840 | tf_op jit(solution)/shard_map/all_to_all | solution.py:313
  59.6 0.6 shard_map.130
  60.2 6.2 %all-to-all-start.2 = ((f32[8,20,128]{2,1,0:T(8,128)}), f32[8,20,128]{2,1,0:T(8,128)S(1)}, u32[]{:S(2)}, u32[]{:S(2)}) async-start(f32[8,20,128]{2,1,0:T(8,128)} %shard_map.130), calls=%async_computation.2 | async-start | bytes 196608 | tf_op jit(solution)/shard_map/all_to_all | solution.py:317
  66.4 1.1 %shard_map.131 = bf16[128,2560]{1,0:T(8,128)(2,1)} custom-call(bf16[4,128,640]{2,1,0:T(8,128)(2,1)S(1)} %get-tuple-element.36.flat_ref), custom_call_target="tpu_custom_call" | custom-call | tf_op jit(solution)/shard_map/pallas_call | solution.py:278
  67.5 7.7 %all-to-all-done.2.sums = f32[8,20,128]{2,1,0:T(8,128)S(1)} async-done(((f32[8,20,128]{2,1,0:T(8,128)}), f32[8,20,128]{2,1,0:T(8,128)S(1)}, u32[]{:S(2)}, u32[]{:S(2)}) %all-to-all-start.2) | async-done | bytes 81952 | tf_op jit(solution)/shard_map/all_to_all | solution.py:317
  75.1 0.0 collective-permute-done.1.got
  75.1 0.1 shard_map.132
  75.3 20.9 %all_to_all.22.got = bf16[8,304,128]{2,1,0:T(8,128)(2,1)S(1)} all-to-all(bf16[8,304,128]{2,1,0:T(8,128)(2,1)S(1)} %shard_map.132), channel_id=1, replica_groups=mesh['yh'=4,'x1'=2,'x0'=2,'core'=2,'yl'=2,'z2'=2,'z1'=2,'z0'=2] {'z2','z..., dimensions={0} | all-to-all | bytes 1245184 | tf_op jit(solution)/shard_map/all_to_all | solution.py:323
  96.1 0.7 shard_map.133
  (1 shorter events, 0.0 us)
Async XLA Ops:
  29.1 13.8 %collective-permute-start = (bf16[8,64,512]{2,1,0:T(8,128)(2,1)S(1)}, bf16[8,64,512]{2,1,0:T(8,128)(2,1)S(1)}, u32[]{:S(2)}, u32[]{:S(2)}) collective-permute-start(bf16[8,64,512]{2,1,0:T(8,128)(2,1)S(1)} %all_to_all.20.near_in), channel_id=1, source_target_pairs={{0,8},{8,0},{1,9},{9,1},{2,10},{10,2},{3,11},{11,3},{4,12},{12,4},... | collective-permute-start | bytes 1572872 | tf_op jit(solution)/shard_map/ppermute | solution.py:291
  33.2 1.1 %copy-start = (bf16[1,1,128,2560]{3,2,1,0:T(8,128)(2,1)S(1)}, bf16[1,1,128,2560]{3,2,1,0:T(8,128)(2,1)}, u32[]{:S(2)}) copy-start(bf16[1,1,128,2560]{3,2,1,0:T(8,128)(2,1)} %param.10) | copy-start | bytes 1966084
  34.3 1.1 %copy-start.1 = (bf16[1,1,128,2560]{3,2,1,0:T(8,128)(2,1)S(1)}, bf16[1,1,128,2560]{3,2,1,0:T(8,128)(2,1)}, u32[]{:S(2)}) copy-start(bf16[1,1,128,2560]{3,2,1,0:T(8,128)(2,1)} %param.14) | copy-start | bytes 1966084
  35.4 0.9 copy-start.2
  36.3 0.9 copy-start.3
  37.2 0.7 copy-start.4
  47.8 27.4 %collective-permute-start.1 = (bf16[8,256,128]{2,1,0:T(8,128)(2,1)S(1)}, bf16[8,256,128]{2,1,0:T(8,128)(2,1)S(1)}, u32[]{:S(2)}, u32[]{:S(2)}) collective-permute-start(bf16[8,256,128]{2,1,0:T(8,128)(2,1)S(1)} %get-tuple-element.41), channel_id=1, source_target_pairs={{0,8},{8,0},{1,9},{9,1},{2,10},{10,2},{3,11},{11,3},{4,12},{12,4},... | collective-permute-start | bytes 1572872 | tf_op jit(solution)/shard_map/ppermute | solution.py:291
  60.2 14.9 %all-to-all-start.2 = ((f32[8,20,128]{2,1,0:T(8,128)}), f32[8,20,128]{2,1,0:T(8,128)S(1)}, u32[]{:S(2)}, u32[]{:S(2)}) async-start(f32[8,20,128]{2,1,0:T(8,128)} %shard_map.130), calls=%async_computation.2 | async-start | bytes 196608 | tf_op jit(solution)/shard_map/all_to_all | solution.py:317

commit v8 on v7

--- a/solution.py
+++ b/solution.py
@@ -19,7 +19,7 @@
 PROMPT = ("yh", "x1", "x0", "core")
 RESP = ("yl", "z2", "z1", "z0")
 SIZES = (4, 2, 2, 2, 2, 2, 2, 2)
-Z = ("z2", "z1", "z0")
+Z = ("z1", "z0", "z2")
 
 
 def dot(a, b, a_dim, b_dim):

time: 98.1 us -> 97.6 us (level)
  waiting for transfers between devices: 10 us -> 8.75 us
    all_to_all x1, blocking collectives: 20.9 us -> 24.1 us  [body(): summed = lax.all_to_all(pairs, Z, 0, 0)]
    all_to_all x1, blocking collectives: 27.6 us -> 24.7 us  [spread(): return lax.all_to_all(copies, axis, 0, 0)]
    ppermute x2, waiting for transfers between devices: 2.33 us -> 1.08 us  [swap(): return lax.ppermute(block, axis, [(0, 1), (1, 0)])]
where the time goes in v8:
time: 97.6 us; the launch traced here: 95.9 us
  blocking collectives  57.1 us (59%)
  starting transfers between devices  13.1 us (13%)
  Pallas kernels  10.1 us (10%)
  waiting for transfers between devices  8.75 us (9%)
  local copies, waits for them, and re-layouts  4.72 us (5%)
  between operations  1.33 us (1%)
    all_to_all x1, blocking collectives, spread(): return lax.all_to_all(copies, axis, 0, 0)  24.7 us
    all_to_all x1, blocking collectives, body(): summed = lax.all_to_all(pairs, Z, 0, 0)  24.1 us
    all_to_all x1, blocking collectives, body(): lax.all_to_all(sums, first, 0, 0)  8.31 us
    all_to_all x1, waiting for transfers between devices, body(): lax.all_to_all(sums, second, 0, 0)  7.67 us
    ppermute x2, starting transfers between devices, swap(): return lax.ppermute(block, axis, [(0, 1), (1, 0)])  6.94 us
    all_to_all x1, starting transfers between devices, body(): lax.all_to_all(sums, second, 0, 0)  6.2 us
    pallas_call x1, Pallas kernels, attend(): pl.pallas_call(attend_kernel, out_shape=(jax.ShapeDtypeStruct((KVH, HD, c...  4.95 us
    unnamed x10, local copies, waits for them, and re-layouts  4.68 us
  transfers between devices with their start and end apart: 3, of which 2 were waited for; matrix products, arithmetic and copies ran while one was open for 0% of the time, Pallas kernels for 4%

profile of v8, /device:TPU:6, one launch (start us, length us, event | category | flops | bytes accessed | tf_op | source)
XLA Modules:
  0.0 95.9 jit_solution(5398643944872189756)
XLA Ops:
  0.6 0.8 pad_maximum_fusion
  1.5 24.7 %all_to_all.20.near_in = bf16[8,64,512]{2,1,0:T(8,128)(2,1)S(1)} all-to-all(bf16[8,64,512]{2,1,0:T(8,128)(2,1)S(1)} %broadcast_in_dim.21), channel_id=1, replica_groups=mesh['yh'=4,'x1'=2,'x0'=2,'core'=2,'yl'=2,'z2'=2,'z1'=2,'z0'=2] {'z1','z..., dimensions={0} | all-to-all | bytes 1048576 | tf_op jit(solution)/shard_map/all_to_all | solution.py:287
  26.2 3.5 %collective-permute-start = (bf16[8,64,512]{2,1,0:T(8,128)(2,1)S(1)}, bf16[8,64,512]{2,1,0:T(8,128)(2,1)S(1)}, u32[]{:S(2)}, u32[]{:S(2)}) collective-permute-start(bf16[8,64,512]{2,1,0:T(8,128)(2,1)S(1)} %all_to_all.20.near_in), channel_id=1, source_target_pairs={{0,8},{8,0},{1,9},{9,1},{2,10},{10,2},{3,11},{11,3},{4,12},{12,4},... | collective-permute-start | bytes 1572872 | tf_op jit(solution)/shard_map/ppermute | solution.py:291
  30.3 0.0 copy-start
  30.3 1.1 %copy-done = bf16[1,1,128,2560]{3,2,1,0:T(8,128)(2,1)S(1)} copy-done((bf16[1,1,128,2560]{3,2,1,0:T(8,128)(2,1)S(1)}, bf16[1,1,128,2560]{3,2,1,0:T(8,128)(2,1)}, u32[]{:S(2)}) %copy-start) | copy-done | bytes 655384
  31.4 0.0 copy-start.1
  31.4 1.1 %copy-done.1 = bf16[1,1,128,2560]{3,2,1,0:T(8,128)(2,1)S(1)} copy-done((bf16[1,1,128,2560]{3,2,1,0:T(8,128)(2,1)S(1)}, bf16[1,1,128,2560]{3,2,1,0:T(8,128)(2,1)}, u32[]{:S(2)}) %copy-start.1) | copy-done | bytes 655384
  32.5 0.0 copy-start.2
  32.5 0.9 copy-done.2
  33.4 0.0 copy-start.3
  33.4 0.9 copy-done.3
  34.3 0.0 copy-start.4
  34.3 0.7 copy-done.4
  35.0 1.0 %shard_map.127 = (bf16[4,640,128]{2,1,0:T(8,128)(2,1)S(1)}, bf16[4,640,128]{2,1,0:T(8,128)(2,1)S(1)}, bf16[128,512]{1,0:T(8,128)(2,1)S(1)}, bf16[128,512]{1,0:T(8,128)(2,1)S(1)}) custom-call(s32[1,1]{1,0:T(1,128)S(6)} %copy.14.length_ref, bf16[128,2560]{1,0:T(8,128)(2,1)S(1)} %bitcast.12, f32[2560]{0:T(1024)S(1)} %copy-done.4, ...), custom_call_target="tpu_custom_call" | custom-call | flops 327680 | bytes 4194304 | tf_op jit(solution)/shard_map/pallas_call | solution.py:62
  36.0 1.6 %shard_map.128 = (f32[4,384,640]{2,1,0:T(8,128)S(1)}, f32[4,384,640]{2,1,0:T(8,128)S(1)}, f32[4,8,640]{2,1,0:T(8,128)S(1)}) custom-call(s32[1,1]{1,0:T(1,128)S(6)} %copy.14.length_ref, bf16[4,640,128]{2,1,0:T(8,128)(2,1)S(1)} %get-tuple-element.26.qs_ref, bf16[4,640,128]{2,1,0:T(8,128)(2,1)S(1)} %get-tuple-element.27.dos_ref, ...), custom_call_target="tpu_custom_call" | custom-call | flops 503316480 | bytes 2097152 | tf_op jit(solution)/shard_map/pallas_call | solution.py:125
  37.6 1.1 %collective-permute-done.far_in = bf16[8,64,512]{2,1,0:T(8,128)(2,1)S(1)} collective-permute-done((bf16[8,64,512]{2,1,0:T(8,128)(2,1)S(1)}, bf16[8,64,512]{2,1,0:T(8,128)(2,1)S(1)}, u32[]{:S(2)}, u32[]{:S(2)}) %collective-permute-start) | collective-permute-done | bytes 524320 | tf_op jit(solution)/shard_map/ppermute | solution.py:291
  38.7 4.9 %shard_map.129 = (bf16[4,128,640]{2,1,0:T(8,128)(2,1)S(1)}, bf16[128,512]{1,0:T(8,128)(2,1)}, bf16[128,512]{1,0:T(8,128)(2,1)}, bf16[8,256,128]{2,1,0:T(8,128)(2...) custom-call(bf16[4,640,128]{2,1,0:T(8,128)(2,1)S(1)} %get-tuple-element.26.qs_ref, ...), custom_call_target="tpu_custom_call" | custom-call | flops 1677721600 | bytes 6291456 | tf_op jit(solution)/shard_map/pallas_call | solution.py:212
  43.6 3.5 %collective-permute-start.1 = (bf16[8,256,128]{2,1,0:T(8,128)(2,1)S(1)}, bf16[8,256,128]{2,1,0:T(8,128)(2,1)S(1)}, u32[]{:S(2)}, u32[]{:S(2)}) collective-permute-start(bf16[8,256,128]{2,1,0:T(8,128)(2,1)S(1)} %get-tuple-element.41), channel_id=1, source_target_pairs={{0,8},{8,0},{1,9},{9,1},{2,10},{10,2},{3,11},{11,3},{4,12},{12,4},... | collective-permute-start | bytes 1572872 | tf_op jit(solution)/shard_map/ppermute | solution.py:291
  47.1 8.3 %all_to_all.21.got = f32[8,20,128]{2,1,0:T(8,128)S(1)} all-to-all(f32[8,20,128]{2,1,0:T(8,128)S(1)} %get-tuple-element.33), channel_id=1, replica_groups=mesh['yh'=4,'x1'=2,'x0'=2,'core'=2,'yl'=2,'z2'=2,'z1'=2,'z0'=2] {'x1','x..., dimensions={0} | all-to-all | bytes 163840 | tf_op jit(solution)/shard_map/all_to_all | solution.py:313
  55.4 0.6 shard_map.130
  56.1 6.2 %all-to-all-start.2 = ((f32[8,20,128]{2,1,0:T(8,128)}), f32[8,20,128]{2,1,0:T(8,128)S(1)}, u32[]{:S(2)}, u32[]{:S(2)}) async-start(f32[8,20,128]{2,1,0:T(8,128)} %shard_map.130), calls=%async_computation.2 | async-start | bytes 196608 | tf_op jit(solution)/shard_map/all_to_all | solution.py:317
  62.3 1.1 %shard_map.131 = bf16[128,2560]{1,0:T(8,128)(2,1)} custom-call(bf16[4,128,640]{2,1,0:T(8,128)(2,1)S(1)} %get-tuple-element.36.flat_ref), custom_call_target="tpu_custom_call" | custom-call | tf_op jit(solution)/shard_map/pallas_call | solution.py:278
  63.3 7.7 %all-to-all-done.2.sums = f32[8,20,128]{2,1,0:T(8,128)S(1)} async-done(((f32[8,20,128]{2,1,0:T(8,128)}), f32[8,20,128]{2,1,0:T(8,128)S(1)}, u32[]{:S(2)}, u32[]{:S(2)}) %all-to-all-start.2) | async-done | bytes 81952 | tf_op jit(solution)/shard_map/all_to_all | solution.py:317
  71.0 0.0 collective-permute-done.1.got
  71.0 0.1 shard_map.132
  71.1 24.1 %all_to_all.22.got = bf16[8,304,128]{2,1,0:T(8,128)(2,1)S(1)} all-to-all(bf16[8,304,128]{2,1,0:T(8,128)(2,1)S(1)} %shard_map.132), channel_id=1, replica_groups=mesh['yh'=4,'x1'=2,'x0'=2,'core'=2,'yl'=2,'z2'=2,'z1'=2,'z0'=2] {'z1','z..., dimensions={0} | all-to-all | bytes 1245184 | tf_op jit(solution)/shard_map/all_to_all | solution.py:323
  95.2 0.7 shard_map.133
  (1 shorter events, 0.0 us)
Async XLA Ops:
  26.2 12.5 %collective-permute-start = (bf16[8,64,512]{2,1,0:T(8,128)(2,1)S(1)}, bf16[8,64,512]{2,1,0:T(8,128)(2,1)S(1)}, u32[]{:S(2)}, u32[]{:S(2)}) collective-permute-start(bf16[8,64,512]{2,1,0:T(8,128)(2,1)S(1)} %all_to_all.20.near_in), channel_id=1, source_target_pairs={{0,8},{8,0},{1,9},{9,1},{2,10},{10,2},{3,11},{11,3},{4,12},{12,4},... | collective-permute-start | bytes 1572872 | tf_op jit(solution)/shard_map/ppermute | solution.py:291
  30.3 1.1 %copy-start = (bf16[1,1,128,2560]{3,2,1,0:T(8,128)(2,1)S(1)}, bf16[1,1,128,2560]{3,2,1,0:T(8,128)(2,1)}, u32[]{:S(2)}) copy-start(bf16[1,1,128,2560]{3,2,1,0:T(8,128)(2,1)} %param.10) | copy-start | bytes 1966084
  31.4 1.1 %copy-start.1 = (bf16[1,1,128,2560]{3,2,1,0:T(8,128)(2,1)S(1)}, bf16[1,1,128,2560]{3,2,1,0:T(8,128)(2,1)}, u32[]{:S(2)}) copy-start(bf16[1,1,128,2560]{3,2,1,0:T(8,128)(2,1)} %param.14) | copy-start | bytes 1966084
  32.5 0.9 copy-start.2
  33.4 0.9 copy-start.3
  34.3 0.7 copy-start.4
  43.6 27.4 %collective-permute-start.1 = (bf16[8,256,128]{2,1,0:T(8,128)(2,1)S(1)}, bf16[8,256,128]{2,1,0:T(8,128)(2,1)S(1)}, u32[]{:S(2)}, u32[]{:S(2)}) collective-permute-start(bf16[8,256,128]{2,1,0:T(8,128)(2,1)S(1)} %get-tuple-element.41), channel_id=1, source_target_pairs={{0,8},{8,0},{1,9},{9,1},{2,10},{10,2},{3,11},{11,3},{4,12},{12,4},... | collective-permute-start | bytes 1572872 | tf_op jit(solution)/shard_map/ppermute | solution.py:291
  56.1 14.9 %all-to-all-start.2 = ((f32[8,20,128]{2,1,0:T(8,128)}), f32[8,20,128]{2,1,0:T(8,128)S(1)}, u32[]{:S(2)}, u32[]{:S(2)}) async-start(f32[8,20,128]{2,1,0:T(8,128)} %shard_map.130), calls=%async_computation.2 | async-start | bytes 196608 | tf_op jit(solution)/shard_map/all_to_all | solution.py:317
